TPU v7x, 32 devices: a whole 2x2x4 slice. The times are simulated.
32 devices in a mesh: row: 4 (over z), col: 8 (over y, x, core).
Axes of the slice: x: 2, y: 2, z: 4, core: 2. Of those that a mesh axis runs over, the one named last changes fastest.
Arguments:
- three_index: float32 [32, 512, 1024], P('col', None, 'row'), may hold values from -1.2 to 1.2
- occ_energy: float32 [32], replicated, may hold values from -2 to -0.5
- vir_energy: float32 [512], replicated, may hold values from 0.5 to 3
- block_mask: int32 [32, 8, 16], replicated, may hold values from 0 to 1, as said below
- pair_list: int32 [32, 4], P('col'), may hold values from -1 to 3, as said below
Outputs:
- response_density: float32 [32, 512, 1024], P('col', None, 'row')
- virtual_density: float32 [512, 512], replicated
Inputs may be any that keep to these rules, and one draw needn't show every extreme that they name: `block_mask`: each orbital keeps between 32 and 64 of its 128 blocks; some orbital keeps exactly 64. `pair_list`: in each row the live entries come first and are distinct, then -1; every orbital lists at least one partner class; some orbital lists 4.
All inputs are finite; a program needn't handle non-finite values.
Results may differ from a plain program's by a relative error of at most 0.0003.
Values sent between devices are 32-bit elements; how exact they have to be, the bound alone decides.
No kernel may reach another device: no remote copies, remote signals or barrier semaphores. Data moves between devices by JAX's collectives and lax.ppermute only.
A program may use at most 128 MiB of HBM per device.

v0:
```python
import functools

import jax
import jax.numpy as jnp
from jax import lax
from jax.experimental import pallas as pl
from jax.experimental.pallas import tpu as pltpu
from jax.sharding import PartitionSpec as P

BLOCK = 64
NPANEL = 4
TILE = 256
VMEM_LIMIT = 60 * 1024 * 1024
NT = (((1,), (1,)), ((), ()))


def staged(kernel, smalls, bigs, count, *refs):
    small, refs = refs[:smalls], refs[smalls:]
    sources, targets, scratch = refs[:bigs], refs[bigs : bigs + count], refs[bigs + count : -2]
    in_sem, out_sem = refs[-2:]
    held, made, own = scratch[:bigs], scratch[bigs : bigs + count], scratch[bigs + count :]
    loads = [
        pltpu.make_async_copy(source, target, in_sem.at[at])
        for at, (source, target) in enumerate(zip(sources, held))
    ]
    stores = [
        pltpu.make_async_copy(source, target, out_sem.at[at])
        for at, (source, target) in enumerate(zip(made, targets))
    ]
    for load in loads:
        load.start()
    kernel(small, held, made, own, [load.wait for load in loads], [store.start for store in stores])
    for store in stores:
        store.wait()


def call(kernel, name, outs, small, big, scratch):
    any_space = pl.BlockSpec(memory_space=pl.ANY)
    specs = [pl.BlockSpec(memory_space=pltpu.SMEM)]
    specs += [pl.BlockSpec(memory_space=pltpu.VMEM)] * (len(small) - 1)
    buffers = [pltpu.VMEM(at.shape, at.dtype) for at in [*big, *outs]]
    sems = [pltpu.SemaphoreType.DMA((len(big),)), pltpu.SemaphoreType.DMA((len(outs),))]
    return pl.pallas_call(
        functools.partial(staged, kernel, len(small), len(big), len(outs)),
        out_shape=outs,
        in_specs=specs + [any_space] * len(big),
        out_specs=[any_space] * len(outs),
        scratch_shapes=[*buffers, *scratch, *sems],
        compiler_params=pltpu.CompilerParams(vmem_limit_bytes=VMEM_LIMIT),
        cost_estimate=pl.CostEstimate(flops=0, bytes_accessed=0, transcendentals=0),
        name=name,
    )(*small, *big)


def shape(*sizes, kind=jnp.float32):
    return jax.ShapeDtypeStruct(sizes, kind)


def halves(value):
    high = value.astype(jnp.bfloat16)
    return high, (value - high.astype(jnp.float32)).astype(jnp.bfloat16)


def dot(left, right):
    return jnp.dot(left, right, preferred_element_type=jnp.float32)


def dot_nt(left, right):
    return lax.dot_general(left, right, NT, preferred_element_type=jnp.float32)


def split_rows(cuts, pieces, waits, mask, high, low):
    for (part, first, count), piece, wait in zip(cuts, pieces, waits):
        wait()
        width = piece.shape[1]
        cols = slice(part * width, (part + 1) * width)
        for start in range(0, count, BLOCK):
            at = first + start
            kept = mask[at // BLOCK : at // BLOCK + 1, cols]
            value = piece[start : start + BLOCK, :] * kept
            high[at : at + BLOCK, cols], low[at : at + BLOCK, cols] = halves(value)


def amplitudes(energy, live, vir_col, vir_row, own, panel, amp, a_parts, w_parts):
    nvir = amp.shape[0]
    for start in range(0, nvir, TILE):
        cols = slice(start, start + TILE)
        cross = dot_nt(own[0][...], panel[0][cols, :])
        cross += dot_nt(own[0][...], panel[1][cols, :])
        cross += dot_nt(own[1][...], panel[0][cols, :])
        value = cross / (energy - vir_col[...] - vir_row[:, cols]) * live
        amp[:, cols] = value
        a_parts[0][:, cols], a_parts[1][:, cols] = halves(value)
    for above in range(0, nvir, TILE):
        rows = slice(above, above + TILE)
        for start in range(0, nvir, TILE):
            cols = slice(start, start + TILE)
            value = 2.0 * amp[rows, cols] - amp[cols, rows].T
            w_parts[0][rows, cols], w_parts[1][rows, cols] = halves(value)


def respond(rows, w_parts, panel, cols):
    value = dot(w_parts[0][rows, :], panel[0][:, cols])
    value += dot(w_parts[0][rows, :], panel[1][:, cols])
    return value + dot(w_parts[1][rows, :], panel[0][:, cols])


def density_tile(cols, w_parts, a_parts):
    value = dot_nt(w_parts[0][...], a_parts[0][cols, :])
    value += dot_nt(w_parts[0][...], a_parts[1][cols, :])
    return value + dot_nt(w_parts[1][...], a_parts[0][cols, :])


def early_kernel(cuts, small, held, made, own_scratch, wait, give):
    scalars, vir_col, vir_row, masks = small
    count = len(cuts)
    own_high, own_low, density, *slices = made
    m_high, m_low, amp, a_high, a_low, w_high, w_low = own_scratch
    split_rows(cuts, held[:count], wait[:count], masks.at[0], own_high, own_low)
    give[0]()
    give[1]()
    nvir = amp.shape[0]
    panel, a_parts, w_parts = (m_high, m_low), (a_high, a_low), (w_high, w_low)
    for turn in range(2):
        where = slice((1 + turn) * count, (2 + turn) * count)
        split_rows(cuts, held[where], wait[where], masks.at[1 + turn], m_high, m_low)
        amplitudes(
            scalars[2 * turn], scalars[2 * turn + 1], vir_col, vir_row,
            (own_high, own_low), panel, amp, a_parts, w_parts,
        )
        for start in range(0, nvir, TILE):
            cols = slice(start, start + TILE)
            value = density_tile(cols, w_parts, a_parts)
            density[:, cols] = value if turn == 0 else density[:, cols] + value
        if turn:
            give[2]()
        for part, piece in enumerate(slices):
            width = piece.shape[1]
            cols = slice(part * width, (part + 1) * width)
            value = respond(slice(0, nvir), w_parts, panel, cols)
            piece[...] = value if turn == 0 else piece[...] + value
            if turn:
                give[3 + part]()


def squares(nvir, naux):
    half = jnp.bfloat16
    return [pltpu.VMEM((nvir, naux), half)] * 2, [pltpu.VMEM((nvir, nvir), half)] * 4


def early(cuts, scalars, virtual, masks, own, near, twin):
    nvir, width = own[0].shape
    naux = masks.shape[2]
    parts = naux // width
    outs = [shape(nvir, naux, kind=jnp.bfloat16)] * 2 + [shape(nvir, nvir)]
    outs += [shape(nvir, width)] * parts
    wide, square = squares(nvir, naux)
    small = [scalars, virtual[:, None], virtual[None, :], masks]
    kernel = functools.partial(early_kernel, cuts)
    scratch = [*wide, pltpu.VMEM((nvir, nvir), jnp.float32), *square]
    outs = call(kernel, "early", outs, small, [*own, *near, *twin], scratch)
    return outs[:2], outs[2], list(outs[3:])


def late_kernel(cuts, wanted, scale, small, held, made, own_scratch, wait, give):
    scalars, vir_col, vir_row, masks = small
    count = len(cuts)
    amp, panels = own_scratch[0], (own_scratch[1:7], own_scratch[7:])
    wait[0]()
    wait[1]()
    for turn, (m_high, m_low, a_high, a_low, w_high, w_low) in enumerate(panels):
        where = slice(2 + turn * count, 2 + (1 + turn) * count)
        split_rows(cuts, held[where], wait[where], masks.at[turn], m_high, m_low)
        amplitudes(
            scalars[2 * turn], scalars[2 * turn + 1], vir_col, vir_row,
            held[:2], (m_high, m_low), amp, (a_high, a_low), (w_high, w_low),
        )
    density, *slices = held[2 + 2 * count :]
    total, *pieces = made
    for ready in wait[2 + 2 * count :]:
        ready()
    for start in range(0, density.shape[0], TILE):
        cols = slice(start, start + TILE)
        value = density[:, cols]
        for _, _, a_high, a_low, w_high, w_low in panels:
            value += density_tile(cols, (w_high, w_low), (a_high, a_low))
        total[:, cols] = value * scale
    give[0]()
    for at, ((part, first, height), piece) in enumerate(zip(wanted, pieces)):
        rows = slice(first, first + height)
        width = piece.shape[1]
        cols = slice(part * width, (part + 1) * width)
        value = slices[part][rows, :]
        for m_high, m_low, _, _, w_high, w_low in panels:
            value += respond(rows, (w_high, w_low), (m_high, m_low), cols)
        piece[...] = value
        give[1 + at]()


def late(cuts, wanted, scale, scalars, virtual, masks, own, far, twin, density, slices):
    nvir, naux = own[0].shape
    width = slices[0].shape[1]
    outs = [shape(nvir, nvir)] + [shape(height, width) for _, _, height in wanted]
    wide, square = squares(nvir, naux)
    small = [scalars, virtual[:, None], virtual[None, :], masks]
    kernel = functools.partial(late_kernel, cuts, wanted, scale)
    scratch = [pltpu.VMEM((nvir, nvir), jnp.float32), *wide, *square, *wide, *square]
    big = [*own, *far, *twin, density, *slices]
    outs = call(kernel, "late", outs, small, big, scratch)
    return outs[0], list(outs[1:])


def exchange(value, axis, bit):
    size = lax.axis_size(axis)
    return lax.ppermute(value, axis, [(at, at ^ bit) for at in range(size)])


def after(value, *others):
    return lax.optimization_barrier((value, *others))[0]


def bits(axis):
    size = lax.axis_size(axis)
    return [1 << at for at in range(size.bit_length() - 1)]


def scatter_chip(value):
    half = value.shape[0] // 2
    side = lax.axis_index("col") % 2
    kept = lax.dynamic_slice_in_dim(value, side * half, half, 0)
    sent = lax.dynamic_slice_in_dim(value, (1 - side) * half, half, 0)
    return kept + exchange(sent, "col", 1)


def scatter_plane(value):
    place = lax.axis_index("col") // 2
    chips = lax.axis_size("col") // 2
    count = value.shape[0] // chips
    total = lax.dynamic_slice_in_dim(value, place * count, count, 0)
    for turn in range(1, chips):
        sent = lax.dynamic_slice_in_dim(value, (place ^ turn) * count, count, 0)
        total = total + exchange(sent, "col", 2 * turn)
    return total


def joined(terms, place):
    if len(terms) == 1:
        return terms[0]
    half = len(terms) // 2
    low, high = joined(terms[:half], place), joined(terms[half:], place)
    side = (place // half) % 2
    return jnp.where(side == 0, jnp.concatenate([low, high]), jnp.concatenate([high, low]))


def gather_plane(value):
    col = lax.axis_index("col")
    turns = range(1, lax.axis_size("col") // 2)
    terms = [value] + [exchange(value, "col", 2 * turn) for turn in turns]
    value = joined(terms, col // 2)
    return joined([value, exchange(value, "col", 1)], col)


def cut_list(nvir, row_count):
    return [(part, 0, nvir) for part in range(row_count)]


def on_device(three_index, occ_energy, vir_energy, block_mask, pair_list):
    row = lax.axis_index("row")
    col = lax.axis_index("col")
    row_count = lax.axis_size("row")
    col_count = lax.axis_size("col")
    position = col % NPANEL
    group = col // NPANEL
    groups = col_count // NPANEL
    nvir = three_index.shape[1]
    cuts = cut_list(nvir, row_count)

    own_orbital = col * row_count + row
    panels = [position ^ turn for turn in range(NPANEL)]
    orbitals = jnp.stack([own_orbital] + [at * row_count + row for at in panels])
    kept = block_mask[orbitals].reshape(NPANEL + 1, block_mask.shape[1], row_count, -1)
    kept = kept[:, :, row ^ jnp.arange(row_count), :].reshape(NPANEL + 1, kept.shape[1], -1)
    masks = jnp.repeat(kept.astype(jnp.float32), BLOCK, axis=-1)
    lists = pair_list[row]
    scalars = []
    for turn in range(NPANEL):
        live = jnp.any(lists == panels[turn]).astype(jnp.float32)
        scalars += [occ_energy[own_orbital] + occ_energy[orbitals[1 + turn]], live]
    small = masks[:3], masks[3:], jnp.stack(scalars[:4]), jnp.stack(scalars[4:])

    own, came, near, far = [], [], [], []

    def receive(at):
        part, first, count = cuts[at]
        rows = lax.dynamic_index_in_dim(three_index, row ^ part, 0, keepdims=False)
        rows = rows[first : first + count]
        if part == row_count - 1:
            rows = after(rows, near[0])
        elif part > 1:
            rows = after(rows, scalars[1])
        own.append(exchange(rows, "row", part) if part else rows)

    for at in range(len(cuts)):
        while len(own) < min(at + 1 if at > 1 else row_count - 1, len(cuts)):
            receive(len(own))
        rows = own[at]
        if at:
            rows = after(rows, came[-1])
        reach = 1
        while reach < groups:
            span = min(reach, groups - reach) * NPANEL
            links = [(one, one + reach * NPANEL) for one in range(span)]
            got = lax.ppermute(rows, "col", links)
            rows = jnp.where((group >= reach) & (group < 2 * reach), got, rows)
            reach *= 2
        came.append(got)
        near.append(rows)
        sent = after(rows, far[-1]) if at else after(rows, *small)
        far.append(exchange(sent, "col", 2))

    near_twin = [exchange(piece, "col", 1) for piece in near]
    halved, density, slices = early(
        cuts, small[2], vir_energy, small[0], own, near, near_twin
    )
    far_twin = [exchange(piece, "col", 1) for piece in far[:-1]]
    far_twin.append(exchange(after(far[-1], density), "col", 1))

    middle, edge, most = row_count // 2, row_count - 1, nvir // 4 * 3
    wanted = [(middle, 0, most), (middle, most, nvir - most)]
    wanted += [(at, 0, nvir) for at in range(row_count) if at != middle]
    scale = 1.0 / (row_count * col_count)
    total, pieces = late(
        cuts, wanted, scale, small[3], vir_energy, small[1], halved, far, far_twin,
        density, slices,
    )

    def leave(at, *others):
        return exchange(after(pieces[at], *others), "row", wanted[at][0])

    ends = [leave(0)]
    total = scatter_plane(scatter_chip(total))
    ends.append(leave(1, total))
    total = after(total, ends[0])
    for bit in bits("row")[:-1]:
        total = total + exchange(total, "row", bit)
    total = after(total, ends[1])
    ends.append(pieces[2])
    ends += [leave(at, total) for at in range(3, len(wanted) - 1)]
    total = total + exchange(total, "row", bits("row")[-1])
    ends.append(leave(len(wanted) - 1, total))
    total = gather_plane(total)

    returned = jnp.zeros_like(three_index)
    for (part, first, _), piece in zip(wanted, ends):
        returned = lax.dynamic_update_slice(returned, piece[None], (row ^ part, first, 0))
    return returned, total


def solution(mesh):
    placed = (P("col", None, "row"), P(), P(), P(), P("col", None))
    return jax.shard_map(
        on_device,
        mesh=mesh,
        in_specs=placed,
        out_specs=(P("col", None, "row"), P()),
        check_vma=False,
    )
```

profile of v0, /device:TPU:0, one launch (start us, length us, event | category | flops | bytes accessed | tf_op | source)
XLA Modules:
  0.0 169.5 jit_solution(14379765527416229414)
XLA Ops:
  0.7 2.7 %dynamic-slice_bitcast_fusion = (f32[512,256]{1,0:T(8,128)}, f32[512,256]{1,0:T(8,128)S(1)}, f32[512,256]{1,0:T(8,128)S(1)}, f32[512,256]{1,0:T(8,128)}) fusion(f32[4,512,256]{2,1,0:T(8,128)} %param.5, s32[]{:T(128)S(6)} %select_n.171, s32[]{:T(128)S(6)} %select_n.169, s32[]{:T(128)S(6)} %select_n.163, s32[]{:T(128)S(6)} %select_n.170), kind=kLoop, calls=%fused_computation.8 | loop fusion | bytes 4194320 | tf_op jit(solution)/shard_map/jit(dynamic_index_in_dim)/squeeze | solution.py:295
  3.4 4.9 %collective-permute-start.2 = (f32[512,256]{1,0:T(8,128)S(1)}, f32[512,256]{1,0:T(8,128)S(1)}, u32[]{:S(2)}, u32[]{:S(2)}) collective-permute-start(f32[512,256]{1,0:T(8,128)S(1)} %get-tuple-element.64.refs_4_), channel_id=1, source_target_pairs={{0,4},{1,5},{2,6},{3,7},{8,12},{9,13},{10,14},{11,15},{16,20},{17,... | collective-permute-start | bytes 1572872 | tf_op jit(solution)/shard_map/ppermute | solution.py:313
  8.3 1.6 collective-permute-start
  9.9 1.4 compare_reduce_fusion.1
  12.0 2.7 %collective-permute-start.1 = (f32[512,256]{1,0:T(8,128)}, f32[512,256]{1,0:T(8,128)S(1)}, u32[]{:S(2)}, u32[]{:S(2)}) collective-permute-start(f32[512,256]{1,0:T(8,128)} %get-tuple-element.30), channel_id=1, source_target_pairs={{0,16},{8,24},{16,0},{24,8},{1,17},{9,25},{17,1},{25,9},{2,18},{10... | collective-permute-start | bytes 1572872 | tf_op jit(solution)/shard_map/ppermute | solution.py:215
  14.6 0.1 stack.59
  14.8 0.1 copy.12
  14.9 0.6 gather_fusion
  15.5 0.6 gather_fusion.1
  16.2 0.7 fusion.2
  23.8 0.1 broadcast_in_dim.37
  23.9 0.8 slice.25.refs_3_
  24.7 0.1 broadcast_in_dim.36
  24.8 0.7 slice.22.refs_3_
  25.6 0.6 pad_maximum_fusion.1.refs_0_
  26.1 0.6 pad_maximum_fusion.refs_0_
  26.8 3.8 %collective-permute-done.refs_5_ = f32[512,256]{1,0:T(8,128)S(1)} collective-permute-done((f32[512,256]{1,0:T(8,128)S(1)}, f32[512,256]{1,0:T(8,128)S(1)}, u32[]{:S(2)}, u32[]{:S(2)}) %collective-permute-start) | collective-permute-done | bytes 524320 | tf_op jit(solution)/shard_map/ppermute | solution.py:215
  30.5 2.3 %collective-permute-start.4 = (f32[512,256]{1,0:T(8,128)S(1)}, f32[512,256]{1,0:T(8,128)}, u32[]{:S(2)}, u32[]{:S(2)}) collective-permute-start(f32[512,256]{1,0:T(8,128)S(1)} %collective-permute-done.refs_5_), channel_id=1, source_target_pairs={{0,4},{1,5},{2,6},{3,7},{8,12},{9,13},{10,14},{11,15},{16,20},{17,... | collective-permute-start | bytes 1572872 | tf_op jit(solution)/shard_map/ppermute | solution.py:313
  32.9 1.6 collective-permute-start.11
  34.5 2.5 %collective-permute-start.3 = (f32[512,256]{1,0:T(8,128)}, f32[512,256]{1,0:T(8,128)S(1)}, u32[]{:S(2)}, u32[]{:S(2)}) collective-permute-start(f32[512,256]{1,0:T(8,128)} %get-tuple-element.31), channel_id=1, source_target_pairs={{0,24},{8,16},{16,8},{24,0},{1,25},{9,17},{17,9},{25,1},{2,26},{10... | collective-permute-start | bytes 1572872 | tf_op jit(solution)/shard_map/ppermute | solution.py:215
  37.0 13.5 %collective-permute-done.1.refs_6_ = f32[512,256]{1,0:T(8,128)S(1)} collective-permute-done((f32[512,256]{1,0:T(8,128)}, f32[512,256]{1,0:T(8,128)S(1)}, u32[]{:S(2)}, u32[]{:S(2)}) %collective-permute-start.1) | collective-permute-done | bytes 524320 | tf_op jit(solution)/shard_map/ppermute | solution.py:215
  50.5 1.3 collective-permute-start.5
  51.8 0.1 broadcast_select_fusion.2.refs_9_
  51.9 1.6 collective-permute-start.12
  53.5 8.5 %collective-permute-done.5 = f32[512,256]{1,0:T(8,128)S(1)} collective-permute-done((f32[512,256]{1,0:T(8,128)S(1)}, f32[512,256]{1,0:T(8,128)S(1)}, u32[]{:S(2)}, u32[]{:S(2)}) %collective-permute-start.5) | collective-permute-done | bytes 524320 | tf_op jit(solution)/shard_map/ppermute | solution.py:313
  62.0 4.4 %collective-permute-start.6 = (f32[512,256]{1,0:T(8,128)S(1)}, f32[512,256]{1,0:T(8,128)S(1)}, u32[]{:S(2)}, u32[]{:S(2)}) collective-permute-start(f32[512,256]{1,0:T(8,128)S(1)} %collective-permute-done.3.refs_7_), channel_id=1, source_target_pairs={{0,4},{1,5},{2,6},{3,7},{8,12},{9,13},{10,14},{11,15},{16,20},{17,... | collective-permute-start | bytes 1572872 | tf_op jit(solution)/shard_map/ppermute | solution.py:313
  66.7 0.5 collective-permute-start.8
  67.1 0.1 collective-permute-start.9
  67.2 5.8 %collective-permute-done.6 = f32[512,256]{1,0:T(8,128)S(1)} collective-permute-done((f32[512,256]{1,0:T(8,128)S(1)}, f32[512,256]{1,0:T(8,128)S(1)}, u32[]{:S(2)}, u32[]{:S(2)}) %collective-permute-start.6) | collective-permute-done | bytes 524320 | tf_op jit(solution)/shard_map/ppermute | solution.py:313
  73.2 2.5 %collective-permute-done.13.refs_8_ = f32[512,256]{1,0:T(8,128)S(1)} collective-permute-done((f32[512,256]{1,0:T(8,128)S(1)}, f32[512,256]{1,0:T(8,128)S(1)}, u32[]{:S(2)}, u32[]{:S(2)}) %collective-permute-start.13) | collective-permute-done | bytes 524320 | tf_op jit(solution)/shard_map/ppermute | solution.py:215
  75.7 0.5 collective-permute-start.14
  76.3 0.3 copy-done.11
  76.6 0.9 copy.19.refs_1_
  77.4 0.5 collective-permute-start.16
  78.1 13.4 %early.1 = (bf16[512,1024]{1,0:T(8,128)(2,1)}, bf16[512,1024]{1,0:T(8,128)(2,1)}, f32[512,512]{1,0:T(8,128)}, f32[512,256]{1,0:T(8,128)}, f32[512,256]{1,0:T(8,1...) custom-call(f32[4]{0:T(128)} %pad_maximum_fusion.1.refs_0_, f32[512,1]{1,0:T(8,128)} %copy.19.refs_1_, f32[1,512]{1,0:T(1,128)} %bitcast.45, ...), custom_call_target="tpu_custom_call" | custom-call | tf_op jit(solution)/shard_map/early/pallas_call | solution.py:43
  91.5 0.5 collective-permute-start.18
  92.0 1.5 collective-permute-done.18.refs_13_
  93.5 0.8 copy-done.14
  94.3 14.5 %late.1 = (f32[512,512]{1,0:T(8,128)}, f32[384,256]{1,0:T(8,128)}, f32[128,256]{1,0:T(8,128)}, f32[512,256]{1,0:T(8,128)}, f32[512,256]{1,0:T(8,128)}, /*index=5*/f32[512,256]{1,0:T(8,128)}) custom-call(f32[4]{0:T(128)} %pad_maximum_fusion.refs_0_, f32[512,1]{1,0:T(8,128)} %copy.19.refs_1_, f32[1,512]{1,0:T(1,128)} %bitcast.46, ...), custom_call_target="tpu_custom_call" | custom-call | tf_op jit(solution)/shard_map/late/pallas_call | solution.py:43
  108.8 1.1 constant_dynamic-slice_fusion.3
  110.0 0.4 collective-permute-start.20
  110.4 0.5 collective-permute-start.19
  110.9 1.0 collective-permute-done.20
  111.9 1.1 dynamic-slice_add_fusion
  113.1 1.3 collective-permute-start.21
  114.5 2.2 %collective-permute-start.23 = (f32[64,512]{1,0:T(8,128)S(1)}, f32[64,512]{1,0:T(8,128)S(1)}, u32[]{:S(2)}, u32[]{:S(2)}) collective-permute-start(f32[64,512]{1,0:T(8,128)S(1)} %get-tuple-element.67), channel_id=1, source_target_pairs={{0,6},{1,7},{2,4},{3,5},{4,2},{5,3},{6,0},{7,1},{8,14},{9,15},{10,... | collective-permute-start | bytes 393224 | tf_op jit(solution)/shard_map/ppermute | solution.py:215
  116.7 2.8 %collective-permute-done.21 = f32[64,512]{1,0:T(8,128)S(1)} collective-permute-done((f32[64,512]{1,0:T(8,128)S(1)}, f32[64,512]{1,0:T(8,128)S(1)}, u32[]{:S(2)}, u32[]{:S(2)}) %collective-permute-start.21) | collective-permute-done | bytes 131104 | tf_op jit(solution)/shard_map/ppermute | solution.py:215
  119.5 3.2 %collective-permute-done.22 = f32[64,512]{1,0:T(8,128)S(1)} collective-permute-done((f32[64,512]{1,0:T(8,128)S(1)}, f32[64,512]{1,0:T(8,128)S(1)}, u32[]{:S(2)}, u32[]{:S(2)}) %collective-permute-start.22) | collective-permute-done | bytes 131104 | tf_op jit(solution)/shard_map/ppermute | solution.py:215
  122.8 8.2 %collective-permute-done.19 = f32[384,256]{1,0:T(8,128)S(1)} collective-permute-done((f32[384,256]{1,0:T(8,128)}, f32[384,256]{1,0:T(8,128)S(1)}, u32[]{:S(2)}, u32[]{:S(2)}) %collective-permute-start.19) | collective-permute-done | bytes 393248 | tf_op jit(solution)/shard_map/ppermute | solution.py:215
  130.9 2.2 %collective-permute-start.24 = (f32[128,256]{1,0:T(8,128)S(1)}, f32[128,256]{1,0:T(8,128)S(1)}, u32[]{:S(2)}, u32[]{:S(2)}) collective-permute-start(f32[128,256]{1,0:T(8,128)S(1)} %copy-done.21), channel_id=1, source_target_pairs={{0,16},{8,24},{16,0},{24,8},{1,17},{9,25},{17,1},{25,9},{2,18},{10... | collective-permute-start | bytes 393224 | tf_op jit(solution)/shard_map/ppermute | solution.py:215
  133.1 5.1 %collective-permute-done.25 = f32[64,512]{1,0:T(8,128)S(1)} collective-permute-done((f32[64,512]{1,0:T(8,128)S(1)}, f32[64,512]{1,0:T(8,128)S(1)}, u32[]{:S(2)}, u32[]{:S(2)}) %collective-permute-start.25) | collective-permute-done | bytes 131104 | tf_op jit(solution)/shard_map/ppermute | solution.py:215
  138.2 1.9 %collective-permute-done.24 = f32[128,256]{1,0:T(8,128)S(1)} collective-permute-done((f32[128,256]{1,0:T(8,128)S(1)}, f32[128,256]{1,0:T(8,128)S(1)}, u32[]{:S(2)}, u32[]{:S(2)}) %collective-permute-start.24) | collective-permute-done | bytes 131104 | tf_op jit(solution)/shard_map/ppermute | solution.py:215
  140.1 0.3 collective-permute-start.27
  140.4 0.2 broadcast_in_dim.33
  140.7 1.9 %collective-permute-start.26 = (f32[512,256]{1,0:T(8,128)S(1)}, f32[512,256]{1,0:T(8,128)S(1)}, u32[]{:S(2)}, u32[]{:S(2)}) collective-permute-start(f32[512,256]{1,0:T(8,128)S(1)} %copy-done.20), channel_id=1, source_target_pairs={{0,8},{8,0},{16,24},{24,16},{1,9},{9,1},{17,25},{25,17},{2,10},{10... | collective-permute-start | bytes 1572872 | tf_op jit(solution)/shard_map/ppermute | solution.py:215
  142.6 5.1 %collective-permute-done.27 = f32[64,512]{1,0:T(8,128)S(1)} collective-permute-done((f32[64,512]{1,0:T(8,128)S(1)}, f32[64,512]{1,0:T(8,128)S(1)}, u32[]{:S(2)}, u32[]{:S(2)}) %collective-permute-start.27) | collective-permute-done | bytes 131104 | tf_op jit(solution)/shard_map/ppermute | solution.py:215
  147.7 0.8 collective-permute-start.29
  148.5 2.7 %collective-permute-start.31 = (f32[64,512]{1,0:T(8,128)S(1)}, f32[64,512]{1,0:T(8,128)S(1)}, u32[]{:S(2)}, u32[]{:S(2)}) collective-permute-start(f32[64,512]{1,0:T(8,128)S(1)} %add.177), channel_id=1, source_target_pairs={{0,6},{1,7},{2,4},{3,5},{4,2},{5,3},{6,0},{7,1},{8,14},{9,15},{10,... | collective-permute-start | bytes 393224 | tf_op jit(solution)/shard_map/ppermute | solution.py:215
  151.3 1.2 collective-permute-start.28
  152.5 1.6 collective-permute-done.29
  154.2 1.9 %collective-permute-done.30 = f32[64,512]{1,0:T(8,128)S(1)} collective-permute-done((f32[64,512]{1,0:T(8,128)S(1)}, f32[64,512]{1,0:T(8,128)S(1)}, u32[]{:S(2)}, u32[]{:S(2)}) %collective-permute-start.30) | collective-permute-done | bytes 131104 | tf_op jit(solution)/shard_map/ppermute | solution.py:215
  156.3 11.5 %collective-permute-done.26 = f32[512,256]{1,0:T(8,128)S(1)} collective-permute-done((f32[512,256]{1,0:T(8,128)S(1)}, f32[512,256]{1,0:T(8,128)S(1)}, u32[]{:S(2)}, u32[]{:S(2)}) %collective-permute-start.26) | collective-permute-done | bytes 524320 | tf_op jit(solution)/shard_map/ppermute | solution.py:215
  167.9 1.2 maximum_select_fusion
  169.1 0.4 copy-done.8
  (94 shorter events, 1.4 us)
Async XLA Ops:
  0.7 14.1 %copy-start.16 = (s32[32,8,16]{0,2,1:T(8,128)S(1)}, s32[32,8,16]{0,2,1:T(8,128)}, u32[]{:S(2)}) copy-start(s32[32,8,16]{0,2,1:T(8,128)} %param.8) | copy-start | bytes 49156
  0.7 15.5 %copy-start.18 = (f32[32]{0:T(128)S(1)}, f32[32]{0:T(128)}, u32[]{:S(2)}) copy-start(f32[32]{0:T(128)} %param.6) | copy-start | bytes 388
  3.4 48.5 %copy-start = (f32[512,256]{1,0:T(8,128)}, f32[512,256]{1,0:T(8,128)S(1)}, u32[]{:S(2)}) copy-start(f32[512,256]{1,0:T(8,128)S(1)} %get-tuple-element.64.refs_4_) | copy-start | bytes 1572868
  3.4 23.4 %collective-permute-start.2 = (f32[512,256]{1,0:T(8,128)S(1)}, f32[512,256]{1,0:T(8,128)S(1)}, u32[]{:S(2)}, u32[]{:S(2)}) collective-permute-start(f32[512,256]{1,0:T(8,128)S(1)} %get-tuple-element.64.refs_4_), channel_id=1, source_target_pairs={{0,4},{1,5},{2,6},{3,7},{8,12},{9,13},{10,14},{11,15},{16,20},{17,... | collective-permute-start | bytes 1572872 | tf_op jit(solution)/shard_map/ppermute | solution.py:313
  8.3 22.2 %collective-permute-start = (f32[512,256]{1,0:T(8,128)S(1)}, f32[512,256]{1,0:T(8,128)S(1)}, u32[]{:S(2)}, u32[]{:S(2)}) collective-permute-start(f32[512,256]{1,0:T(8,128)S(1)} %get-tuple-element.63), channel_id=1, source_target_pairs={{0,8},{8,0},{16,24},{24,16},{1,9},{9,1},{17,25},{25,17},{2,10},{10... | collective-permute-start | bytes 1572872 | tf_op jit(solution)/shard_map/ppermute | solution.py:215
  12.0 38.5 %collective-permute-start.1 = (f32[512,256]{1,0:T(8,128)}, f32[512,256]{1,0:T(8,128)S(1)}, u32[]{:S(2)}, u32[]{:S(2)}) collective-permute-start(f32[512,256]{1,0:T(8,128)} %get-tuple-element.30), channel_id=1, source_target_pairs={{0,16},{8,24},{16,0},{24,8},{1,17},{9,25},{17,1},{25,9},{2,18},{10... | collective-permute-start | bytes 1572872 | tf_op jit(solution)/shard_map/ppermute | solution.py:215
  30.5 35.9 %copy-start.1 = (f32[512,256]{1,0:T(8,128)}, f32[512,256]{1,0:T(8,128)S(1)}, u32[]{:S(2)}) copy-start(f32[512,256]{1,0:T(8,128)S(1)} %collective-permute-done.refs_5_) | copy-start | bytes 1572868
  30.5 20.0 %collective-permute-start.4 = (f32[512,256]{1,0:T(8,128)S(1)}, f32[512,256]{1,0:T(8,128)}, u32[]{:S(2)}, u32[]{:S(2)}) collective-permute-start(f32[512,256]{1,0:T(8,128)S(1)} %collective-permute-done.refs_5_), channel_id=1, source_target_pairs={{0,4},{1,5},{2,6},{3,7},{8,12},{9,13},{10,14},{11,15},{16,20},{17,... | collective-permute-start | bytes 1572872 | tf_op jit(solution)/shard_map/ppermute | solution.py:313
  32.9 40.2 %copy-start.3 = (f32[512,256]{1,0:T(8,128)}, f32[512,256]{1,0:T(8,128)S(1)}, u32[]{:S(2)}) copy-start(f32[512,256]{1,0:T(8,128)S(1)} %broadcast_select_fusion.3.refs_8_) | copy-start | bytes 1572868
  32.9 19.0 %collective-permute-start.11 = (f32[512,256]{1,0:T(8,128)S(1)}, f32[512,256]{1,0:T(8,128)S(1)}, u32[]{:S(2)}, u32[]{:S(2)}) collective-permute-start(f32[512,256]{1,0:T(8,128)S(1)} %broadcast_select_fusion.3.refs_8_), channel_id=1, source_target_pairs={{0,2},{1,3},{2,0},{3,1},{4,6},{5,7},{6,4},{7,5},{8,10},{9,11},{10,... | collective-permute-start | bytes 1572872 | tf_op jit(solution)/shard_map/ppermute | solution.py:215
  34.5 42.1 %copy-start.17 = (f32[512]{0:T(512)S(1)}, f32[512]{0:T(512)}, u32[]{:S(2)}) copy-start(f32[512]{0:T(512)} %param.7) | copy-start | bytes 6148
  34.5 19.0 %collective-permute-start.3 = (f32[512,256]{1,0:T(8,128)}, f32[512,256]{1,0:T(8,128)S(1)}, u32[]{:S(2)}, u32[]{:S(2)}) collective-permute-start(f32[512,256]{1,0:T(8,128)} %get-tuple-element.31), channel_id=1, source_target_pairs={{0,24},{8,16},{16,8},{24,0},{1,25},{9,17},{17,9},{25,1},{2,26},{10... | collective-permute-start | bytes 1572872 | tf_op jit(solution)/shard_map/ppermute | solution.py:215
  50.5 22.6 %copy-start.2 = (f32[512,256]{1,0:T(8,128)}, f32[512,256]{1,0:T(8,128)S(1)}, u32[]{:S(2)}) copy-start(f32[512,256]{1,0:T(8,128)S(1)} %collective-permute-done.1.refs_6_) | copy-start | bytes 1572868
  50.5 11.5 %collective-permute-start.5 = (f32[512,256]{1,0:T(8,128)S(1)}, f32[512,256]{1,0:T(8,128)S(1)}, u32[]{:S(2)}, u32[]{:S(2)}) collective-permute-start(f32[512,256]{1,0:T(8,128)S(1)} %collective-permute-done.1.refs_6_), channel_id=1, source_target_pairs={{0,4},{1,5},{2,6},{3,7},{8,12},{9,13},{10,14},{11,15},{16,20},{17,... | collective-permute-start | bytes 1572872 | tf_op jit(solution)/shard_map/ppermute | solution.py:313
  51.9 26.1 %copy-start.5 = (f32[512,256]{1,0:T(8,128)}, f32[512,256]{1,0:T(8,128)S(1)}, u32[]{:S(2)}) copy-start(f32[512,256]{1,0:T(8,128)S(1)} %broadcast_select_fusion.2.refs_9_) | copy-start | bytes 1572868
  51.9 23.8 %copy-start.9 = (f32[512,256]{1,0:T(8,128)}, f32[512,256]{1,0:T(8,128)S(1)}, u32[]{:S(2)}) copy-start(f32[512,256]{1,0:T(8,128)S(1)} %collective-permute-done.11.refs_6_) | copy-start | bytes 1572868
  51.9 14.5 %collective-permute-start.12 = (f32[512,256]{1,0:T(8,128)S(1)}, f32[512,256]{1,0:T(8,128)S(1)}, u32[]{:S(2)}, u32[]{:S(2)}) collective-permute-start(f32[512,256]{1,0:T(8,128)S(1)} %broadcast_select_fusion.2.refs_9_), channel_id=1, source_target_pairs={{0,2},{1,3},{2,0},{3,1},{4,6},{5,7},{6,4},{7,5},{8,10},{9,11},{10,... | collective-permute-start | bytes 1572872 | tf_op jit(solution)/shard_map/ppermute | solution.py:215
  53.5 24.5 %copy-start.4 = (f32[512,256]{1,0:T(8,128)}, f32[512,256]{1,0:T(8,128)S(1)}, u32[]{:S(2)}) copy-start(f32[512,256]{1,0:T(8,128)S(1)} %collective-permute-done.3.refs_7_) | copy-start | bytes 1572868
  62.0 11.1 %collective-permute-start.6 = (f32[512,256]{1,0:T(8,128)S(1)}, f32[512,256]{1,0:T(8,128)S(1)}, u32[]{:S(2)}, u32[]{:S(2)}) collective-permute-start(f32[512,256]{1,0:T(8,128)S(1)} %collective-permute-done.3.refs_7_), channel_id=1, source_target_pairs={{0,4},{1,5},{2,6},{3,7},{8,12},{9,13},{10,14},{11,15},{16,20},{17,... | collective-permute-start | bytes 1572872 | tf_op jit(solution)/shard_map/ppermute | solution.py:313
  66.5 11.6 %copy-start.6 = (f32[512,256]{1,0:T(8,128)}, f32[512,256]{1,0:T(8,128)S(1)}, u32[]{:S(2)}) copy-start(f32[512,256]{1,0:T(8,128)S(1)} %broadcast_select_fusion.1.refs_10_) | copy-start | bytes 1572868
  66.5 9.8 %copy-start.10 = (f32[512,256]{1,0:T(8,128)}, f32[512,256]{1,0:T(8,128)S(1)}, u32[]{:S(2)}) copy-start(f32[512,256]{1,0:T(8,128)S(1)} %collective-permute-done.12.refs_7_) | copy-start | bytes 1572868
  66.5 9.2 %collective-permute-start.13 = (f32[512,256]{1,0:T(8,128)S(1)}, f32[512,256]{1,0:T(8,128)S(1)}, u32[]{:S(2)}, u32[]{:S(2)}) collective-permute-start(f32[512,256]{1,0:T(8,128)S(1)} %broadcast_select_fusion.1.refs_10_), channel_id=1, source_target_pairs={{0,2},{1,3},{2,0},{3,1},{4,6},{5,7},{6,4},{7,5},{8,10},{9,11},{10,... | collective-permute-start | bytes 1572872 | tf_op jit(solution)/shard_map/ppermute | solution.py:215
  66.6 10.9 %collective-permute-start.7 = (f32[512,256]{1,0:T(8,128)S(1)}, f32[512,256]{1,0:T(8,128)}, u32[]{:S(2)}, u32[]{:S(2)}) collective-permute-start(f32[512,256]{1,0:T(8,128)S(1)} %broadcast_select_fusion.3.refs_8_), channel_id=1, source_target_pairs={{0,1},{1,0},{2,3},{3,2},{4,5},{5,4},{6,7},{7,6},{8,9},{9,8},{10,11... | collective-permute-start | bytes 1572872 | tf_op jit(solution)/shard_map/ppermute | solution.py:215
  66.7 10.8 %collective-permute-start.8 = (f32[512,256]{1,0:T(8,128)S(1)}, f32[512,256]{1,0:T(8,128)}, u32[]{:S(2)}, u32[]{:S(2)}) collective-permute-start(f32[512,256]{1,0:T(8,128)S(1)} %broadcast_select_fusion.2.refs_9_), channel_id=1, source_target_pairs={{0,1},{1,0},{2,3},{3,2},{4,5},{5,4},{6,7},{7,6},{8,9},{9,8},{10,11... | collective-permute-start | bytes 1572872 | tf_op jit(solution)/shard_map/ppermute | solution.py:215
  67.1 10.8 %collective-permute-start.9 = (f32[512,256]{1,0:T(8,128)S(1)}, f32[512,256]{1,0:T(8,128)}, u32[]{:S(2)}, u32[]{:S(2)}) collective-permute-start(f32[512,256]{1,0:T(8,128)S(1)} %broadcast_select_fusion.1.refs_10_), channel_id=1, source_target_pairs={{0,1},{1,0},{2,3},{3,2},{4,5},{5,4},{6,7},{7,6},{8,9},{9,8},{10,11... | collective-permute-start | bytes 1572872 | tf_op jit(solution)/shard_map/ppermute | solution.py:215
  73.1 4.9 %copy-start.7 = (f32[512,256]{1,0:T(8,128)}, f32[512,256]{1,0:T(8,128)S(1)}, u32[]{:S(2)}) copy-start(f32[512,256]{1,0:T(8,128)S(1)} %broadcast_select_fusion.refs_11_) | copy-start | bytes 1572868
  73.1 4.9 %collective-permute-start.10 = (f32[512,256]{1,0:T(8,128)S(1)}, f32[512,256]{1,0:T(8,128)}, u32[]{:S(2)}, u32[]{:S(2)}) collective-permute-start(f32[512,256]{1,0:T(8,128)S(1)} %broadcast_select_fusion.refs_11_), channel_id=1, source_target_pairs={{0,1},{1,0},{2,3},{3,2},{4,5},{5,4},{6,7},{7,6},{8,9},{9,8},{10,11... | collective-permute-start | bytes 1572872 | tf_op jit(solution)/shard_map/ppermute | solution.py:215
  75.7 0.8 copy-start.11
  75.7 15.7 %collective-permute-start.14 = (f32[512,256]{1,0:T(8,128)S(1)}, f32[512,256]{1,0:T(8,128)S(1)}, u32[]{:S(2)}, u32[]{:S(2)}) collective-permute-start(f32[512,256]{1,0:T(8,128)S(1)} %broadcast_select_fusion.refs_11_), channel_id=1, source_target_pairs={{0,2},{1,3},{2,0},{3,1},{4,6},{5,7},{6,4},{7,5},{8,10},{9,11},{10,... | collective-permute-start | bytes 1572872 | tf_op jit(solution)/shard_map/ppermute | solution.py:215
  77.4 14.5 %collective-permute-start.15 = (f32[512,256]{1,0:T(8,128)}, f32[512,256]{1,0:T(8,128)S(1)}, u32[]{:S(2)}, u32[]{:S(2)}) collective-permute-start(f32[512,256]{1,0:T(8,128)} %copy-done.9), channel_id=1, source_target_pairs={{0,1},{1,0},{2,3},{3,2},{4,5},{5,4},{6,7},{7,6},{8,9},{9,8},{10,11... | collective-permute-start | bytes 1572872 | tf_op jit(solution)/shard_map/ppermute | solution.py:215
  77.4 14.5 %collective-permute-start.16 = (f32[512,256]{1,0:T(8,128)}, f32[512,256]{1,0:T(8,128)}, u32[]{:S(2)}, u32[]{:S(2)}) collective-permute-start(f32[512,256]{1,0:T(8,128)} %copy-done.10), channel_id=1, source_target_pairs={{0,1},{1,0},{2,3},{3,2},{4,5},{5,4},{6,7},{7,6},{8,9},{9,8},{10,11... | collective-permute-start | bytes 1572872 | tf_op jit(solution)/shard_map/ppermute | solution.py:215
  78.0 14.0 %collective-permute-start.17 = (f32[512,256]{1,0:T(8,128)}, f32[512,256]{1,0:T(8,128)}, u32[]{:S(2)}, u32[]{:S(2)}) collective-permute-start(f32[512,256]{1,0:T(8,128)} %copy-done.11), channel_id=1, source_target_pairs={{0,1},{1,0},{2,3},{3,2},{4,5},{5,4},{6,7},{7,6},{8,9},{9,8},{10,11... | collective-permute-start | bytes 1572872 | tf_op jit(solution)/shard_map/ppermute | solution.py:215
  91.5 2.1 %copy-start.12 = (f32[512,256]{1,0:T(8,128)}, f32[512,256]{1,0:T(8,128)S(1)}, u32[]{:S(2)}) copy-start(f32[512,256]{1,0:T(8,128)S(1)} %collective-permute-done.14.refs_9_) | copy-start | bytes 1572868
  91.5 2.0 %collective-permute-start.18 = (f32[512,256]{1,0:T(8,128)S(1)}, f32[512,256]{1,0:T(8,128)S(1)}, u32[]{:S(2)}, u32[]{:S(2)}) collective-permute-start(f32[512,256]{1,0:T(8,128)S(1)} %collective-permute-done.14.refs_9_), channel_id=1, source_target_pairs={{0,1},{1,0},{2,3},{3,2},{4,5},{5,4},{6,7},{7,6},{8,9},{9,8},{10,11... | collective-permute-start | bytes 1572872 | tf_op jit(solution)/shard_map/ppermute | solution.py:215
  92.0 1.5 copy-start.13
  93.5 0.8 copy-start.14
  108.8 22.1 %copy-start.21 = (f32[128,256]{1,0:T(8,128)S(1)}, f32[128,256]{1,0:T(8,128)}, u32[]{:S(2)}) copy-start(f32[128,256]{1,0:T(8,128)} %get-tuple-element.50) | copy-start | bytes 393220
  110.0 2.0 %collective-permute-start.20 = (f32[256,512]{1,0:T(8,128)S(1)}, f32[256,512]{1,0:T(8,128)S(1)}, u32[]{:S(2)}, u32[]{:S(2)}) collective-permute-start(f32[256,512]{1,0:T(8,128)S(1)} %constant_dynamic-slice_fusion.3), channel_id=1, source_target_pairs={{0,1},{1,0},{2,3},{3,2},{4,5},{5,4},{6,7},{7,6},{8,9},{9,8},{10,11... | collective-permute-start | bytes 1572872 | tf_op jit(solution)/shard_map/ppermute | solution.py:215
  110.4 20.5 %collective-permute-start.19 = (f32[384,256]{1,0:T(8,128)}, f32[384,256]{1,0:T(8,128)S(1)}, u32[]{:S(2)}, u32[]{:S(2)}) collective-permute-start(f32[384,256]{1,0:T(8,128)} %get-tuple-element.47), channel_id=1, source_target_pairs={{0,16},{8,24},{16,0},{24,8},{1,17},{9,25},{17,1},{25,9},{2,18},{10... | collective-permute-start | bytes 1179656 | tf_op jit(solution)/shard_map/ppermute | solution.py:215
  113.1 27.6 %copy-start.20 = (f32[512,256]{1,0:T(8,128)S(1)}, f32[512,256]{1,0:T(8,128)}, u32[]{:S(2)}) copy-start(f32[512,256]{1,0:T(8,128)} %get-tuple-element.55) | copy-start | bytes 1572868
  113.1 6.4 %collective-permute-start.21 = (f32[64,512]{1,0:T(8,128)S(1)}, f32[64,512]{1,0:T(8,128)S(1)}, u32[]{:S(2)}, u32[]{:S(2)}) collective-permute-start(f32[64,512]{1,0:T(8,128)S(1)} %get-tuple-element.66), channel_id=1, source_target_pairs={{0,2},{1,3},{2,0},{3,1},{4,6},{5,7},{6,4},{7,5},{8,10},{9,11},{10,... | collective-permute-start | bytes 393224 | tf_op jit(solution)/shard_map/ppermute | solution.py:215
  114.4 8.3 %collective-permute-start.22 = (f32[64,512]{1,0:T(8,128)S(1)}, f32[64,512]{1,0:T(8,128)S(1)}, u32[]{:S(2)}, u32[]{:S(2)}) collective-permute-start(f32[64,512]{1,0:T(8,128)S(1)} %get-tuple-element.68), channel_id=1, source_target_pairs={{0,4},{1,5},{2,6},{3,7},{4,0},{5,1},{6,2},{7,3},{8,12},{9,13},{10,... | collective-permute-start | bytes 393224 | tf_op jit(solution)/shard_map/ppermute | solution.py:215
  114.5 8.2 %collective-permute-start.23 = (f32[64,512]{1,0:T(8,128)S(1)}, f32[64,512]{1,0:T(8,128)S(1)}, u32[]{:S(2)}, u32[]{:S(2)}) collective-permute-start(f32[64,512]{1,0:T(8,128)S(1)} %get-tuple-element.67), channel_id=1, source_target_pairs={{0,6},{1,7},{2,4},{3,5},{4,2},{5,3},{6,0},{7,1},{8,14},{9,15},{10,... | collective-permute-start | bytes 393224 | tf_op jit(solution)/shard_map/ppermute | solution.py:215
  122.8 28.5 %copy-start.19 = (f32[512,256]{1,0:T(8,128)S(1)}, f32[512,256]{1,0:T(8,128)}, u32[]{:S(2)}) copy-start(f32[512,256]{1,0:T(8,128)} %get-tuple-element.57) | copy-start | bytes 1572868
  130.9 7.2 %collective-permute-start.25 = (f32[64,512]{1,0:T(8,128)S(1)}, f32[64,512]{1,0:T(8,128)S(1)}, u32[]{:S(2)}, u32[]{:S(2)}) collective-permute-start(f32[64,512]{1,0:T(8,128)S(1)} %add_add_fusion), channel_id=1, source_target_pairs={{0,8},{8,0},{16,24},{24,16},{1,9},{9,1},{17,25},{25,17},{2,10},{10... | collective-permute-start | bytes 393224 | tf_op jit(solution)/shard_map/ppermute | solution.py:215
  130.9 9.2 %collective-permute-start.24 = (f32[128,256]{1,0:T(8,128)S(1)}, f32[128,256]{1,0:T(8,128)S(1)}, u32[]{:S(2)}, u32[]{:S(2)}) collective-permute-start(f32[128,256]{1,0:T(8,128)S(1)} %copy-done.21), channel_id=1, source_target_pairs={{0,16},{8,24},{16,0},{24,8},{1,17},{9,25},{17,1},{25,9},{2,18},{10... | collective-permute-start | bytes 393224 | tf_op jit(solution)/shard_map/ppermute | solution.py:215
  140.1 7.6 %collective-permute-start.27 = (f32[64,512]{1,0:T(8,128)S(1)}, f32[64,512]{1,0:T(8,128)S(1)}, u32[]{:S(2)}, u32[]{:S(2)}) collective-permute-start(f32[64,512]{1,0:T(8,128)S(1)} %add.176), channel_id=1, source_target_pairs={{0,16},{8,24},{16,0},{24,8},{1,17},{9,25},{17,1},{25,9},{2,18},{10... | collective-permute-start | bytes 393224 | tf_op jit(solution)/shard_map/ppermute | solution.py:215
  140.6 15.7 %copy-start.15 = (f32[512,256]{1,0:T(8,128)S(1)}, f32[512,256]{1,0:T(8,128)}, u32[]{:S(2)}) copy-start(f32[512,256]{1,0:T(8,128)} %get-tuple-element.51) | copy-start | bytes 1572868
  140.7 27.1 %collective-permute-start.26 = (f32[512,256]{1,0:T(8,128)S(1)}, f32[512,256]{1,0:T(8,128)S(1)}, u32[]{:S(2)}, u32[]{:S(2)}) collective-permute-start(f32[512,256]{1,0:T(8,128)S(1)} %copy-done.20), channel_id=1, source_target_pairs={{0,8},{8,0},{16,24},{24,16},{1,9},{9,1},{17,25},{25,17},{2,10},{10... | collective-permute-start | bytes 1572872 | tf_op jit(solution)/shard_map/ppermute | solution.py:215
  147.7 6.5 %collective-permute-start.29 = (f32[64,512]{1,0:T(8,128)S(1)}, f32[64,512]{1,0:T(8,128)S(1)}, u32[]{:S(2)}, u32[]{:S(2)}) collective-permute-start(f32[64,512]{1,0:T(8,128)S(1)} %add.177), channel_id=1, source_target_pairs={{0,2},{1,3},{2,0},{3,1},{4,6},{5,7},{6,4},{7,5},{8,10},{9,11},{10,... | collective-permute-start | bytes 393224 | tf_op jit(solution)/shard_map/ppermute | solution.py:215
  148.5 7.6 %collective-permute-start.30 = (f32[64,512]{1,0:T(8,128)S(1)}, f32[64,512]{1,0:T(8,128)S(1)}, u32[]{:S(2)}, u32[]{:S(2)}) collective-permute-start(f32[64,512]{1,0:T(8,128)S(1)} %add.177), channel_id=1, source_target_pairs={{0,4},{1,5},{2,6},{3,7},{4,0},{5,1},{6,2},{7,3},{8,12},{9,13},{10,... | collective-permute-start | bytes 393224 | tf_op jit(solution)/shard_map/ppermute | solution.py:215
  148.5 7.6 %collective-permute-start.31 = (f32[64,512]{1,0:T(8,128)S(1)}, f32[64,512]{1,0:T(8,128)S(1)}, u32[]{:S(2)}, u32[]{:S(2)}) collective-permute-start(f32[64,512]{1,0:T(8,128)S(1)} %add.177), channel_id=1, source_target_pairs={{0,6},{1,7},{2,4},{3,5},{4,2},{5,3},{6,0},{7,1},{8,14},{9,15},{10,... | collective-permute-start | bytes 393224 | tf_op jit(solution)/shard_map/ppermute | solution.py:215
  151.3 16.5 %collective-permute-start.28 = (f32[512,256]{1,0:T(8,128)S(1)}, f32[512,256]{1,0:T(8,128)S(1)}, u32[]{:S(2)}, u32[]{:S(2)}) collective-permute-start(f32[512,256]{1,0:T(8,128)S(1)} %copy-done.19), channel_id=1, source_target_pairs={{0,24},{8,16},{16,8},{24,0},{1,25},{9,17},{17,9},{25,1},{2,26},{10... | collective-permute-start | bytes 1572872 | tf_op jit(solution)/shard_map/ppermute | solution.py:215
  156.2 11.7 %collective-permute-start.32 = (f32[256,512]{1,0:T(8,128)S(1)}, f32[256,512]{1,0:T(8,128)S(1)}, u32[]{:S(2)}, u32[]{:S(2)}) collective-permute-start(f32[256,512]{1,0:T(8,128)S(1)} %maximum_select_fusion.1), channel_id=1, source_target_pairs={{0,1},{1,0},{2,3},{3,2},{4,5},{5,4},{6,7},{7,6},{8,9},{9,8},{10,11... | collective-permute-start | bytes 1572872 | tf_op jit(solution)/shard_map/ppermute | solution.py:215
  167.9 1.7 copy-start.8
where the time goes:
time: 173 us; the launch traced here: 170 us
  waiting for transfers between devices  77.9 us (45%)
  starting transfers between devices  39 us (23%)
  Pallas kernels  27.8 us (16%)
  local copies, waits for them, and re-layouts  10.6 us (6%)
  between operations  8.68 us (5%)
  other arithmetic  5.43 us (3%)
    ppermute x29, waiting for transfers between devices, exchange(): return lax.ppermute(value, axis, [(at, at ^ bit) for at in range(size)])  63.7 us
    pallas_call x2, Pallas kernels, call(): pl.pallas_call(functools.partial(staged, kernel, len(small), len(big), le...  27.8 us
    ppermute x29, starting transfers between devices, exchange(): return lax.ppermute(value, axis, [(at, at ^ bit) for at in range(size)])  26.1 us
    ppermute x4, waiting for transfers between devices, on_device(): got = lax.ppermute(rows, 'col', links)  14.3 us
    ppermute x4, starting transfers between devices, on_device(): got = lax.ppermute(rows, 'col', links)  13 us
  transfers between devices with their start and end apart: 33, of which 16 were waited for; matrix products, arithmetic and copies ran while one was open for 6% of the time, Pallas kernels for 8%

commit v1 on v0

--- a/solution.py
+++ b/solution.py
@@ -27,9 +27,7 @@
         pltpu.make_async_copy(source, target, out_sem.at[at])
         for at, (source, target) in enumerate(zip(made, targets))
     ]
-    for load in loads:
-        load.start()
-    kernel(small, held, made, own, [load.wait for load in loads], [store.start for store in stores])
+    kernel(small, held, made, own, loads, [store.start for store in stores])
     for store in stores:
         store.wait()
 
@@ -69,9 +67,14 @@
     return lax.dot_general(left, right, NT, preferred_element_type=jnp.float32)
 
 
-def split_rows(cuts, pieces, waits, mask, high, low):
-    for (part, first, count), piece, wait in zip(cuts, pieces, waits):
-        wait()
+def begin(loads):
+    for load in loads:
+        load.start()
+
+
+def split_rows(cuts, pieces, loads, mask, high, low):
+    for (part, first, count), piece, load in zip(cuts, pieces, loads):
+        load.wait()
         width = piece.shape[1]
         cols = slice(part * width, (part + 1) * width)
         for start in range(0, count, BLOCK):
@@ -111,19 +114,21 @@
     return value + dot_nt(w_parts[1][...], a_parts[0][cols, :])
 
 
-def early_kernel(cuts, small, held, made, own_scratch, wait, give):
+def early_kernel(cuts, small, held, made, own_scratch, loads, give):
     scalars, vir_col, vir_row, masks = small
     count = len(cuts)
     own_high, own_low, density, *slices = made
     m_high, m_low, amp, a_high, a_low, w_high, w_low = own_scratch
-    split_rows(cuts, held[:count], wait[:count], masks.at[0], own_high, own_low)
+    begin(loads[: 2 * count])
+    split_rows(cuts, held[:count], loads[:count], masks.at[0], own_high, own_low)
+    begin(loads[2 * count :])
     give[0]()
     give[1]()
     nvir = amp.shape[0]
     panel, a_parts, w_parts = (m_high, m_low), (a_high, a_low), (w_high, w_low)
     for turn in range(2):
         where = slice((1 + turn) * count, (2 + turn) * count)
-        split_rows(cuts, held[where], wait[where], masks.at[1 + turn], m_high, m_low)
+        split_rows(cuts, held[where], loads[where], masks.at[1 + turn], m_high, m_low)
         amplitudes(
             scalars[2 * turn], scalars[2 * turn + 1], vir_col, vir_row,
             (own_high, own_low), panel, amp, a_parts, w_parts,
@@ -162,23 +167,26 @@
     return outs[:2], outs[2], list(outs[3:])
 
 
-def late_kernel(cuts, wanted, scale, small, held, made, own_scratch, wait, give):
+def late_kernel(cuts, wanted, scale, small, held, made, own_scratch, loads, give):
     scalars, vir_col, vir_row, masks = small
     count = len(cuts)
     amp, panels = own_scratch[0], (own_scratch[1:7], own_scratch[7:])
-    wait[0]()
-    wait[1]()
+    begin(loads[: 2 + count])
     for turn, (m_high, m_low, a_high, a_low, w_high, w_low) in enumerate(panels):
         where = slice(2 + turn * count, 2 + (1 + turn) * count)
-        split_rows(cuts, held[where], wait[where], masks.at[turn], m_high, m_low)
+        split_rows(cuts, held[where], loads[where], masks.at[turn], m_high, m_low)
+        if turn == 0:
+            loads[0].wait()
+            loads[1].wait()
+            begin(loads[2 + count :])
         amplitudes(
             scalars[2 * turn], scalars[2 * turn + 1], vir_col, vir_row,
             held[:2], (m_high, m_low), amp, (a_high, a_low), (w_high, w_low),
         )
     density, *slices = held[2 + 2 * count :]
     total, *pieces = made
-    for ready in wait[2 + 2 * count :]:
-        ready()
+    for load in loads[2 + 2 * count :]:
+        load.wait()
     for start in range(0, density.shape[0], TILE):
         cols = slice(start, start + TILE)
         value = density[:, cols]
@@ -327,7 +335,8 @@
 
     middle, edge, most = row_count // 2, row_count - 1, nvir // 4 * 3
     wanted = [(middle, 0, most), (middle, most, nvir - most)]
-    wanted += [(at, 0, nvir) for at in range(row_count) if at != middle]
+    wanted += [(edge, at, nvir // 2) for at in (0, nvir // 2)]
+    wanted += [(at, 0, nvir) for at in range(edge) if at != middle]
     scale = 1.0 / (row_count * col_count)
     total, pieces = late(
         cuts, wanted, scale, small[3], vir_energy, small[1], halved, far, far_twin,
@@ -339,16 +348,15 @@
 
     ends = [leave(0)]
     total = scatter_plane(scatter_chip(total))
-    ends.append(leave(1, total))
+    ends += [leave(1, total), leave(2, total)]
     total = after(total, ends[0])
     for bit in bits("row")[:-1]:
         total = total + exchange(total, "row", bit)
     total = after(total, ends[1])
-    ends.append(pieces[2])
-    ends += [leave(at, total) for at in range(3, len(wanted) - 1)]
+    others = [leave(at, total) for at in range(5, len(wanted))]
     total = total + exchange(total, "row", bits("row")[-1])
-    ends.append(leave(len(wanted) - 1, total))
-    total = gather_plane(total)
+    ends += [leave(3, total), pieces[4], *others]
+    total = gather_plane(after(total, ends[2]))
 
     returned = jnp.zeros_like(three_index)
     for (part, first, _), piece in zip(wanted, ends):

time: 173 us -> 172 us (level); the launches traced: 170 us -> 171 us
    ppermute x29 -> x30, starting transfers between devices: 26.1 us -> 26.8 us  [exchange(): return lax.ppermute(value, axis, [(at, at ^ bit) for at in range(size)])]
    ppermute x29 -> x30, waiting for transfers between devices: 63.7 us -> 64 us  [exchange(): return lax.ppermute(value, axis, [(at, at ^ bit) for at in range(size)])]
  transfers between devices with their start and end apart: 33 -> 34, of which waited for: 16 -> 16; matrix products, arithmetic and copies ran while one was open for 6% -> 6% of each run, Pallas kernels for 8% -> 8%
where the time goes in v1:
time: 172 us; the launch traced here: 171 us
  waiting for transfers between devices  78.3 us (46%)
  starting transfers between devices  39.8 us (23%)
  Pallas kernels  27.9 us (16%)
  local copies, waits for them, and re-layouts  10.7 us (6%)
  between operations  8.78 us (5%)
  other arithmetic  5.54 us (3%)
    ppermute x30, waiting for transfers between devices, exchange(): return lax.ppermute(value, axis, [(at, at ^ bit) for at in range(size)])  64 us
    pallas_call x2, Pallas kernels, call(): pl.pallas_call(functools.partial(staged, kernel, len(small), len(big), le...  27.9 us
    ppermute x30, starting transfers between devices, exchange(): return lax.ppermute(value, axis, [(at, at ^ bit) for at in range(size)])  26.8 us
    ppermute x4, waiting for transfers between devices, on_device(): got = lax.ppermute(rows, 'col', links)  14.3 us
    ppermute x4, starting transfers between devices, on_device(): got = lax.ppermute(rows, 'col', links)  12.9 us
  transfers between devices with their start and end apart: 34, of which 16 were waited for; matrix products, arithmetic and copies ran while one was open for 6% of the time, Pallas kernels for 8%

profile of v1, /device:TPU:0, one launch (start us, length us, event | category | flops | bytes accessed | tf_op | source)
XLA Modules:
  0.0 171.0 jit_solution(18135169341559129839)
XLA Ops:
  0.7 2.7 %dynamic-slice_bitcast_fusion = (f32[512,256]{1,0:T(8,128)}, f32[512,256]{1,0:T(8,128)S(1)}, f32[512,256]{1,0:T(8,128)S(1)}, f32[512,256]{1,0:T(8,128)}) fusion(f32[4,512,256]{2,1,0:T(8,128)} %param.5, s32[]{:T(128)S(6)} %select_n.172, s32[]{:T(128)S(6)} %select_n.170, s32[]{:T(128)S(6)} %select_n.164, s32[]{:T(128)S(6)} %select_n.171), kind=kLoop, calls=%fused_computation.7 | loop fusion | bytes 4194320 | tf_op jit(solution)/shard_map/jit(dynamic_index_in_dim)/squeeze | solution.py:303
  3.4 4.9 %collective-permute-start.2 = (f32[512,256]{1,0:T(8,128)S(1)}, f32[512,256]{1,0:T(8,128)S(1)}, u32[]{:S(2)}, u32[]{:S(2)}) collective-permute-start(f32[512,256]{1,0:T(8,128)S(1)} %get-tuple-element.70.refs_4_), channel_id=1, source_target_pairs={{0,4},{1,5},{2,6},{3,7},{8,12},{9,13},{10,14},{11,15},{16,20},{17,... | collective-permute-start | bytes 1572872 | tf_op jit(solution)/shard_map/ppermute | solution.py:321
  8.3 1.6 collective-permute-start
  9.9 1.4 compare_reduce_fusion.1
  12.0 2.7 %collective-permute-start.1 = (f32[512,256]{1,0:T(8,128)}, f32[512,256]{1,0:T(8,128)S(1)}, u32[]{:S(2)}, u32[]{:S(2)}) collective-permute-start(f32[512,256]{1,0:T(8,128)} %get-tuple-element.33), channel_id=1, source_target_pairs={{0,16},{8,24},{16,0},{24,8},{1,17},{9,25},{17,1},{25,9},{2,18},{10... | collective-permute-start | bytes 1572872 | tf_op jit(solution)/shard_map/ppermute | solution.py:223
  14.7 0.1 stack.59
  14.8 0.1 copy.12
  14.9 0.6 gather_fusion
  15.6 0.6 gather_fusion.1
  16.2 0.7 fusion.2
  23.9 0.1 broadcast_in_dim.40
  24.0 0.8 slice.25.refs_3_
  24.8 0.1 broadcast_in_dim.39
  24.9 0.7 slice.22.refs_3_
  25.6 0.7 pad_maximum_fusion.1.refs_0_
  26.3 0.7 pad_maximum_fusion.refs_0_
  27.0 3.5 %collective-permute-done.refs_5_ = f32[512,256]{1,0:T(8,128)S(1)} collective-permute-done((f32[512,256]{1,0:T(8,128)S(1)}, f32[512,256]{1,0:T(8,128)S(1)}, u32[]{:S(2)}, u32[]{:S(2)}) %collective-permute-start) | collective-permute-done | bytes 524320 | tf_op jit(solution)/shard_map/ppermute | solution.py:223
  30.5 2.3 %collective-permute-start.4 = (f32[512,256]{1,0:T(8,128)S(1)}, f32[512,256]{1,0:T(8,128)}, u32[]{:S(2)}, u32[]{:S(2)}) collective-permute-start(f32[512,256]{1,0:T(8,128)S(1)} %collective-permute-done.refs_5_), channel_id=1, source_target_pairs={{0,4},{1,5},{2,6},{3,7},{8,12},{9,13},{10,14},{11,15},{16,20},{17,... | collective-permute-start | bytes 1572872 | tf_op jit(solution)/shard_map/ppermute | solution.py:321
  32.9 1.6 collective-permute-start.11
  34.5 2.5 %collective-permute-start.3 = (f32[512,256]{1,0:T(8,128)}, f32[512,256]{1,0:T(8,128)S(1)}, u32[]{:S(2)}, u32[]{:S(2)}) collective-permute-start(f32[512,256]{1,0:T(8,128)} %get-tuple-element.34), channel_id=1, source_target_pairs={{0,24},{8,16},{16,8},{24,0},{1,25},{9,17},{17,9},{25,1},{2,26},{10... | collective-permute-start | bytes 1572872 | tf_op jit(solution)/shard_map/ppermute | solution.py:223
  36.9 13.6 %collective-permute-done.1.refs_6_ = f32[512,256]{1,0:T(8,128)S(1)} collective-permute-done((f32[512,256]{1,0:T(8,128)}, f32[512,256]{1,0:T(8,128)S(1)}, u32[]{:S(2)}, u32[]{:S(2)}) %collective-permute-start.1) | collective-permute-done | bytes 524320 | tf_op jit(solution)/shard_map/ppermute | solution.py:223
  50.5 1.3 collective-permute-start.5
  52.0 1.6 collective-permute-start.12
  53.5 8.5 %collective-permute-done.5 = f32[512,256]{1,0:T(8,128)S(1)} collective-permute-done((f32[512,256]{1,0:T(8,128)S(1)}, f32[512,256]{1,0:T(8,128)S(1)}, u32[]{:S(2)}, u32[]{:S(2)}) %collective-permute-start.5) | collective-permute-done | bytes 524320 | tf_op jit(solution)/shard_map/ppermute | solution.py:321
  62.1 4.4 %collective-permute-start.6 = (f32[512,256]{1,0:T(8,128)S(1)}, f32[512,256]{1,0:T(8,128)S(1)}, u32[]{:S(2)}, u32[]{:S(2)}) collective-permute-start(f32[512,256]{1,0:T(8,128)S(1)} %collective-permute-done.3.refs_7_), channel_id=1, source_target_pairs={{0,4},{1,5},{2,6},{3,7},{8,12},{9,13},{10,14},{11,15},{16,20},{17,... | collective-permute-start | bytes 1572872 | tf_op jit(solution)/shard_map/ppermute | solution.py:321
  66.8 0.5 collective-permute-start.8
  67.3 0.1 collective-permute-start.9
  67.4 5.8 %collective-permute-done.6 = f32[512,256]{1,0:T(8,128)S(1)} collective-permute-done((f32[512,256]{1,0:T(8,128)S(1)}, f32[512,256]{1,0:T(8,128)S(1)}, u32[]{:S(2)}, u32[]{:S(2)}) %collective-permute-start.6) | collective-permute-done | bytes 524320 | tf_op jit(solution)/shard_map/ppermute | solution.py:321
  73.3 2.5 %collective-permute-done.13.refs_8_ = f32[512,256]{1,0:T(8,128)S(1)} collective-permute-done((f32[512,256]{1,0:T(8,128)S(1)}, f32[512,256]{1,0:T(8,128)S(1)}, u32[]{:S(2)}, u32[]{:S(2)}) %collective-permute-start.13) | collective-permute-done | bytes 524320 | tf_op jit(solution)/shard_map/ppermute | solution.py:223
  75.9 0.4 collective-permute-start.14
  76.3 0.4 copy-done.11
  76.7 0.9 copy.19.refs_1_
  77.6 0.5 collective-permute-start.16
  78.2 13.4 %early.1 = (bf16[512,1024]{1,0:T(8,128)(2,1)}, bf16[512,1024]{1,0:T(8,128)(2,1)}, f32[512,512]{1,0:T(8,128)}, f32[512,256]{1,0:T(8,128)}, f32[512,256]{1,0:T(8,1...) custom-call(f32[4]{0:T(128)} %pad_maximum_fusion.1.refs_0_, f32[512,1]{1,0:T(8,128)} %copy.19.refs_1_, f32[1,512]{1,0:T(1,128)} %bitcast.47, ...), custom_call_target="tpu_custom_call" | custom-call | tf_op jit(solution)/shard_map/early/pallas_call | solution.py:41
  91.6 0.5 collective-permute-start.18
  92.1 1.5 collective-permute-done.18.refs_13_
  93.6 0.8 copy-done.14
  94.5 14.5 %late.1 = (f32[512,512]{1,0:T(8,128)}, f32[384,256]{1,0:T(8,128)}, f32[128,256]{1,0:T(8,128)}, f32[256,256]{1,0:T(8,128)}, f32[256,256]{1,0:T(8,128)}, /*index=5*/f32[512,256]{1,0:T(8,128)}, f32[512,256]{1,0:T(8,128)}) custom-call(f32[4]{0:T(128)} %pad_maximum_fusion.refs_0_, f32[512,1]{1,0:T(8,128)} %copy.19.refs_1_, f32[1,512]{1,0:T(1,128)} %bitcast.48, ...), custom_call_target="tpu_custom_call" | custom-call | tf_op jit(solution)/shard_map/late/pallas_call | solution.py:41
  109.0 1.1 constant_dynamic-slice_fusion.3
  110.1 0.4 collective-permute-start.20
  110.6 0.4 collective-permute-start.19
  111.0 1.1 collective-permute-done.20
  112.1 1.1 dynamic-slice_add_fusion
  113.3 1.3 collective-permute-start.21
  114.7 2.2 %collective-permute-start.23 = (f32[64,512]{1,0:T(8,128)S(1)}, f32[64,512]{1,0:T(8,128)S(1)}, u32[]{:S(2)}, u32[]{:S(2)}) collective-permute-start(f32[64,512]{1,0:T(8,128)S(1)} %get-tuple-element.73), channel_id=1, source_target_pairs={{0,6},{1,7},{2,4},{3,5},{4,2},{5,3},{6,0},{7,1},{8,14},{9,15},{10,... | collective-permute-start | bytes 393224 | tf_op jit(solution)/shard_map/ppermute | solution.py:223
  116.9 2.8 %collective-permute-done.21 = f32[64,512]{1,0:T(8,128)S(1)} collective-permute-done((f32[64,512]{1,0:T(8,128)S(1)}, f32[64,512]{1,0:T(8,128)S(1)}, u32[]{:S(2)}, u32[]{:S(2)}) %collective-permute-start.21) | collective-permute-done | bytes 131104 | tf_op jit(solution)/shard_map/ppermute | solution.py:223
  119.7 3.2 %collective-permute-done.22 = f32[64,512]{1,0:T(8,128)S(1)} collective-permute-done((f32[64,512]{1,0:T(8,128)S(1)}, f32[64,512]{1,0:T(8,128)S(1)}, u32[]{:S(2)}, u32[]{:S(2)}) %collective-permute-start.22) | collective-permute-done | bytes 131104 | tf_op jit(solution)/shard_map/ppermute | solution.py:223
  123.0 8.2 %collective-permute-done.19 = f32[384,256]{1,0:T(8,128)S(1)} collective-permute-done((f32[384,256]{1,0:T(8,128)}, f32[384,256]{1,0:T(8,128)S(1)}, u32[]{:S(2)}, u32[]{:S(2)}) %collective-permute-start.19) | collective-permute-done | bytes 393248 | tf_op jit(solution)/shard_map/ppermute | solution.py:223
  131.1 2.1 %collective-permute-start.24 = (f32[128,256]{1,0:T(8,128)S(1)}, f32[128,256]{1,0:T(8,128)S(1)}, u32[]{:S(2)}, u32[]{:S(2)}) collective-permute-start(f32[128,256]{1,0:T(8,128)S(1)} %copy-done.22), channel_id=1, source_target_pairs={{0,16},{8,24},{16,0},{24,8},{1,17},{9,25},{17,1},{25,9},{2,18},{10... | collective-permute-start | bytes 393224 | tf_op jit(solution)/shard_map/ppermute | solution.py:223
  133.2 2.3 %collective-permute-start.25 = (f32[256,256]{1,0:T(8,128)S(1)}, f32[256,256]{1,0:T(8,128)S(1)}, u32[]{:S(2)}, u32[]{:S(2)}) collective-permute-start(f32[256,256]{1,0:T(8,128)S(1)} %copy-done.21), channel_id=1, source_target_pairs={{0,24},{8,16},{16,8},{24,0},{1,25},{9,17},{17,9},{25,1},{2,26},{10... | collective-permute-start | bytes 786440 | tf_op jit(solution)/shard_map/ppermute | solution.py:223
  135.5 0.2 broadcast_in_dim.36
  135.7 2.6 %collective-permute-done.26 = f32[64,512]{1,0:T(8,128)S(1)} collective-permute-done((f32[64,512]{1,0:T(8,128)S(1)}, f32[64,512]{1,0:T(8,128)S(1)}, u32[]{:S(2)}, u32[]{:S(2)}) %collective-permute-start.26) | collective-permute-done | bytes 131104 | tf_op jit(solution)/shard_map/ppermute | solution.py:223
  138.3 10.0 %collective-permute-done.24 = f32[128,256]{1,0:T(8,128)S(1)} collective-permute-done((f32[128,256]{1,0:T(8,128)S(1)}, f32[128,256]{1,0:T(8,128)S(1)}, u32[]{:S(2)}, u32[]{:S(2)}) %collective-permute-start.24) | collective-permute-done | bytes 131104 | tf_op jit(solution)/shard_map/ppermute | solution.py:223
  148.3 0.7 collective-permute-start.29
  149.0 8.3 %collective-permute-done.27 = f32[64,512]{1,0:T(8,128)S(1)} collective-permute-done((f32[64,512]{1,0:T(8,128)S(1)}, f32[64,512]{1,0:T(8,128)S(1)}, u32[]{:S(2)}, u32[]{:S(2)}) %collective-permute-start.27) | collective-permute-done | bytes 131104 | tf_op jit(solution)/shard_map/ppermute | solution.py:223
  157.3 1.3 collective-permute-start.30
  158.6 0.1 collective-permute-start.31
  158.7 2.2 %collective-permute-start.32 = (f32[64,512]{1,0:T(8,128)S(1)}, f32[64,512]{1,0:T(8,128)S(1)}, u32[]{:S(2)}, u32[]{:S(2)}) collective-permute-start(f32[64,512]{1,0:T(8,128)S(1)} %add.178), channel_id=1, source_target_pairs={{0,6},{1,7},{2,4},{3,5},{4,2},{5,3},{6,0},{7,1},{8,14},{9,15},{10,... | collective-permute-start | bytes 393224 | tf_op jit(solution)/shard_map/ppermute | solution.py:223
  160.9 1.5 collective-permute-start.28
  162.4 1.1 collective-permute-done.30
  163.5 2.2 %collective-permute-done.31 = f32[64,512]{1,0:T(8,128)S(1)} collective-permute-done((f32[64,512]{1,0:T(8,128)S(1)}, f32[64,512]{1,0:T(8,128)S(1)}, u32[]{:S(2)}, u32[]{:S(2)}) %collective-permute-start.31) | collective-permute-done | bytes 131104 | tf_op jit(solution)/shard_map/ppermute | solution.py:223
  165.9 3.3 %collective-permute-done.28 = f32[256,256]{1,0:T(8,128)S(1)} collective-permute-done((f32[256,256]{1,0:T(8,128)S(1)}, f32[256,256]{1,0:T(8,128)S(1)}, u32[]{:S(2)}, u32[]{:S(2)}) %collective-permute-start.28) | collective-permute-done | bytes 262176 | tf_op jit(solution)/shard_map/ppermute | solution.py:223
  169.4 1.2 maximum_select_fusion
  170.6 0.4 copy-done.8
  (99 shorter events, 1.5 us)
Async XLA Ops:
  0.7 14.1 %copy-start.16 = (s32[32,8,16]{0,2,1:T(8,128)S(1)}, s32[32,8,16]{0,2,1:T(8,128)}, u32[]{:S(2)}) copy-start(s32[32,8,16]{0,2,1:T(8,128)} %param.8) | copy-start | bytes 49156
  0.7 15.5 %copy-start.18 = (f32[32]{0:T(128)S(1)}, f32[32]{0:T(128)}, u32[]{:S(2)}) copy-start(f32[32]{0:T(128)} %param.6) | copy-start | bytes 388
  3.4 48.6 %copy-start = (f32[512,256]{1,0:T(8,128)}, f32[512,256]{1,0:T(8,128)S(1)}, u32[]{:S(2)}) copy-start(f32[512,256]{1,0:T(8,128)S(1)} %get-tuple-element.70.refs_4_) | copy-start | bytes 1572868
  3.4 23.6 %collective-permute-start.2 = (f32[512,256]{1,0:T(8,128)S(1)}, f32[512,256]{1,0:T(8,128)S(1)}, u32[]{:S(2)}, u32[]{:S(2)}) collective-permute-start(f32[512,256]{1,0:T(8,128)S(1)} %get-tuple-element.70.refs_4_), channel_id=1, source_target_pairs={{0,4},{1,5},{2,6},{3,7},{8,12},{9,13},{10,14},{11,15},{16,20},{17,... | collective-permute-start | bytes 1572872 | tf_op jit(solution)/shard_map/ppermute | solution.py:321
  8.3 22.2 %collective-permute-start = (f32[512,256]{1,0:T(8,128)S(1)}, f32[512,256]{1,0:T(8,128)S(1)}, u32[]{:S(2)}, u32[]{:S(2)}) collective-permute-start(f32[512,256]{1,0:T(8,128)S(1)} %get-tuple-element.69), channel_id=1, source_target_pairs={{0,8},{8,0},{16,24},{24,16},{1,9},{9,1},{17,25},{25,17},{2,10},{10... | collective-permute-start | bytes 1572872 | tf_op jit(solution)/shard_map/ppermute | solution.py:223
  12.0 38.5 %collective-permute-start.1 = (f32[512,256]{1,0:T(8,128)}, f32[512,256]{1,0:T(8,128)S(1)}, u32[]{:S(2)}, u32[]{:S(2)}) collective-permute-start(f32[512,256]{1,0:T(8,128)} %get-tuple-element.33), channel_id=1, source_target_pairs={{0,16},{8,24},{16,0},{24,8},{1,17},{9,25},{17,1},{25,9},{2,18},{10... | collective-permute-start | bytes 1572872 | tf_op jit(solution)/shard_map/ppermute | solution.py:223
  30.5 36.1 %copy-start.1 = (f32[512,256]{1,0:T(8,128)}, f32[512,256]{1,0:T(8,128)S(1)}, u32[]{:S(2)}) copy-start(f32[512,256]{1,0:T(8,128)S(1)} %collective-permute-done.refs_5_) | copy-start | bytes 1572868
  30.5 20.1 %collective-permute-start.4 = (f32[512,256]{1,0:T(8,128)S(1)}, f32[512,256]{1,0:T(8,128)}, u32[]{:S(2)}, u32[]{:S(2)}) collective-permute-start(f32[512,256]{1,0:T(8,128)S(1)} %collective-permute-done.refs_5_), channel_id=1, source_target_pairs={{0,4},{1,5},{2,6},{3,7},{8,12},{9,13},{10,14},{11,15},{16,20},{17,... | collective-permute-start | bytes 1572872 | tf_op jit(solution)/shard_map/ppermute | solution.py:321
  32.9 40.3 %copy-start.3 = (f32[512,256]{1,0:T(8,128)}, f32[512,256]{1,0:T(8,128)S(1)}, u32[]{:S(2)}) copy-start(f32[512,256]{1,0:T(8,128)S(1)} %broadcast_select_fusion.3.refs_8_) | copy-start | bytes 1572868
  32.9 19.1 %collective-permute-start.11 = (f32[512,256]{1,0:T(8,128)S(1)}, f32[512,256]{1,0:T(8,128)S(1)}, u32[]{:S(2)}, u32[]{:S(2)}) collective-permute-start(f32[512,256]{1,0:T(8,128)S(1)} %broadcast_select_fusion.3.refs_8_), channel_id=1, source_target_pairs={{0,2},{1,3},{2,0},{3,1},{4,6},{5,7},{6,4},{7,5},{8,10},{9,11},{10,... | collective-permute-start | bytes 1572872 | tf_op jit(solution)/shard_map/ppermute | solution.py:223
  34.4 42.2 %copy-start.17 = (f32[512]{0:T(512)S(1)}, f32[512]{0:T(512)}, u32[]{:S(2)}) copy-start(f32[512]{0:T(512)} %param.7) | copy-start | bytes 6148
  34.5 19.1 %collective-permute-start.3 = (f32[512,256]{1,0:T(8,128)}, f32[512,256]{1,0:T(8,128)S(1)}, u32[]{:S(2)}, u32[]{:S(2)}) collective-permute-start(f32[512,256]{1,0:T(8,128)} %get-tuple-element.34), channel_id=1, source_target_pairs={{0,24},{8,16},{16,8},{24,0},{1,25},{9,17},{17,9},{25,1},{2,26},{10... | collective-permute-start | bytes 1572872 | tf_op jit(solution)/shard_map/ppermute | solution.py:223
  50.5 22.7 %copy-start.2 = (f32[512,256]{1,0:T(8,128)}, f32[512,256]{1,0:T(8,128)S(1)}, u32[]{:S(2)}) copy-start(f32[512,256]{1,0:T(8,128)S(1)} %collective-permute-done.1.refs_6_) | copy-start | bytes 1572868
  50.5 11.6 %collective-permute-start.5 = (f32[512,256]{1,0:T(8,128)S(1)}, f32[512,256]{1,0:T(8,128)S(1)}, u32[]{:S(2)}, u32[]{:S(2)}) collective-permute-start(f32[512,256]{1,0:T(8,128)S(1)} %collective-permute-done.1.refs_6_), channel_id=1, source_target_pairs={{0,4},{1,5},{2,6},{3,7},{8,12},{9,13},{10,14},{11,15},{16,20},{17,... | collective-permute-start | bytes 1572872 | tf_op jit(solution)/shard_map/ppermute | solution.py:321
  51.9 26.2 %copy-start.5 = (f32[512,256]{1,0:T(8,128)}, f32[512,256]{1,0:T(8,128)S(1)}, u32[]{:S(2)}) copy-start(f32[512,256]{1,0:T(8,128)S(1)} %broadcast_select_fusion.2.refs_9_) | copy-start | bytes 1572868
  52.0 23.9 %copy-start.9 = (f32[512,256]{1,0:T(8,128)}, f32[512,256]{1,0:T(8,128)S(1)}, u32[]{:S(2)}) copy-start(f32[512,256]{1,0:T(8,128)S(1)} %collective-permute-done.11.refs_6_) | copy-start | bytes 1572868
  52.0 14.6 %collective-permute-start.12 = (f32[512,256]{1,0:T(8,128)S(1)}, f32[512,256]{1,0:T(8,128)S(1)}, u32[]{:S(2)}, u32[]{:S(2)}) collective-permute-start(f32[512,256]{1,0:T(8,128)S(1)} %broadcast_select_fusion.2.refs_9_), channel_id=1, source_target_pairs={{0,2},{1,3},{2,0},{3,1},{4,6},{5,7},{6,4},{7,5},{8,10},{9,11},{10,... | collective-permute-start | bytes 1572872 | tf_op jit(solution)/shard_map/ppermute | solution.py:223
  53.5 24.6 %copy-start.4 = (f32[512,256]{1,0:T(8,128)}, f32[512,256]{1,0:T(8,128)S(1)}, u32[]{:S(2)}) copy-start(f32[512,256]{1,0:T(8,128)S(1)} %collective-permute-done.3.refs_7_) | copy-start | bytes 1572868
  62.1 11.1 %collective-permute-start.6 = (f32[512,256]{1,0:T(8,128)S(1)}, f32[512,256]{1,0:T(8,128)S(1)}, u32[]{:S(2)}, u32[]{:S(2)}) collective-permute-start(f32[512,256]{1,0:T(8,128)S(1)} %collective-permute-done.3.refs_7_), channel_id=1, source_target_pairs={{0,4},{1,5},{2,6},{3,7},{8,12},{9,13},{10,14},{11,15},{16,20},{17,... | collective-permute-start | bytes 1572872 | tf_op jit(solution)/shard_map/ppermute | solution.py:321
  66.6 11.6 %copy-start.6 = (f32[512,256]{1,0:T(8,128)}, f32[512,256]{1,0:T(8,128)S(1)}, u32[]{:S(2)}) copy-start(f32[512,256]{1,0:T(8,128)S(1)} %broadcast_select_fusion.1.refs_10_) | copy-start | bytes 1572868
  66.6 9.7 %copy-start.10 = (f32[512,256]{1,0:T(8,128)}, f32[512,256]{1,0:T(8,128)S(1)}, u32[]{:S(2)}) copy-start(f32[512,256]{1,0:T(8,128)S(1)} %collective-permute-done.12.refs_7_) | copy-start | bytes 1572868
  66.6 9.2 %collective-permute-start.13 = (f32[512,256]{1,0:T(8,128)S(1)}, f32[512,256]{1,0:T(8,128)S(1)}, u32[]{:S(2)}, u32[]{:S(2)}) collective-permute-start(f32[512,256]{1,0:T(8,128)S(1)} %broadcast_select_fusion.1.refs_10_), channel_id=1, source_target_pairs={{0,2},{1,3},{2,0},{3,1},{4,6},{5,7},{6,4},{7,5},{8,10},{9,11},{10,... | collective-permute-start | bytes 1572872 | tf_op jit(solution)/shard_map/ppermute | solution.py:223
  66.7 10.9 %collective-permute-start.7 = (f32[512,256]{1,0:T(8,128)S(1)}, f32[512,256]{1,0:T(8,128)}, u32[]{:S(2)}, u32[]{:S(2)}) collective-permute-start(f32[512,256]{1,0:T(8,128)S(1)} %broadcast_select_fusion.3.refs_8_), channel_id=1, source_target_pairs={{0,1},{1,0},{2,3},{3,2},{4,5},{5,4},{6,7},{7,6},{8,9},{9,8},{10,11... | collective-permute-start | bytes 1572872 | tf_op jit(solution)/shard_map/ppermute | solution.py:223
  66.8 10.8 %collective-permute-start.8 = (f32[512,256]{1,0:T(8,128)S(1)}, f32[512,256]{1,0:T(8,128)}, u32[]{:S(2)}, u32[]{:S(2)}) collective-permute-start(f32[512,256]{1,0:T(8,128)S(1)} %broadcast_select_fusion.2.refs_9_), channel_id=1, source_target_pairs={{0,1},{1,0},{2,3},{3,2},{4,5},{5,4},{6,7},{7,6},{8,9},{9,8},{10,11... | collective-permute-start | bytes 1572872 | tf_op jit(solution)/shard_map/ppermute | solution.py:223
  67.3 10.8 %collective-permute-start.9 = (f32[512,256]{1,0:T(8,128)S(1)}, f32[512,256]{1,0:T(8,128)}, u32[]{:S(2)}, u32[]{:S(2)}) collective-permute-start(f32[512,256]{1,0:T(8,128)S(1)} %broadcast_select_fusion.1.refs_10_), channel_id=1, source_target_pairs={{0,1},{1,0},{2,3},{3,2},{4,5},{5,4},{6,7},{7,6},{8,9},{9,8},{10,11... | collective-permute-start | bytes 1572872 | tf_op jit(solution)/shard_map/ppermute | solution.py:223
  73.2 4.9 %copy-start.7 = (f32[512,256]{1,0:T(8,128)}, f32[512,256]{1,0:T(8,128)S(1)}, u32[]{:S(2)}) copy-start(f32[512,256]{1,0:T(8,128)S(1)} %broadcast_select_fusion.refs_11_) | copy-start | bytes 1572868
  73.3 4.9 %collective-permute-start.10 = (f32[512,256]{1,0:T(8,128)S(1)}, f32[512,256]{1,0:T(8,128)}, u32[]{:S(2)}, u32[]{:S(2)}) collective-permute-start(f32[512,256]{1,0:T(8,128)S(1)} %broadcast_select_fusion.refs_11_), channel_id=1, source_target_pairs={{0,1},{1,0},{2,3},{3,2},{4,5},{5,4},{6,7},{7,6},{8,9},{9,8},{10,11... | collective-permute-start | bytes 1572872 | tf_op jit(solution)/shard_map/ppermute | solution.py:223
  75.9 0.8 copy-start.11
  75.9 15.7 %collective-permute-start.14 = (f32[512,256]{1,0:T(8,128)S(1)}, f32[512,256]{1,0:T(8,128)S(1)}, u32[]{:S(2)}, u32[]{:S(2)}) collective-permute-start(f32[512,256]{1,0:T(8,128)S(1)} %broadcast_select_fusion.refs_11_), channel_id=1, source_target_pairs={{0,2},{1,3},{2,0},{3,1},{4,6},{5,7},{6,4},{7,5},{8,10},{9,11},{10,... | collective-permute-start | bytes 1572872 | tf_op jit(solution)/shard_map/ppermute | solution.py:223
  77.6 14.5 %collective-permute-start.15 = (f32[512,256]{1,0:T(8,128)}, f32[512,256]{1,0:T(8,128)S(1)}, u32[]{:S(2)}, u32[]{:S(2)}) collective-permute-start(f32[512,256]{1,0:T(8,128)} %copy-done.9), channel_id=1, source_target_pairs={{0,1},{1,0},{2,3},{3,2},{4,5},{5,4},{6,7},{7,6},{8,9},{9,8},{10,11... | collective-permute-start | bytes 1572872 | tf_op jit(solution)/shard_map/ppermute | solution.py:223
  77.6 14.5 %collective-permute-start.16 = (f32[512,256]{1,0:T(8,128)}, f32[512,256]{1,0:T(8,128)}, u32[]{:S(2)}, u32[]{:S(2)}) collective-permute-start(f32[512,256]{1,0:T(8,128)} %copy-done.10), channel_id=1, source_target_pairs={{0,1},{1,0},{2,3},{3,2},{4,5},{5,4},{6,7},{7,6},{8,9},{9,8},{10,11... | collective-permute-start | bytes 1572872 | tf_op jit(solution)/shard_map/ppermute | solution.py:223
  78.1 14.0 %collective-permute-start.17 = (f32[512,256]{1,0:T(8,128)}, f32[512,256]{1,0:T(8,128)}, u32[]{:S(2)}, u32[]{:S(2)}) collective-permute-start(f32[512,256]{1,0:T(8,128)} %copy-done.11), channel_id=1, source_target_pairs={{0,1},{1,0},{2,3},{3,2},{4,5},{5,4},{6,7},{7,6},{8,9},{9,8},{10,11... | collective-permute-start | bytes 1572872 | tf_op jit(solution)/shard_map/ppermute | solution.py:223
  91.6 2.1 %copy-start.12 = (f32[512,256]{1,0:T(8,128)}, f32[512,256]{1,0:T(8,128)S(1)}, u32[]{:S(2)}) copy-start(f32[512,256]{1,0:T(8,128)S(1)} %collective-permute-done.14.refs_9_) | copy-start | bytes 1572868
  91.6 2.0 %collective-permute-start.18 = (f32[512,256]{1,0:T(8,128)S(1)}, f32[512,256]{1,0:T(8,128)S(1)}, u32[]{:S(2)}, u32[]{:S(2)}) collective-permute-start(f32[512,256]{1,0:T(8,128)S(1)} %collective-permute-done.14.refs_9_), channel_id=1, source_target_pairs={{0,1},{1,0},{2,3},{3,2},{4,5},{5,4},{6,7},{7,6},{8,9},{9,8},{10,11... | collective-permute-start | bytes 1572872 | tf_op jit(solution)/shard_map/ppermute | solution.py:223
  92.1 1.5 copy-start.13
  93.6 0.8 copy-start.14
  109.0 22.1 %copy-start.22 = (f32[128,256]{1,0:T(8,128)S(1)}, f32[128,256]{1,0:T(8,128)}, u32[]{:S(2)}) copy-start(f32[128,256]{1,0:T(8,128)} %get-tuple-element.53) | copy-start | bytes 393220
  109.0 24.2 %copy-start.21 = (f32[256,256]{1,0:T(8,128)S(1)}, f32[256,256]{1,0:T(8,128)}, u32[]{:S(2)}) copy-start(f32[256,256]{1,0:T(8,128)} %get-tuple-element.55) | copy-start | bytes 786436
  110.1 2.0 %collective-permute-start.20 = (f32[256,512]{1,0:T(8,128)S(1)}, f32[256,512]{1,0:T(8,128)S(1)}, u32[]{:S(2)}, u32[]{:S(2)}) collective-permute-start(f32[256,512]{1,0:T(8,128)S(1)} %constant_dynamic-slice_fusion.3), channel_id=1, source_target_pairs={{0,1},{1,0},{2,3},{3,2},{4,5},{5,4},{6,7},{7,6},{8,9},{9,8},{10,11... | collective-permute-start | bytes 1572872 | tf_op jit(solution)/shard_map/ppermute | solution.py:223
  110.6 20.5 %collective-permute-start.19 = (f32[384,256]{1,0:T(8,128)}, f32[384,256]{1,0:T(8,128)S(1)}, u32[]{:S(2)}, u32[]{:S(2)}) collective-permute-start(f32[384,256]{1,0:T(8,128)} %get-tuple-element.50), channel_id=1, source_target_pairs={{0,16},{8,24},{16,0},{24,8},{1,17},{9,25},{17,1},{25,9},{2,18},{10... | collective-permute-start | bytes 1179656 | tf_op jit(solution)/shard_map/ppermute | solution.py:223
  113.3 35.0 %copy-start.19 = (f32[512,256]{1,0:T(8,128)S(1)}, f32[512,256]{1,0:T(8,128)}, u32[]{:S(2)}) copy-start(f32[512,256]{1,0:T(8,128)} %get-tuple-element.62) | copy-start | bytes 1572868
  113.3 6.4 %collective-permute-start.21 = (f32[64,512]{1,0:T(8,128)S(1)}, f32[64,512]{1,0:T(8,128)S(1)}, u32[]{:S(2)}, u32[]{:S(2)}) collective-permute-start(f32[64,512]{1,0:T(8,128)S(1)} %get-tuple-element.72), channel_id=1, source_target_pairs={{0,2},{1,3},{2,0},{3,1},{4,6},{5,7},{6,4},{7,5},{8,10},{9,11},{10,... | collective-permute-start | bytes 393224 | tf_op jit(solution)/shard_map/ppermute | solution.py:223
  114.6 8.3 %collective-permute-start.22 = (f32[64,512]{1,0:T(8,128)S(1)}, f32[64,512]{1,0:T(8,128)S(1)}, u32[]{:S(2)}, u32[]{:S(2)}) collective-permute-start(f32[64,512]{1,0:T(8,128)S(1)} %get-tuple-element.74), channel_id=1, source_target_pairs={{0,4},{1,5},{2,6},{3,7},{4,0},{5,1},{6,2},{7,3},{8,12},{9,13},{10,... | collective-permute-start | bytes 393224 | tf_op jit(solution)/shard_map/ppermute | solution.py:223
  114.7 8.2 %collective-permute-start.23 = (f32[64,512]{1,0:T(8,128)S(1)}, f32[64,512]{1,0:T(8,128)S(1)}, u32[]{:S(2)}, u32[]{:S(2)}) collective-permute-start(f32[64,512]{1,0:T(8,128)S(1)} %get-tuple-element.73), channel_id=1, source_target_pairs={{0,6},{1,7},{2,4},{3,5},{4,2},{5,3},{6,0},{7,1},{8,14},{9,15},{10,... | collective-permute-start | bytes 393224 | tf_op jit(solution)/shard_map/ppermute | solution.py:223
  122.9 37.9 %copy-start.20 = (f32[256,256]{1,0:T(8,128)S(1)}, f32[256,256]{1,0:T(8,128)}, u32[]{:S(2)}) copy-start(f32[256,256]{1,0:T(8,128)} %get-tuple-element.59) | copy-start | bytes 786436
  131.1 7.2 %collective-permute-start.26 = (f32[64,512]{1,0:T(8,128)S(1)}, f32[64,512]{1,0:T(8,128)S(1)}, u32[]{:S(2)}, u32[]{:S(2)}) collective-permute-start(f32[64,512]{1,0:T(8,128)S(1)} %add_add_fusion), channel_id=1, source_target_pairs={{0,8},{8,0},{16,24},{24,16},{1,9},{9,1},{17,25},{25,17},{2,10},{10... | collective-permute-start | bytes 393224 | tf_op jit(solution)/shard_map/ppermute | solution.py:223
  131.1 17.1 %collective-permute-start.24 = (f32[128,256]{1,0:T(8,128)S(1)}, f32[128,256]{1,0:T(8,128)S(1)}, u32[]{:S(2)}, u32[]{:S(2)}) collective-permute-start(f32[128,256]{1,0:T(8,128)S(1)} %copy-done.22), channel_id=1, source_target_pairs={{0,16},{8,24},{16,0},{24,8},{1,17},{9,25},{17,1},{25,9},{2,18},{10... | collective-permute-start | bytes 393224 | tf_op jit(solution)/shard_map/ppermute | solution.py:223
  133.2 24.1 %collective-permute-start.25 = (f32[256,256]{1,0:T(8,128)S(1)}, f32[256,256]{1,0:T(8,128)S(1)}, u32[]{:S(2)}, u32[]{:S(2)}) collective-permute-start(f32[256,256]{1,0:T(8,128)S(1)} %copy-done.21), channel_id=1, source_target_pairs={{0,24},{8,16},{16,8},{24,0},{1,25},{9,17},{17,9},{25,1},{2,26},{10... | collective-permute-start | bytes 786440 | tf_op jit(solution)/shard_map/ppermute | solution.py:223
  135.7 33.5 %copy-start.15 = (f32[512,256]{1,0:T(8,128)S(1)}, f32[512,256]{1,0:T(8,128)}, u32[]{:S(2)}) copy-start(f32[512,256]{1,0:T(8,128)} %get-tuple-element.60) | copy-start | bytes 1572868
  148.3 9.0 %collective-permute-start.27 = (f32[64,512]{1,0:T(8,128)S(1)}, f32[64,512]{1,0:T(8,128)S(1)}, u32[]{:S(2)}, u32[]{:S(2)}) collective-permute-start(f32[64,512]{1,0:T(8,128)S(1)} %add.177), channel_id=1, source_target_pairs={{0,16},{8,24},{16,0},{24,8},{1,17},{9,25},{17,1},{25,9},{2,18},{10... | collective-permute-start | bytes 393224 | tf_op jit(solution)/shard_map/ppermute | solution.py:223
  148.3 21.0 %collective-permute-start.29 = (f32[512,256]{1,0:T(8,128)S(1)}, f32[512,256]{1,0:T(8,128)S(1)}, u32[]{:S(2)}, u32[]{:S(2)}) collective-permute-start(f32[512,256]{1,0:T(8,128)S(1)} %copy-done.19), channel_id=1, source_target_pairs={{0,8},{8,0},{16,24},{24,16},{1,9},{9,1},{17,25},{25,17},{2,10},{10... | collective-permute-start | bytes 1572872 | tf_op jit(solution)/shard_map/ppermute | solution.py:223
  157.3 6.2 %collective-permute-start.30 = (f32[64,512]{1,0:T(8,128)S(1)}, f32[64,512]{1,0:T(8,128)S(1)}, u32[]{:S(2)}, u32[]{:S(2)}) collective-permute-start(f32[64,512]{1,0:T(8,128)S(1)} %add.178), channel_id=1, source_target_pairs={{0,2},{1,3},{2,0},{3,1},{4,6},{5,7},{6,4},{7,5},{8,10},{9,11},{10,... | collective-permute-start | bytes 393224 | tf_op jit(solution)/shard_map/ppermute | solution.py:223
  158.6 7.1 %collective-permute-start.31 = (f32[64,512]{1,0:T(8,128)S(1)}, f32[64,512]{1,0:T(8,128)S(1)}, u32[]{:S(2)}, u32[]{:S(2)}) collective-permute-start(f32[64,512]{1,0:T(8,128)S(1)} %add.178), channel_id=1, source_target_pairs={{0,4},{1,5},{2,6},{3,7},{4,0},{5,1},{6,2},{7,3},{8,12},{9,13},{10,... | collective-permute-start | bytes 393224 | tf_op jit(solution)/shard_map/ppermute | solution.py:223
  158.7 7.1 %collective-permute-start.32 = (f32[64,512]{1,0:T(8,128)S(1)}, f32[64,512]{1,0:T(8,128)S(1)}, u32[]{:S(2)}, u32[]{:S(2)}) collective-permute-start(f32[64,512]{1,0:T(8,128)S(1)} %add.178), channel_id=1, source_target_pairs={{0,6},{1,7},{2,4},{3,5},{4,2},{5,3},{6,0},{7,1},{8,14},{9,15},{10,... | collective-permute-start | bytes 393224 | tf_op jit(solution)/shard_map/ppermute | solution.py:223
  160.9 8.4 %collective-permute-start.28 = (f32[256,256]{1,0:T(8,128)S(1)}, f32[256,256]{1,0:T(8,128)S(1)}, u32[]{:S(2)}, u32[]{:S(2)}) collective-permute-start(f32[256,256]{1,0:T(8,128)S(1)} %copy-done.20), channel_id=1, source_target_pairs={{0,24},{8,16},{16,8},{24,0},{1,25},{9,17},{17,9},{25,1},{2,26},{10... | collective-permute-start | bytes 786440 | tf_op jit(solution)/shard_map/ppermute | solution.py:223
  165.8 3.6 %collective-permute-start.33 = (f32[256,512]{1,0:T(8,128)S(1)}, f32[256,512]{1,0:T(8,128)S(1)}, u32[]{:S(2)}, u32[]{:S(2)}) collective-permute-start(f32[256,512]{1,0:T(8,128)S(1)} %maximum_select_fusion.1), channel_id=1, source_target_pairs={{0,1},{1,0},{2,3},{3,2},{4,5},{5,4},{6,7},{7,6},{8,9},{9,8},{10,11... | collective-permute-start | bytes 1572872 | tf_op jit(solution)/shard_map/ppermute | solution.py:223
  169.4 1.7 copy-start.8

commit v2 on v1

--- a/solution.py
+++ b/solution.py
@@ -227,6 +227,12 @@
     return lax.optimization_barrier((value, *others))[0]
 
 
+def across(value, inner):
+    edge = lax.axis_size("row") - 1
+    pairs = [(at, edge - at) for at in range(edge + 1)]
+    return lax.ppermute(value, "row", [at for at in pairs if (abs(at[0] - at[1]) == 1) == inner])
+
+
 def bits(axis):
     size = lax.axis_size(axis)
     return [1 << at for at in range(size.bit_length() - 1)]
@@ -269,7 +275,7 @@
 
 
 def cut_list(nvir, row_count):
-    return [(part, 0, nvir) for part in range(row_count)]
+    return [(part, 0, nvir) for part in (0, 1, row_count - 1, *range(2, row_count - 1))]
 
 
 def on_device(three_index, occ_energy, vir_energy, block_mask, pair_list):
@@ -299,17 +305,16 @@
     own, came, near, far = [], [], [], []
 
     def receive(at):
-        part, first, count = cuts[at]
+        part = cuts[at][0]
         rows = lax.dynamic_index_in_dim(three_index, row ^ part, 0, keepdims=False)
-        rows = rows[first : first + count]
         if part == row_count - 1:
-            rows = after(rows, near[0])
-        elif part > 1:
-            rows = after(rows, scalars[1])
-        own.append(exchange(rows, "row", part) if part else rows)
+            rows = across(rows, True) + across(after(rows, scalars[1]), False)
+        elif part:
+            rows = exchange(after(rows, *near[:1]), "row", part)
+        own.append(rows)
 
     for at in range(len(cuts)):
-        while len(own) < min(at + 1 if at > 1 else row_count - 1, len(cuts)):
+        while len(own) < (len(cuts) if at else 3):
             receive(len(own))
         rows = own[at]
         if at:
@@ -333,30 +338,26 @@
     far_twin = [exchange(piece, "col", 1) for piece in far[:-1]]
     far_twin.append(exchange(after(far[-1], density), "col", 1))
 
-    middle, edge, most = row_count // 2, row_count - 1, nvir // 4 * 3
-    wanted = [(middle, 0, most), (middle, most, nvir - most)]
-    wanted += [(edge, at, nvir // 2) for at in (0, nvir // 2)]
-    wanted += [(at, 0, nvir) for at in range(edge) if at != middle]
+    wanted = [cuts[at] for at in (2, 1, *range(3, len(cuts)), 0)]
     scale = 1.0 / (row_count * col_count)
     total, pieces = late(
         cuts, wanted, scale, small[3], vir_energy, small[1], halved, far, far_twin,
         density, slices,
     )
 
-    def leave(at, *others):
-        return exchange(after(pieces[at], *others), "row", wanted[at][0])
-
-    ends = [leave(0)]
+    inner, first = across(pieces[0], True), exchange(pieces[1], "row", 1)
     total = scatter_plane(scatter_chip(total))
-    ends += [leave(1, total), leave(2, total)]
-    total = after(total, ends[0])
+    outer = across(after(pieces[0], total), False)
+    total = after(total, inner, first)
     for bit in bits("row")[:-1]:
         total = total + exchange(total, "row", bit)
-    total = after(total, ends[1])
-    others = [leave(at, total) for at in range(5, len(wanted))]
+    others = [
+        exchange(after(piece, total), "row", cut[0])
+        for cut, piece in zip(wanted[2:-1], pieces[2:-1])
+    ]
     total = total + exchange(total, "row", bits("row")[-1])
-    ends += [leave(3, total), pieces[4], *others]
-    total = gather_plane(after(total, ends[2]))
+    total = gather_plane(after(total, outer))
+    ends = [inner + outer, first, *others, pieces[-1]]
 
     returned = jnp.zeros_like(three_index)
     for (part, first, _), piece in zip(wanted, ends):

time: 172 us -> 179 us (1.041)
  starting transfers between devices: 39.8 us -> 51.4 us
  waiting for transfers between devices: 78.3 us -> 73.4 us
    ppermute x0 -> x4, starting transfers between devices: none -> 9.78 us  [across(): lax.ppermute(value, 'row', [at for at in pairs if (abs(at[0] - at[1]) ==...]
    ppermute x30 -> x26, waiting for transfers between devices: 64 us -> 59.2 us  [exchange(): return lax.ppermute(value, axis, [(at, at ^ bit) for at in range(size)])]
    ppermute x30 -> x26, starting transfers between devices: 26.8 us -> 28.5 us  [exchange(): return lax.ppermute(value, axis, [(at, at ^ bit) for at in range(size)])]
  transfers between devices with their start and end apart: 34 -> 34, of which waited for: 16 -> 13; matrix products, arithmetic and copies ran while one was open for 6% -> 5% of each run, Pallas kernels for 8% -> 7%
where the time goes in v2:
time: 179 us
  waiting for transfers between devices  73.4 us (41%)
  starting transfers between devices  51.4 us (29%)
  Pallas kernels  27.4 us (15%)
  local copies, waits for them, and re-layouts  11.1 us (6%)
  between operations  8.95 us (5%)
  other arithmetic  6.63 us (4%)
    ppermute x26, waiting for transfers between devices, exchange(): return lax.ppermute(value, axis, [(at, at ^ bit) for at in range(size)])  59.2 us
    ppermute x26, starting transfers between devices, exchange(): return lax.ppermute(value, axis, [(at, at ^ bit) for at in range(size)])  28.5 us
    pallas_call x2, Pallas kernels, call(): pl.pallas_call(functools.partial(staged, kernel, len(small), len(big), le...  27.4 us
    ppermute x4, starting transfers between devices, on_device(): got = lax.ppermute(rows, 'col', links)  13.1 us
    ppermute x4, waiting for transfers between devices, on_device(): got = lax.ppermute(rows, 'col', links)  13.1 us
    ppermute x4, starting transfers between devices, across(): lax.ppermute(value, 'row', [at for at in pairs if (abs(at[0] - at[1]) ==...  9.78 us
  transfers between devices with their start and end apart: 34, of which 13 were waited for; matrix products, arithmetic and copies ran while one was open for 5% of the time, Pallas kernels for 7%

profile of v2, /device:TPU:0, one launch (start us, length us, event | category | flops | bytes accessed | tf_op | source)
XLA Modules:
  0.0 178.9 jit_solution(13205684734698127243)
XLA Ops:
  0.7 2.7 %dynamic-slice_bitcast_fusion = (f32[512,256]{1,0:T(8,128)}, f32[512,256]{1,0:T(8,128)S(1)}, f32[512,256]{1,0:T(8,128)S(1)}, f32[512,256]{1,0:T(8,128)}) fusion(f32[4,512,256]{2,1,0:T(8,128)} %param.5, s32[]{:T(128)S(6)} %select_n.170, s32[]{:T(128)S(6)} %select_n.168, s32[]{:T(128)S(6)} %select_n.162, s32[]{:T(128)S(6)} %select_n.169), kind=kLoop, calls=%fused_computation.9 | loop fusion | bytes 4194320 | tf_op jit(solution)/shard_map/jit(dynamic_index_in_dim)/squeeze | solution.py:309
  3.4 4.9 %collective-permute-start.3 = (f32[512,256]{1,0:T(8,128)S(1)}, f32[512,256]{1,0:T(8,128)S(1)}, u32[]{:S(2)}, u32[]{:S(2)}) collective-permute-start(f32[512,256]{1,0:T(8,128)S(1)} %get-tuple-element.60.refs_4_), channel_id=1, source_target_pairs={{0,4},{1,5},{2,6},{3,7},{8,12},{9,13},{10,14},{11,15},{16,20},{17,... | collective-permute-start | bytes 1572872 | tf_op jit(solution)/shard_map/ppermute | solution.py:326
  8.3 1.6 collective-permute-start
  9.9 0.7 collective-permute-start.1
  10.6 1.4 compare_reduce_fusion.1
  12.7 4.4 %collective-permute-start.2 = (f32[512,256]{1,0:T(8,128)}, f32[512,256]{1,0:T(8,128)}, u32[]{:S(2)}, u32[]{:S(2)}) collective-permute-start(f32[512,256]{1,0:T(8,128)} %get-tuple-element.28), channel_id=1, source_target_pairs={{0,24},{24,0},{1,25},{25,1},{2,26},{26,2},{3,27},{27,3},{4,28},{28... | collective-permute-start | bytes 1572872 | tf_op jit(solution)/shard_map/ppermute | solution.py:233
  17.1 0.1 stack.59
  17.3 0.1 copy.12
  17.4 0.6 gather_fusion
  18.0 0.6 gather_fusion.1
  18.7 0.7 fusion.2
  26.5 0.1 broadcast_in_dim.34
  26.6 0.8 slice.25.refs_3_
  27.5 0.7 slice.22.refs_3_
  28.2 0.6 pad_maximum_fusion.1.refs_0_
  28.8 0.6 pad_maximum_fusion.refs_0_
  29.4 2.1 %collective-permute-start.5 = (f32[512,256]{1,0:T(8,128)S(1)}, f32[512,256]{1,0:T(8,128)}, u32[]{:S(2)}, u32[]{:S(2)}) collective-permute-start(f32[512,256]{1,0:T(8,128)S(1)} %collective-permute-done.refs_5_), channel_id=1, source_target_pairs={{0,4},{1,5},{2,6},{3,7},{8,12},{9,13},{10,14},{11,15},{16,20},{17,... | collective-permute-start | bytes 1572872 | tf_op jit(solution)/shard_map/ppermute | solution.py:326
  31.6 1.6 collective-permute-start.12
  33.2 0.8 collective-permute-start.4
  34.0 1.2 collective-permute-done.2
  35.2 1.1 add.169.refs_6_
  36.3 5.0 %collective-permute-done.5 = f32[512,256]{1,0:T(8,128)} collective-permute-done((f32[512,256]{1,0:T(8,128)S(1)}, f32[512,256]{1,0:T(8,128)}, u32[]{:S(2)}, u32[]{:S(2)}) %collective-permute-start.5) | collective-permute-done | bytes 524320 | tf_op jit(solution)/shard_map/ppermute | solution.py:326
  41.3 4.5 %collective-permute-start.6 = (f32[512,256]{1,0:T(8,128)S(1)}, f32[512,256]{1,0:T(8,128)S(1)}, u32[]{:S(2)}, u32[]{:S(2)}) collective-permute-start(f32[512,256]{1,0:T(8,128)S(1)} %add.169.refs_6_), channel_id=1, source_target_pairs={{0,4},{1,5},{2,6},{3,7},{8,12},{9,13},{10,14},{11,15},{16,20},{17,... | collective-permute-start | bytes 1572872 | tf_op jit(solution)/shard_map/ppermute | solution.py:326
  46.0 1.6 collective-permute-start.13
  47.6 12.1 %collective-permute-done.4.refs_7_ = f32[512,256]{1,0:T(8,128)S(1)} collective-permute-done((f32[512,256]{1,0:T(8,128)}, f32[512,256]{1,0:T(8,128)S(1)}, u32[]{:S(2)}, u32[]{:S(2)}) %collective-permute-start.4) | collective-permute-done | bytes 524320 | tf_op jit(solution)/shard_map/ppermute | solution.py:223
  59.7 1.6 collective-permute-start.7
  61.4 1.6 collective-permute-start.14
  62.9 0.5 collective-permute-start.9
  63.4 8.1 %collective-permute-done.7 = f32[512,256]{1,0:T(8,128)S(1)} collective-permute-done((f32[512,256]{1,0:T(8,128)S(1)}, f32[512,256]{1,0:T(8,128)S(1)}, u32[]{:S(2)}, u32[]{:S(2)}) %collective-permute-start.7) | collective-permute-done | bytes 524320 | tf_op jit(solution)/shard_map/ppermute | solution.py:326
  71.7 2.3 %collective-permute-done.14.refs_8_ = f32[512,256]{1,0:T(8,128)S(1)} collective-permute-done((f32[512,256]{1,0:T(8,128)S(1)}, f32[512,256]{1,0:T(8,128)S(1)}, u32[]{:S(2)}, u32[]{:S(2)}) %collective-permute-start.14) | collective-permute-done | bytes 524320 | tf_op jit(solution)/shard_map/ppermute | solution.py:223
  73.9 0.8 copy-done.11
  74.8 1.5 collective-permute-start.15
  76.2 0.9 copy.19.refs_1_
  77.1 0.5 collective-permute-start.17
  77.7 13.4 %early.1 = (bf16[512,1024]{1,0:T(8,128)(2,1)}, bf16[512,1024]{1,0:T(8,128)(2,1)}, f32[512,512]{1,0:T(8,128)}, f32[512,256]{1,0:T(8,128)}, f32[512,256]{1,0:T(8,1...) custom-call(f32[4]{0:T(128)} %pad_maximum_fusion.1.refs_0_, f32[512,1]{1,0:T(8,128)} %copy.19.refs_1_, f32[1,512]{1,0:T(1,128)} %bitcast.43, ...), custom_call_target="tpu_custom_call" | custom-call | tf_op jit(solution)/shard_map/early/pallas_call | solution.py:41
  91.1 0.5 collective-permute-start.19
  91.7 1.7 collective-permute-done.19.refs_13_
  93.4 0.8 copy-done.13
  94.2 14.0 %late.1 = (f32[512,512]{1,0:T(8,128)}, f32[512,256]{1,0:T(8,128)}, f32[512,256]{1,0:T(8,128)}, f32[512,256]{1,0:T(8,128)}, f32[512,256]{1,0:T(8,128)}) custom-call(f32[4]{0:T(128)} %pad_maximum_fusion.refs_0_, f32[512,1]{1,0:T(8,128)} %copy.19.refs_1_, f32[1,512]{1,0:T(1,128)} %bitcast.44, f32[2,8,1024]{2,1,0:T(8,128)} %slice.22.refs_3_, ...), custom_call_target="tpu_custom_call" | custom-call | tf_op jit(solution)/shard_map/late/pallas_call | solution.py:41
  108.2 1.2 constant_dynamic-slice_fusion.3
  109.4 0.4 collective-permute-start.21
  109.8 1.5 collective-permute-done.21
  111.4 1.1 dynamic-slice_add_fusion
  112.5 0.6 collective-permute-start.22
  113.2 0.3 collective-permute-start.23
  113.5 2.6 %collective-permute-start.24 = (f32[64,512]{1,0:T(8,128)S(1)}, f32[64,512]{1,0:T(8,128)S(1)}, u32[]{:S(2)}, u32[]{:S(2)}) collective-permute-start(f32[64,512]{1,0:T(8,128)S(1)} %get-tuple-element.63), channel_id=1, source_target_pairs={{0,6},{1,7},{2,4},{3,5},{4,2},{5,3},{6,0},{7,1},{8,14},{9,15},{10,... | collective-permute-start | bytes 393224 | tf_op jit(solution)/shard_map/ppermute | solution.py:223
  116.1 0.7 collective-permute-start.20
  116.8 5.2 %collective-permute-start.26 = (f32[512,256]{1,0:T(8,128)}, f32[512,256]{1,0:T(8,128)S(1)}, u32[]{:S(2)}, u32[]{:S(2)}) collective-permute-start(f32[512,256]{1,0:T(8,128)} %get-tuple-element.48), channel_id=1, source_target_pairs={{0,8},{8,0},{16,24},{24,16},{1,9},{9,1},{17,25},{25,17},{2,10},{10... | collective-permute-start | bytes 1572872 | tf_op jit(solution)/shard_map/ppermute | solution.py:223
  122.1 4.0 %collective-permute-start.25 = (f32[512,256]{1,0:T(8,128)S(1)}, f32[512,256]{1,0:T(8,128)S(1)}, u32[]{:S(2)}, u32[]{:S(2)}) collective-permute-start(f32[512,256]{1,0:T(8,128)S(1)} %copy-done.19), channel_id=1, source_target_pairs={{0,24},{24,0},{1,25},{25,1},{2,26},{26,2},{3,27},{27,3},{4,28},{28... | collective-permute-start | bytes 1572872 | tf_op jit(solution)/shard_map/ppermute | solution.py:233
  126.2 8.6 %collective-permute-done.26 = f32[512,256]{1,0:T(8,128)S(1)} collective-permute-done((f32[512,256]{1,0:T(8,128)}, f32[512,256]{1,0:T(8,128)S(1)}, u32[]{:S(2)}, u32[]{:S(2)}) %collective-permute-start.26) | collective-permute-done | bytes 524320 | tf_op jit(solution)/shard_map/ppermute | solution.py:223
  134.7 2.4 %collective-permute-start.27 = (f32[64,512]{1,0:T(8,128)S(1)}, f32[64,512]{1,0:T(8,128)S(1)}, u32[]{:S(2)}, u32[]{:S(2)}) collective-permute-start(f32[64,512]{1,0:T(8,128)S(1)} %add_add_fusion), channel_id=1, source_target_pairs={{0,8},{8,0},{16,24},{24,16},{1,9},{9,1},{17,25},{25,17},{2,10},{10... | collective-permute-start | bytes 393224 | tf_op jit(solution)/shard_map/ppermute | solution.py:223
  137.1 11.1 %collective-permute-done.27 = f32[64,512]{1,0:T(8,128)S(1)} collective-permute-done((f32[64,512]{1,0:T(8,128)S(1)}, f32[64,512]{1,0:T(8,128)S(1)}, u32[]{:S(2)}, u32[]{:S(2)}) %collective-permute-start.27) | collective-permute-done | bytes 131104 | tf_op jit(solution)/shard_map/ppermute | solution.py:223
  148.3 1.8 %collective-permute-start.29 = (f32[64,512]{1,0:T(8,128)S(1)}, f32[64,512]{1,0:T(8,128)S(1)}, u32[]{:S(2)}, u32[]{:S(2)}) collective-permute-start(f32[64,512]{1,0:T(8,128)S(1)} %add.183), channel_id=1, source_target_pairs={{0,16},{8,24},{16,0},{24,8},{1,17},{9,25},{17,1},{25,9},{2,18},{10... | collective-permute-start | bytes 393224 | tf_op jit(solution)/shard_map/ppermute | solution.py:223
  150.1 1.1 collective-permute-start.28
  151.3 16.1 %collective-permute-done.29 = f32[64,512]{1,0:T(8,128)S(1)} collective-permute-done((f32[64,512]{1,0:T(8,128)S(1)}, f32[64,512]{1,0:T(8,128)S(1)}, u32[]{:S(2)}, u32[]{:S(2)}) %collective-permute-start.29) | collective-permute-done | bytes 131104 | tf_op jit(solution)/shard_map/ppermute | solution.py:223
  167.4 0.6 collective-permute-start.30
  168.0 0.3 collective-permute-start.31
  168.3 2.6 %collective-permute-start.32 = (f32[64,512]{1,0:T(8,128)S(1)}, f32[64,512]{1,0:T(8,128)S(1)}, u32[]{:S(2)}, u32[]{:S(2)}) collective-permute-start(f32[64,512]{1,0:T(8,128)S(1)} %add.186), channel_id=1, source_target_pairs={{0,6},{1,7},{2,4},{3,5},{4,2},{5,3},{6,0},{7,1},{8,14},{9,15},{10,... | collective-permute-start | bytes 393224 | tf_op jit(solution)/shard_map/ppermute | solution.py:223
  170.9 0.2 broadcast_in_dim.30
  171.2 1.2 collective-permute-done.30
  172.4 1.9 %collective-permute-done.31 = f32[64,512]{1,0:T(8,128)S(1)} collective-permute-done((f32[64,512]{1,0:T(8,128)S(1)}, f32[64,512]{1,0:T(8,128)S(1)}, u32[]{:S(2)}, u32[]{:S(2)}) %collective-permute-start.31) | collective-permute-done | bytes 131104 | tf_op jit(solution)/shard_map/ppermute | solution.py:223
  174.6 2.5 %collective-permute-done.28 = f32[512,256]{1,0:T(8,128)S(1)} collective-permute-done((f32[512,256]{1,0:T(8,128)S(1)}, f32[512,256]{1,0:T(8,128)S(1)}, u32[]{:S(2)}, u32[]{:S(2)}) %collective-permute-start.28) | collective-permute-done | bytes 524320 | tf_op jit(solution)/shard_map/ppermute | solution.py:223
  177.2 1.2 maximum_select_fusion
  178.4 0.4 copy-done.8
  (92 shorter events, 1.4 us)
Async XLA Ops:
  0.7 16.6 %copy-start.15 = (s32[32,8,16]{0,2,1:T(8,128)S(1)}, s32[32,8,16]{0,2,1:T(8,128)}, u32[]{:S(2)}) copy-start(s32[32,8,16]{0,2,1:T(8,128)} %param.8) | copy-start | bytes 49156
  0.7 18.0 %copy-start.17 = (f32[32]{0:T(128)S(1)}, f32[32]{0:T(128)}, u32[]{:S(2)}) copy-start(f32[32]{0:T(128)} %param.6) | copy-start | bytes 388
  3.4 32.9 %copy-start.1 = (f32[512,256]{1,0:T(8,128)}, f32[512,256]{1,0:T(8,128)S(1)}, u32[]{:S(2)}) copy-start(f32[512,256]{1,0:T(8,128)S(1)} %get-tuple-element.60.refs_4_) | copy-start | bytes 1572868
  3.4 26.1 %collective-permute-start.3 = (f32[512,256]{1,0:T(8,128)S(1)}, f32[512,256]{1,0:T(8,128)S(1)}, u32[]{:S(2)}, u32[]{:S(2)}) collective-permute-start(f32[512,256]{1,0:T(8,128)S(1)} %get-tuple-element.60.refs_4_), channel_id=1, source_target_pairs={{0,4},{1,5},{2,6},{3,7},{8,12},{9,13},{10,14},{11,15},{16,20},{17,... | collective-permute-start | bytes 1572872 | tf_op jit(solution)/shard_map/ppermute | solution.py:326
  8.3 21.2 %collective-permute-start = (f32[512,256]{1,0:T(8,128)S(1)}, f32[512,256]{1,0:T(8,128)S(1)}, u32[]{:S(2)}, u32[]{:S(2)}) collective-permute-start(f32[512,256]{1,0:T(8,128)S(1)} %get-tuple-element.59), channel_id=1, source_target_pairs={{0,8},{8,0},{16,24},{24,16},{1,9},{9,1},{17,25},{25,17},{2,10},{10... | collective-permute-start | bytes 1572872 | tf_op jit(solution)/shard_map/ppermute | solution.py:223
  9.9 25.3 %collective-permute-start.1 = (f32[512,256]{1,0:T(8,128)}, f32[512,256]{1,0:T(8,128)S(1)}, u32[]{:S(2)}, u32[]{:S(2)}) collective-permute-start(f32[512,256]{1,0:T(8,128)} %get-tuple-element.28), channel_id=1, source_target_pairs={{8,16},{16,8},{9,17},{17,9},{10,18},{18,10},{11,19},{19,11},{12,20... | collective-permute-start | bytes 1572872 | tf_op jit(solution)/shard_map/ppermute | solution.py:233
  12.7 22.5 %collective-permute-start.2 = (f32[512,256]{1,0:T(8,128)}, f32[512,256]{1,0:T(8,128)}, u32[]{:S(2)}, u32[]{:S(2)}) collective-permute-start(f32[512,256]{1,0:T(8,128)} %get-tuple-element.28), channel_id=1, source_target_pairs={{0,24},{24,0},{1,25},{25,1},{2,26},{26,2},{3,27},{27,3},{4,28},{28... | collective-permute-start | bytes 1572872 | tf_op jit(solution)/shard_map/ppermute | solution.py:233
  29.4 16.5 %copy-start.2 = (f32[512,256]{1,0:T(8,128)}, f32[512,256]{1,0:T(8,128)S(1)}, u32[]{:S(2)}) copy-start(f32[512,256]{1,0:T(8,128)S(1)} %collective-permute-done.refs_5_) | copy-start | bytes 1572868
  29.4 11.9 %collective-permute-start.5 = (f32[512,256]{1,0:T(8,128)S(1)}, f32[512,256]{1,0:T(8,128)}, u32[]{:S(2)}, u32[]{:S(2)}) collective-permute-start(f32[512,256]{1,0:T(8,128)S(1)} %collective-permute-done.refs_5_), channel_id=1, source_target_pairs={{0,4},{1,5},{2,6},{3,7},{8,12},{9,13},{10,14},{11,15},{16,20},{17,... | collective-permute-start | bytes 1572872 | tf_op jit(solution)/shard_map/ppermute | solution.py:326
  31.6 31.3 %copy-start.3 = (f32[512,256]{1,0:T(8,128)}, f32[512,256]{1,0:T(8,128)S(1)}, u32[]{:S(2)}) copy-start(f32[512,256]{1,0:T(8,128)S(1)} %broadcast_select_fusion.3.refs_8_) | copy-start | bytes 1572868
  31.6 14.3 %collective-permute-start.12 = (f32[512,256]{1,0:T(8,128)S(1)}, f32[512,256]{1,0:T(8,128)S(1)}, u32[]{:S(2)}, u32[]{:S(2)}) collective-permute-start(f32[512,256]{1,0:T(8,128)S(1)} %broadcast_select_fusion.3.refs_8_), channel_id=1, source_target_pairs={{0,2},{1,3},{2,0},{3,1},{4,6},{5,7},{6,4},{7,5},{8,10},{9,11},{10,... | collective-permute-start | bytes 1572872 | tf_op jit(solution)/shard_map/ppermute | solution.py:223
  33.2 26.5 %collective-permute-start.4 = (f32[512,256]{1,0:T(8,128)}, f32[512,256]{1,0:T(8,128)S(1)}, u32[]{:S(2)}, u32[]{:S(2)}) collective-permute-start(f32[512,256]{1,0:T(8,128)} %get-tuple-element.29), channel_id=1, source_target_pairs={{0,16},{8,24},{16,0},{24,8},{1,17},{9,25},{17,1},{25,9},{2,18},{10... | collective-permute-start | bytes 1572872 | tf_op jit(solution)/shard_map/ppermute | solution.py:223
  36.3 35.3 %copy-start = (f32[512,256]{1,0:T(8,128)}, f32[512,256]{1,0:T(8,128)S(1)}, u32[]{:S(2)}) copy-start(f32[512,256]{1,0:T(8,128)S(1)} %add.169.refs_6_) | copy-start | bytes 1572868
  36.3 39.9 %copy-start.16 = (f32[512]{0:T(512)S(1)}, f32[512]{0:T(512)}, u32[]{:S(2)}) copy-start(f32[512]{0:T(512)} %param.7) | copy-start | bytes 6148
  41.3 18.3 %collective-permute-start.6 = (f32[512,256]{1,0:T(8,128)S(1)}, f32[512,256]{1,0:T(8,128)S(1)}, u32[]{:S(2)}, u32[]{:S(2)}) collective-permute-start(f32[512,256]{1,0:T(8,128)S(1)} %add.169.refs_6_), channel_id=1, source_target_pairs={{0,4},{1,5},{2,6},{3,7},{8,12},{9,13},{10,14},{11,15},{16,20},{17,... | collective-permute-start | bytes 1572872 | tf_op jit(solution)/shard_map/ppermute | solution.py:326
  46.0 31.7 %copy-start.5 = (f32[512,256]{1,0:T(8,128)}, f32[512,256]{1,0:T(8,128)S(1)}, u32[]{:S(2)}) copy-start(f32[512,256]{1,0:T(8,128)S(1)} %broadcast_select_fusion.2.refs_9_) | copy-start | bytes 1572868
  46.0 45.1 %copy-start.9 = (f32[512,256]{1,0:T(8,128)}, f32[512,256]{1,0:T(8,128)S(1)}, u32[]{:S(2)}) copy-start(f32[512,256]{1,0:T(8,128)S(1)} %collective-permute-done.12.refs_6_) | copy-start | bytes 1572868
  46.0 15.3 %collective-permute-start.13 = (f32[512,256]{1,0:T(8,128)S(1)}, f32[512,256]{1,0:T(8,128)S(1)}, u32[]{:S(2)}, u32[]{:S(2)}) collective-permute-start(f32[512,256]{1,0:T(8,128)S(1)} %broadcast_select_fusion.2.refs_9_), channel_id=1, source_target_pairs={{0,2},{1,3},{2,0},{3,1},{4,6},{5,7},{6,4},{7,5},{8,10},{9,11},{10,... | collective-permute-start | bytes 1572872 | tf_op jit(solution)/shard_map/ppermute | solution.py:223
  59.7 18.0 %copy-start.4 = (f32[512,256]{1,0:T(8,128)}, f32[512,256]{1,0:T(8,128)S(1)}, u32[]{:S(2)}) copy-start(f32[512,256]{1,0:T(8,128)S(1)} %collective-permute-done.4.refs_7_) | copy-start | bytes 1572868
  59.7 11.8 %collective-permute-start.7 = (f32[512,256]{1,0:T(8,128)S(1)}, f32[512,256]{1,0:T(8,128)S(1)}, u32[]{:S(2)}, u32[]{:S(2)}) collective-permute-start(f32[512,256]{1,0:T(8,128)S(1)} %collective-permute-done.4.refs_7_), channel_id=1, source_target_pairs={{0,4},{1,5},{2,6},{3,7},{8,12},{9,13},{10,14},{11,15},{16,20},{17,... | collective-permute-start | bytes 1572872 | tf_op jit(solution)/shard_map/ppermute | solution.py:326
  61.3 16.4 %copy-start.6 = (f32[512,256]{1,0:T(8,128)}, f32[512,256]{1,0:T(8,128)S(1)}, u32[]{:S(2)}) copy-start(f32[512,256]{1,0:T(8,128)S(1)} %broadcast_select_fusion.1.refs_10_) | copy-start | bytes 1572868
  61.3 2.1 %copy-start.10 = (f32[512,256]{1,0:T(8,128)}, f32[512,256]{1,0:T(8,128)S(1)}, u32[]{:S(2)}) copy-start(f32[512,256]{1,0:T(8,128)S(1)} %collective-permute-done.13.refs_7_) | copy-start | bytes 1572868
  61.4 12.6 %collective-permute-start.14 = (f32[512,256]{1,0:T(8,128)S(1)}, f32[512,256]{1,0:T(8,128)S(1)}, u32[]{:S(2)}, u32[]{:S(2)}) collective-permute-start(f32[512,256]{1,0:T(8,128)S(1)} %broadcast_select_fusion.1.refs_10_), channel_id=1, source_target_pairs={{0,2},{1,3},{2,0},{3,1},{4,6},{5,7},{6,4},{7,5},{8,10},{9,11},{10,... | collective-permute-start | bytes 1572872 | tf_op jit(solution)/shard_map/ppermute | solution.py:223
  62.9 14.2 %collective-permute-start.8 = (f32[512,256]{1,0:T(8,128)S(1)}, f32[512,256]{1,0:T(8,128)}, u32[]{:S(2)}, u32[]{:S(2)}) collective-permute-start(f32[512,256]{1,0:T(8,128)S(1)} %broadcast_select_fusion.3.refs_8_), channel_id=1, source_target_pairs={{0,1},{1,0},{2,3},{3,2},{4,5},{5,4},{6,7},{7,6},{8,9},{9,8},{10,11... | collective-permute-start | bytes 1572872 | tf_op jit(solution)/shard_map/ppermute | solution.py:223
  62.9 14.2 %collective-permute-start.9 = (f32[512,256]{1,0:T(8,128)S(1)}, f32[512,256]{1,0:T(8,128)}, u32[]{:S(2)}, u32[]{:S(2)}) collective-permute-start(f32[512,256]{1,0:T(8,128)S(1)} %broadcast_select_fusion.2.refs_9_), channel_id=1, source_target_pairs={{0,1},{1,0},{2,3},{3,2},{4,5},{5,4},{6,7},{7,6},{8,9},{9,8},{10,11... | collective-permute-start | bytes 1572872 | tf_op jit(solution)/shard_map/ppermute | solution.py:223
  63.4 14.2 %collective-permute-start.10 = (f32[512,256]{1,0:T(8,128)S(1)}, f32[512,256]{1,0:T(8,128)}, u32[]{:S(2)}, u32[]{:S(2)}) collective-permute-start(f32[512,256]{1,0:T(8,128)S(1)} %broadcast_select_fusion.1.refs_10_), channel_id=1, source_target_pairs={{0,1},{1,0},{2,3},{3,2},{4,5},{5,4},{6,7},{7,6},{8,9},{9,8},{10,11... | collective-permute-start | bytes 1572872 | tf_op jit(solution)/shard_map/ppermute | solution.py:223
  71.6 6.1 %copy-start.7 = (f32[512,256]{1,0:T(8,128)}, f32[512,256]{1,0:T(8,128)S(1)}, u32[]{:S(2)}) copy-start(f32[512,256]{1,0:T(8,128)S(1)} %broadcast_select_fusion.refs_11_) | copy-start | bytes 1572868
  71.6 6.1 %collective-permute-start.11 = (f32[512,256]{1,0:T(8,128)S(1)}, f32[512,256]{1,0:T(8,128)}, u32[]{:S(2)}, u32[]{:S(2)}) collective-permute-start(f32[512,256]{1,0:T(8,128)S(1)} %broadcast_select_fusion.refs_11_), channel_id=1, source_target_pairs={{0,1},{1,0},{2,3},{3,2},{4,5},{5,4},{6,7},{7,6},{8,9},{9,8},{10,11... | collective-permute-start | bytes 1572872 | tf_op jit(solution)/shard_map/ppermute | solution.py:223
  73.9 0.8 copy-start.11
  74.8 16.4 %collective-permute-start.15 = (f32[512,256]{1,0:T(8,128)S(1)}, f32[512,256]{1,0:T(8,128)}, u32[]{:S(2)}, u32[]{:S(2)}) collective-permute-start(f32[512,256]{1,0:T(8,128)S(1)} %broadcast_select_fusion.refs_11_), channel_id=1, source_target_pairs={{0,2},{1,3},{2,0},{3,1},{4,6},{5,7},{6,4},{7,5},{8,10},{9,11},{10,... | collective-permute-start | bytes 1572872 | tf_op jit(solution)/shard_map/ppermute | solution.py:223
  77.1 14.5 %collective-permute-start.16 = (f32[512,256]{1,0:T(8,128)S(1)}, f32[512,256]{1,0:T(8,128)S(1)}, u32[]{:S(2)}, u32[]{:S(2)}) collective-permute-start(f32[512,256]{1,0:T(8,128)S(1)} %collective-permute-done.12.refs_6_), channel_id=1, source_target_pairs={{0,1},{1,0},{2,3},{3,2},{4,5},{5,4},{6,7},{7,6},{8,9},{9,8},{10,11... | collective-permute-start | bytes 1572872 | tf_op jit(solution)/shard_map/ppermute | solution.py:223
  77.1 14.5 %collective-permute-start.17 = (f32[512,256]{1,0:T(8,128)}, f32[512,256]{1,0:T(8,128)}, u32[]{:S(2)}, u32[]{:S(2)}) collective-permute-start(f32[512,256]{1,0:T(8,128)} %copy-done.10), channel_id=1, source_target_pairs={{0,1},{1,0},{2,3},{3,2},{4,5},{5,4},{6,7},{7,6},{8,9},{9,8},{10,11... | collective-permute-start | bytes 1572872 | tf_op jit(solution)/shard_map/ppermute | solution.py:223
  77.6 14.0 %collective-permute-start.18 = (f32[512,256]{1,0:T(8,128)}, f32[512,256]{1,0:T(8,128)}, u32[]{:S(2)}, u32[]{:S(2)}) collective-permute-start(f32[512,256]{1,0:T(8,128)} %copy-done.11), channel_id=1, source_target_pairs={{0,1},{1,0},{2,3},{3,2},{4,5},{5,4},{6,7},{7,6},{8,9},{9,8},{10,11... | collective-permute-start | bytes 1572872 | tf_op jit(solution)/shard_map/ppermute | solution.py:223
  91.1 2.3 %collective-permute-start.19 = (f32[512,256]{1,0:T(8,128)}, f32[512,256]{1,0:T(8,128)S(1)}, u32[]{:S(2)}, u32[]{:S(2)}) collective-permute-start(f32[512,256]{1,0:T(8,128)} %collective-permute-done.15.refs_9_), channel_id=1, source_target_pairs={{0,1},{1,0},{2,3},{3,2},{4,5},{5,4},{6,7},{7,6},{8,9},{9,8},{10,11... | collective-permute-start | bytes 1572872 | tf_op jit(solution)/shard_map/ppermute | solution.py:223
  91.6 1.7 copy-start.12
  93.4 0.8 copy-start.13
  108.2 7.9 %copy-start.19 = (f32[512,256]{1,0:T(8,128)S(1)}, f32[512,256]{1,0:T(8,128)}, u32[]{:S(2)}) copy-start(f32[512,256]{1,0:T(8,128)} %get-tuple-element.47) | copy-start | bytes 1572868
  108.2 41.9 %copy-start.18 = (f32[512,256]{1,0:T(8,128)S(1)}, f32[512,256]{1,0:T(8,128)}, u32[]{:S(2)}) copy-start(f32[512,256]{1,0:T(8,128)} %get-tuple-element.51) | copy-start | bytes 1572868
  109.4 2.0 %collective-permute-start.21 = (f32[256,512]{1,0:T(8,128)S(1)}, f32[256,512]{1,0:T(8,128)S(1)}, u32[]{:S(2)}, u32[]{:S(2)}) collective-permute-start(f32[256,512]{1,0:T(8,128)S(1)} %constant_dynamic-slice_fusion.3), channel_id=1, source_target_pairs={{0,1},{1,0},{2,3},{3,2},{4,5},{5,4},{6,7},{7,6},{8,9},{9,8},{10,11... | collective-permute-start | bytes 1572872 | tf_op jit(solution)/shard_map/ppermute | solution.py:223
  112.5 9.5 %collective-permute-start.22 = (f32[64,512]{1,0:T(8,128)S(1)}, f32[64,512]{1,0:T(8,128)S(1)}, u32[]{:S(2)}, u32[]{:S(2)}) collective-permute-start(f32[64,512]{1,0:T(8,128)S(1)} %get-tuple-element.62), channel_id=1, source_target_pairs={{0,2},{1,3},{2,0},{3,1},{4,6},{5,7},{6,4},{7,5},{8,10},{9,11},{10,... | collective-permute-start | bytes 393224 | tf_op jit(solution)/shard_map/ppermute | solution.py:223
  113.2 8.9 %collective-permute-start.23 = (f32[64,512]{1,0:T(8,128)S(1)}, f32[64,512]{1,0:T(8,128)S(1)}, u32[]{:S(2)}, u32[]{:S(2)}) collective-permute-start(f32[64,512]{1,0:T(8,128)S(1)} %get-tuple-element.64), channel_id=1, source_target_pairs={{0,4},{1,5},{2,6},{3,7},{4,0},{5,1},{6,2},{7,3},{8,12},{9,13},{10,... | collective-permute-start | bytes 393224 | tf_op jit(solution)/shard_map/ppermute | solution.py:223
  113.5 8.5 %collective-permute-start.24 = (f32[64,512]{1,0:T(8,128)S(1)}, f32[64,512]{1,0:T(8,128)S(1)}, u32[]{:S(2)}, u32[]{:S(2)}) collective-permute-start(f32[64,512]{1,0:T(8,128)S(1)} %get-tuple-element.63), channel_id=1, source_target_pairs={{0,6},{1,7},{2,4},{3,5},{4,2},{5,3},{6,0},{7,1},{8,14},{9,15},{10,... | collective-permute-start | bytes 393224 | tf_op jit(solution)/shard_map/ppermute | solution.py:223
  116.1 10.0 %collective-permute-start.20 = (f32[512,256]{1,0:T(8,128)S(1)}, f32[512,256]{1,0:T(8,128)S(1)}, u32[]{:S(2)}, u32[]{:S(2)}) collective-permute-start(f32[512,256]{1,0:T(8,128)S(1)} %copy-done.19), channel_id=1, source_target_pairs={{8,16},{16,8},{9,17},{17,9},{10,18},{18,10},{11,19},{19,11},{12,20... | collective-permute-start | bytes 1572872 | tf_op jit(solution)/shard_map/ppermute | solution.py:233
  116.8 17.9 %collective-permute-start.26 = (f32[512,256]{1,0:T(8,128)}, f32[512,256]{1,0:T(8,128)S(1)}, u32[]{:S(2)}, u32[]{:S(2)}) collective-permute-start(f32[512,256]{1,0:T(8,128)} %get-tuple-element.48), channel_id=1, source_target_pairs={{0,8},{8,0},{16,24},{24,16},{1,9},{9,1},{17,25},{25,17},{2,10},{10... | collective-permute-start | bytes 1572872 | tf_op jit(solution)/shard_map/ppermute | solution.py:223
  122.1 45.3 %collective-permute-start.25 = (f32[512,256]{1,0:T(8,128)S(1)}, f32[512,256]{1,0:T(8,128)S(1)}, u32[]{:S(2)}, u32[]{:S(2)}) collective-permute-start(f32[512,256]{1,0:T(8,128)S(1)} %copy-done.19), channel_id=1, source_target_pairs={{0,24},{24,0},{1,25},{25,1},{2,26},{26,2},{3,27},{27,3},{4,28},{28... | collective-permute-start | bytes 1572872 | tf_op jit(solution)/shard_map/ppermute | solution.py:233
  134.7 13.5 %collective-permute-start.27 = (f32[64,512]{1,0:T(8,128)S(1)}, f32[64,512]{1,0:T(8,128)S(1)}, u32[]{:S(2)}, u32[]{:S(2)}) collective-permute-start(f32[64,512]{1,0:T(8,128)S(1)} %add_add_fusion), channel_id=1, source_target_pairs={{0,8},{8,0},{16,24},{24,16},{1,9},{9,1},{17,25},{25,17},{2,10},{10... | collective-permute-start | bytes 393224 | tf_op jit(solution)/shard_map/ppermute | solution.py:223
  148.3 19.1 %collective-permute-start.29 = (f32[64,512]{1,0:T(8,128)S(1)}, f32[64,512]{1,0:T(8,128)S(1)}, u32[]{:S(2)}, u32[]{:S(2)}) collective-permute-start(f32[64,512]{1,0:T(8,128)S(1)} %add.183), channel_id=1, source_target_pairs={{0,16},{8,24},{16,0},{24,8},{1,17},{9,25},{17,1},{25,9},{2,18},{10... | collective-permute-start | bytes 393224 | tf_op jit(solution)/shard_map/ppermute | solution.py:223
  150.1 27.0 %collective-permute-start.28 = (f32[512,256]{1,0:T(8,128)S(1)}, f32[512,256]{1,0:T(8,128)S(1)}, u32[]{:S(2)}, u32[]{:S(2)}) collective-permute-start(f32[512,256]{1,0:T(8,128)S(1)} %copy-done.18), channel_id=1, source_target_pairs={{0,16},{8,24},{16,0},{24,8},{1,17},{9,25},{17,1},{25,9},{2,18},{10... | collective-permute-start | bytes 1572872 | tf_op jit(solution)/shard_map/ppermute | solution.py:223
  167.4 5.0 %collective-permute-start.30 = (f32[64,512]{1,0:T(8,128)S(1)}, f32[64,512]{1,0:T(8,128)S(1)}, u32[]{:S(2)}, u32[]{:S(2)}) collective-permute-start(f32[64,512]{1,0:T(8,128)S(1)} %add.186), channel_id=1, source_target_pairs={{0,2},{1,3},{2,0},{3,1},{4,6},{5,7},{6,4},{7,5},{8,10},{9,11},{10,... | collective-permute-start | bytes 393224 | tf_op jit(solution)/shard_map/ppermute | solution.py:223
  168.0 6.4 %collective-permute-start.31 = (f32[64,512]{1,0:T(8,128)S(1)}, f32[64,512]{1,0:T(8,128)S(1)}, u32[]{:S(2)}, u32[]{:S(2)}) collective-permute-start(f32[64,512]{1,0:T(8,128)S(1)} %add.186), channel_id=1, source_target_pairs={{0,4},{1,5},{2,6},{3,7},{4,0},{5,1},{6,2},{7,3},{8,12},{9,13},{10,... | collective-permute-start | bytes 393224 | tf_op jit(solution)/shard_map/ppermute | solution.py:223
  168.3 6.1 %collective-permute-start.32 = (f32[64,512]{1,0:T(8,128)S(1)}, f32[64,512]{1,0:T(8,128)S(1)}, u32[]{:S(2)}, u32[]{:S(2)}) collective-permute-start(f32[64,512]{1,0:T(8,128)S(1)} %add.186), channel_id=1, source_target_pairs={{0,6},{1,7},{2,4},{3,5},{4,2},{5,3},{6,0},{7,1},{8,14},{9,15},{10,... | collective-permute-start | bytes 393224 | tf_op jit(solution)/shard_map/ppermute | solution.py:223
  171.2 6.0 %copy-start.14 = (f32[512,256]{1,0:T(8,128)S(1)}, f32[512,256]{1,0:T(8,128)}, u32[]{:S(2)}) copy-start(f32[512,256]{1,0:T(8,128)} %get-tuple-element.52) | copy-start | bytes 1572868
  174.4 2.8 %collective-permute-start.33 = (f32[256,512]{1,0:T(8,128)S(1)}, f32[256,512]{1,0:T(8,128)S(1)}, u32[]{:S(2)}, u32[]{:S(2)}) collective-permute-start(f32[256,512]{1,0:T(8,128)S(1)} %maximum_select_fusion.1), channel_id=1, source_target_pairs={{0,1},{1,0},{2,3},{3,2},{4,5},{5,4},{6,7},{7,6},{8,9},{9,8},{10,11... | collective-permute-start | bytes 1572872 | tf_op jit(solution)/shard_map/ppermute | solution.py:223
  177.2 1.7 copy-start.8

commit v3 on v1

--- a/solution.py
+++ b/solution.py
@@ -160,7 +160,7 @@
     outs = [shape(nvir, naux, kind=jnp.bfloat16)] * 2 + [shape(nvir, nvir)]
     outs += [shape(nvir, width)] * parts
     wide, square = squares(nvir, naux)
-    small = [scalars, virtual[:, None], virtual[None, :], masks]
+    small = [scalars, *virtual, masks]
     kernel = functools.partial(early_kernel, cuts)
     scratch = [*wide, pltpu.VMEM((nvir, nvir), jnp.float32), *square]
     outs = call(kernel, "early", outs, small, [*own, *near, *twin], scratch)
@@ -210,7 +210,7 @@
     width = slices[0].shape[1]
     outs = [shape(nvir, nvir)] + [shape(height, width) for _, _, height in wanted]
     wide, square = squares(nvir, naux)
-    small = [scalars, virtual[:, None], virtual[None, :], masks]
+    small = [scalars, *virtual, masks]
     kernel = functools.partial(late_kernel, cuts, wanted, scale)
     scratch = [pltpu.VMEM((nvir, nvir), jnp.float32), *wide, *square, *wide, *square]
     big = [*own, *far, *twin, density, *slices]
@@ -295,6 +295,7 @@
         live = jnp.any(lists == panels[turn]).astype(jnp.float32)
         scalars += [occ_energy[own_orbital] + occ_energy[orbitals[1 + turn]], live]
     small = masks[:3], masks[3:], jnp.stack(scalars[:4]), jnp.stack(scalars[4:])
+    virtual = lax.optimization_barrier((vir_energy[:, None], vir_energy[None, :]))
 
     own, came, near, far = [], [], [], []
 
@@ -323,23 +324,22 @@
             reach *= 2
         came.append(got)
         near.append(rows)
-        sent = after(rows, far[-1]) if at else after(rows, *small)
+        sent = after(rows, far[-1]) if at else after(rows, *small, *virtual)
         far.append(exchange(sent, "col", 2))
 
     near_twin = [exchange(piece, "col", 1) for piece in near]
     halved, density, slices = early(
-        cuts, small[2], vir_energy, small[0], own, near, near_twin
+        cuts, small[2], virtual, small[0], own, near, near_twin
     )
     far_twin = [exchange(piece, "col", 1) for piece in far[:-1]]
     far_twin.append(exchange(after(far[-1], density), "col", 1))
 
     middle, edge, most = row_count // 2, row_count - 1, nvir // 4 * 3
-    wanted = [(middle, 0, most), (middle, most, nvir - most)]
-    wanted += [(edge, at, nvir // 2) for at in (0, nvir // 2)]
+    wanted = [(middle, 0, most), (middle, most, nvir - most), (edge, 0, nvir)]
     wanted += [(at, 0, nvir) for at in range(edge) if at != middle]
     scale = 1.0 / (row_count * col_count)
     total, pieces = late(
-        cuts, wanted, scale, small[3], vir_energy, small[1], halved, far, far_twin,
+        cuts, wanted, scale, small[3], virtual, small[1], halved, far, far_twin,
         density, slices,
     )
 
@@ -348,15 +348,15 @@
 
     ends = [leave(0)]
     total = scatter_plane(scatter_chip(total))
-    ends += [leave(1, total), leave(2, total)]
+    ends.append(leave(1, total))
     total = after(total, ends[0])
     for bit in bits("row")[:-1]:
         total = total + exchange(total, "row", bit)
     total = after(total, ends[1])
-    others = [leave(at, total) for at in range(5, len(wanted))]
+    ends += [leave(2, total), pieces[3]]
+    ends += [leave(at, total) for at in range(4, len(wanted))]
     total = total + exchange(total, "row", bits("row")[-1])
-    ends += [leave(3, total), pieces[4], *others]
-    total = gather_plane(after(total, ends[2]))
+    total = gather_plane(total)
 
     returned = jnp.zeros_like(three_index)
     for (part, first, _), piece in zip(wanted, ends):

time: 172 us -> 171 us (level)
    ppermute x30 -> x29, waiting for transfers between devices: 64 us -> 63 us  [exchange(): return lax.ppermute(value, axis, [(at, at ^ bit) for at in range(size)])]
    ppermute x30 -> x29, starting transfers between devices: 26.8 us -> 27.6 us  [exchange(): return lax.ppermute(value, axis, [(at, at ^ bit) for at in range(size)])]
  transfers between devices with their start and end apart: 34 -> 33, of which waited for: 16 -> 16; matrix products, arithmetic and copies ran while one was open for 6% -> 6% of each run, Pallas kernels for 8% -> 8%
where the time goes in v3:
time: 171 us; the launch traced here: 170 us
  waiting for transfers between devices  77.2 us (45%)
  starting transfers between devices  39.8 us (23%)
  Pallas kernels  27.9 us (16%)
  local copies, waits for them, and re-layouts  11.2 us (7%)
  between operations  8.6 us (5%)
  other arithmetic  5.43 us (3%)
    ppermute x29, waiting for transfers between devices, exchange(): return lax.ppermute(value, axis, [(at, at ^ bit) for at in range(size)])  63 us
    pallas_call x2, Pallas kernels, call(): pl.pallas_call(functools.partial(staged, kernel, len(small), len(big), le...  27.9 us
    ppermute x29, starting transfers between devices, exchange(): return lax.ppermute(value, axis, [(at, at ^ bit) for at in range(size)])  27.6 us
    ppermute x4, waiting for transfers between devices, on_device(): got = lax.ppermute(rows, 'col', links)  14.3 us
    ppermute x4, starting transfers between devices, on_device(): got = lax.ppermute(rows, 'col', links)  12.2 us
  transfers between devices with their start and end apart: 33, of which 16 were waited for; matrix products, arithmetic and copies ran while one was open for 6% of the time, Pallas kernels for 8%

profile of v3, /device:TPU:0, one launch (start us, length us, event | category | flops | bytes accessed | tf_op | source)
XLA Modules:
  0.0 170.1 jit_solution(1894791760025298052)
XLA Ops:
  0.7 2.7 %dynamic-slice_bitcast_fusion = (f32[512,256]{1,0:T(8,128)}, f32[512,256]{1,0:T(8,128)S(1)}, f32[512,256]{1,0:T(8,128)S(1)}, f32[512,256]{1,0:T(8,128)}) fusion(f32[4,512,256]{2,1,0:T(8,128)} %param.5, s32[]{:T(128)S(6)} %select_n.171, s32[]{:T(128)S(6)} %select_n.169, s32[]{:T(128)S(6)} %select_n.163, s32[]{:T(128)S(6)} %select_n.170), kind=kLoop, calls=%fused_computation.8 | loop fusion | bytes 4194320 | tf_op jit(solution)/shard_map/jit(dynamic_index_in_dim)/squeeze | solution.py:304
  3.4 4.9 %collective-permute-start.2 = (f32[512,256]{1,0:T(8,128)S(1)}, f32[512,256]{1,0:T(8,128)S(1)}, u32[]{:S(2)}, u32[]{:S(2)}) collective-permute-start(f32[512,256]{1,0:T(8,128)S(1)} %get-tuple-element.68.refs_4_), channel_id=1, source_target_pairs={{0,4},{1,5},{2,6},{3,7},{8,12},{9,13},{10,14},{11,15},{16,20},{17,... | collective-permute-start | bytes 1572872 | tf_op jit(solution)/shard_map/ppermute | solution.py:322
  8.3 1.6 collective-permute-start
  9.9 1.4 compare_reduce_fusion.1
  11.9 2.7 %collective-permute-start.1 = (f32[512,256]{1,0:T(8,128)}, f32[512,256]{1,0:T(8,128)S(1)}, u32[]{:S(2)}, u32[]{:S(2)}) collective-permute-start(f32[512,256]{1,0:T(8,128)} %get-tuple-element.34), channel_id=1, source_target_pairs={{0,16},{8,24},{16,0},{24,8},{1,17},{9,25},{17,1},{25,9},{2,18},{10... | collective-permute-start | bytes 1572872 | tf_op jit(solution)/shard_map/ppermute | solution.py:223
  14.6 0.1 stack.59
  14.7 0.1 copy.12
  14.8 0.6 gather_fusion
  15.4 0.1 copy.13
  15.5 0.6 gather_fusion.1
  16.1 0.7 fusion.2
  23.7 0.1 broadcast_in_dim.35
  23.8 0.8 slice.25.refs_3_
  24.6 0.1 broadcast_in_dim.34
  24.7 0.7 slice.22.refs_3_
  25.5 0.6 pad_maximum_fusion.1.refs_0_
  26.1 0.6 pad_maximum_fusion.refs_0_
  26.7 3.9 %collective-permute-done.refs_5_ = f32[512,256]{1,0:T(8,128)S(1)} collective-permute-done((f32[512,256]{1,0:T(8,128)S(1)}, f32[512,256]{1,0:T(8,128)S(1)}, u32[]{:S(2)}, u32[]{:S(2)}) %collective-permute-start) | collective-permute-done | bytes 524320 | tf_op jit(solution)/shard_map/ppermute | solution.py:223
  30.6 1.6 collective-permute-start.4
  32.2 1.6 collective-permute-start.11
  33.8 2.5 %collective-permute-start.3 = (f32[512,256]{1,0:T(8,128)}, f32[512,256]{1,0:T(8,128)S(1)}, u32[]{:S(2)}, u32[]{:S(2)}) collective-permute-start(f32[512,256]{1,0:T(8,128)} %get-tuple-element.35), channel_id=1, source_target_pairs={{0,24},{8,16},{16,8},{24,0},{1,25},{9,17},{17,9},{25,1},{2,26},{10... | collective-permute-start | bytes 1572872 | tf_op jit(solution)/shard_map/ppermute | solution.py:223
  36.3 14.1 %collective-permute-done.1.refs_6_ = f32[512,256]{1,0:T(8,128)S(1)} collective-permute-done((f32[512,256]{1,0:T(8,128)}, f32[512,256]{1,0:T(8,128)S(1)}, u32[]{:S(2)}, u32[]{:S(2)}) %collective-permute-start.1) | collective-permute-done | bytes 524320 | tf_op jit(solution)/shard_map/ppermute | solution.py:223
  50.4 1.3 collective-permute-start.5
  51.9 1.6 collective-permute-start.12
  53.4 8.4 %collective-permute-done.5 = f32[512,256]{1,0:T(8,128)S(1)} collective-permute-done((f32[512,256]{1,0:T(8,128)S(1)}, f32[512,256]{1,0:T(8,128)S(1)}, u32[]{:S(2)}, u32[]{:S(2)}) %collective-permute-start.5) | collective-permute-done | bytes 524320 | tf_op jit(solution)/shard_map/ppermute | solution.py:322
  61.9 4.4 %collective-permute-start.6 = (f32[512,256]{1,0:T(8,128)S(1)}, f32[512,256]{1,0:T(8,128)S(1)}, u32[]{:S(2)}, u32[]{:S(2)}) collective-permute-start(f32[512,256]{1,0:T(8,128)S(1)} %collective-permute-done.3.refs_7_), channel_id=1, source_target_pairs={{0,4},{1,5},{2,6},{3,7},{8,12},{9,13},{10,14},{11,15},{16,20},{17,... | collective-permute-start | bytes 1572872 | tf_op jit(solution)/shard_map/ppermute | solution.py:322
  66.6 0.5 collective-permute-start.8
  67.1 0.1 collective-permute-start.9
  67.1 5.8 %collective-permute-done.6 = f32[512,256]{1,0:T(8,128)S(1)} collective-permute-done((f32[512,256]{1,0:T(8,128)S(1)}, f32[512,256]{1,0:T(8,128)S(1)}, u32[]{:S(2)}, u32[]{:S(2)}) %collective-permute-start.6) | collective-permute-done | bytes 524320 | tf_op jit(solution)/shard_map/ppermute | solution.py:322
  73.1 2.5 %collective-permute-done.13.refs_8_ = f32[512,256]{1,0:T(8,128)S(1)} collective-permute-done((f32[512,256]{1,0:T(8,128)S(1)}, f32[512,256]{1,0:T(8,128)S(1)}, u32[]{:S(2)}, u32[]{:S(2)}) %collective-permute-start.13) | collective-permute-done | bytes 524320 | tf_op jit(solution)/shard_map/ppermute | solution.py:223
  75.7 0.8 copy-done.11
  76.5 0.6 collective-permute-start.14
  77.0 0.9 copy.19.refs_1_
  77.9 0.5 collective-permute-start.16
  78.5 13.4 %early.1 = (bf16[512,1024]{1,0:T(8,128)(2,1)}, bf16[512,1024]{1,0:T(8,128)(2,1)}, f32[512,512]{1,0:T(8,128)}, f32[512,256]{1,0:T(8,128)}, f32[512,256]{1,0:T(8,1...) custom-call(f32[4]{0:T(128)} %pad_maximum_fusion.1.refs_0_, f32[512,1]{1,0:T(8,128)} %copy.19.refs_1_, f32[1,512]{1,0:T(1,128)} %bitcast.45, ...), custom_call_target="tpu_custom_call" | custom-call | tf_op jit(solution)/shard_map/early/pallas_call | solution.py:41
  91.9 0.5 collective-permute-start.18
  92.5 1.5 collective-permute-done.18.refs_13_
  94.0 0.8 copy-done.14
  94.8 14.5 %late.1 = (f32[512,512]{1,0:T(8,128)}, f32[384,256]{1,0:T(8,128)}, f32[128,256]{1,0:T(8,128)}, f32[512,256]{1,0:T(8,128)}, f32[512,256]{1,0:T(8,128)}, /*index=5*/f32[512,256]{1,0:T(8,128)}) custom-call(f32[4]{0:T(128)} %pad_maximum_fusion.refs_0_, f32[512,1]{1,0:T(8,128)} %copy.19.refs_1_, f32[1,512]{1,0:T(1,128)} %bitcast.46, ...), custom_call_target="tpu_custom_call" | custom-call | tf_op jit(solution)/shard_map/late/pallas_call | solution.py:41
  109.4 1.1 constant_dynamic-slice_fusion.3
  110.5 0.4 collective-permute-start.20
  110.9 0.8 collective-permute-start.19
  111.7 0.7 collective-permute-done.20
  112.5 1.1 dynamic-slice_add_fusion
  113.7 1.5 collective-permute-start.21
  115.3 2.0 %collective-permute-start.23 = (f32[64,512]{1,0:T(8,128)S(1)}, f32[64,512]{1,0:T(8,128)S(1)}, u32[]{:S(2)}, u32[]{:S(2)}) collective-permute-start(f32[64,512]{1,0:T(8,128)S(1)} %get-tuple-element.71), channel_id=1, source_target_pairs={{0,6},{1,7},{2,4},{3,5},{4,2},{5,3},{6,0},{7,1},{8,14},{9,15},{10,... | collective-permute-start | bytes 393224 | tf_op jit(solution)/shard_map/ppermute | solution.py:223
  117.2 2.6 %collective-permute-done.21 = f32[64,512]{1,0:T(8,128)S(1)} collective-permute-done((f32[64,512]{1,0:T(8,128)S(1)}, f32[64,512]{1,0:T(8,128)S(1)}, u32[]{:S(2)}, u32[]{:S(2)}) %collective-permute-start.21) | collective-permute-done | bytes 131104 | tf_op jit(solution)/shard_map/ppermute | solution.py:223
  119.9 3.6 %collective-permute-done.22 = f32[64,512]{1,0:T(8,128)S(1)} collective-permute-done((f32[64,512]{1,0:T(8,128)S(1)}, f32[64,512]{1,0:T(8,128)S(1)}, u32[]{:S(2)}, u32[]{:S(2)}) %collective-permute-start.22) | collective-permute-done | bytes 131104 | tf_op jit(solution)/shard_map/ppermute | solution.py:223
  123.5 7.9 %collective-permute-done.19 = f32[384,256]{1,0:T(8,128)S(1)} collective-permute-done((f32[384,256]{1,0:T(8,128)}, f32[384,256]{1,0:T(8,128)S(1)}, u32[]{:S(2)}, u32[]{:S(2)}) %collective-permute-start.19) | collective-permute-done | bytes 393248 | tf_op jit(solution)/shard_map/ppermute | solution.py:223
  131.5 2.4 %collective-permute-start.24 = (f32[128,256]{1,0:T(8,128)S(1)}, f32[128,256]{1,0:T(8,128)S(1)}, u32[]{:S(2)}, u32[]{:S(2)}) collective-permute-start(f32[128,256]{1,0:T(8,128)S(1)} %copy-done.21), channel_id=1, source_target_pairs={{0,16},{8,24},{16,0},{24,8},{1,17},{9,25},{17,1},{25,9},{2,18},{10... | collective-permute-start | bytes 393224 | tf_op jit(solution)/shard_map/ppermute | solution.py:223
  133.9 5.1 %collective-permute-done.25 = f32[64,512]{1,0:T(8,128)S(1)} collective-permute-done((f32[64,512]{1,0:T(8,128)S(1)}, f32[64,512]{1,0:T(8,128)S(1)}, u32[]{:S(2)}, u32[]{:S(2)}) %collective-permute-start.25) | collective-permute-done | bytes 131104 | tf_op jit(solution)/shard_map/ppermute | solution.py:223
  139.0 1.7 collective-permute-done.24
  140.7 0.3 collective-permute-start.28
  141.0 0.2 broadcast_in_dim.31
  141.2 2.2 %collective-permute-start.27 = (f32[512,256]{1,0:T(8,128)S(1)}, f32[512,256]{1,0:T(8,128)S(1)}, u32[]{:S(2)}, u32[]{:S(2)}) collective-permute-start(f32[512,256]{1,0:T(8,128)S(1)} %copy-done.19), channel_id=1, source_target_pairs={{0,8},{8,0},{16,24},{24,16},{1,9},{9,1},{17,25},{25,17},{2,10},{10... | collective-permute-start | bytes 1572872 | tf_op jit(solution)/shard_map/ppermute | solution.py:223
  143.4 2.0 %collective-permute-start.26 = (f32[512,256]{1,0:T(8,128)S(1)}, f32[512,256]{1,0:T(8,128)S(1)}, u32[]{:S(2)}, u32[]{:S(2)}) collective-permute-start(f32[512,256]{1,0:T(8,128)S(1)} %copy-done.20), channel_id=1, source_target_pairs={{0,24},{8,16},{16,8},{24,0},{1,25},{9,17},{17,9},{25,1},{2,26},{10... | collective-permute-start | bytes 1572872 | tf_op jit(solution)/shard_map/ppermute | solution.py:223
  145.3 3.7 %collective-permute-done.28 = f32[64,512]{1,0:T(8,128)S(1)} collective-permute-done((f32[64,512]{1,0:T(8,128)S(1)}, f32[64,512]{1,0:T(8,128)S(1)}, u32[]{:S(2)}, u32[]{:S(2)}) %collective-permute-start.28) | collective-permute-done | bytes 131104 | tf_op jit(solution)/shard_map/ppermute | solution.py:223
  149.1 0.8 collective-permute-start.29
  149.9 2.7 %collective-permute-start.31 = (f32[64,512]{1,0:T(8,128)S(1)}, f32[64,512]{1,0:T(8,128)S(1)}, u32[]{:S(2)}, u32[]{:S(2)}) collective-permute-start(f32[64,512]{1,0:T(8,128)S(1)} %add.179), channel_id=1, source_target_pairs={{0,6},{1,7},{2,4},{3,5},{4,2},{5,3},{6,0},{7,1},{8,14},{9,15},{10,... | collective-permute-start | bytes 393224 | tf_op jit(solution)/shard_map/ppermute | solution.py:223
  152.6 2.4 %collective-permute-done.29 = f32[64,512]{1,0:T(8,128)S(1)} collective-permute-done((f32[64,512]{1,0:T(8,128)S(1)}, f32[64,512]{1,0:T(8,128)S(1)}, u32[]{:S(2)}, u32[]{:S(2)}) %collective-permute-start.29) | collective-permute-done | bytes 131104 | tf_op jit(solution)/shard_map/ppermute | solution.py:223
  155.0 1.6 collective-permute-done.30
  156.8 11.5 %collective-permute-done.26 = f32[512,256]{1,0:T(8,128)S(1)} collective-permute-done((f32[512,256]{1,0:T(8,128)S(1)}, f32[512,256]{1,0:T(8,128)S(1)}, u32[]{:S(2)}, u32[]{:S(2)}) %collective-permute-start.26) | collective-permute-done | bytes 524320 | tf_op jit(solution)/shard_map/ppermute | solution.py:223
  168.5 1.2 maximum_select_fusion
  169.7 0.4 copy-done.8
  (94 shorter events, 1.4 us)
Async XLA Ops:
  0.7 14.0 %copy-start.16 = (s32[32,8,16]{0,2,1:T(8,128)S(1)}, s32[32,8,16]{0,2,1:T(8,128)}, u32[]{:S(2)}) copy-start(s32[32,8,16]{0,2,1:T(8,128)} %param.8) | copy-start | bytes 49156
  0.7 15.4 %copy-start.18 = (f32[32]{0:T(128)S(1)}, f32[32]{0:T(128)}, u32[]{:S(2)}) copy-start(f32[32]{0:T(128)} %param.6) | copy-start | bytes 388
  3.4 48.4 %copy-start = (f32[512,256]{1,0:T(8,128)}, f32[512,256]{1,0:T(8,128)S(1)}, u32[]{:S(2)}) copy-start(f32[512,256]{1,0:T(8,128)S(1)} %get-tuple-element.68.refs_4_) | copy-start | bytes 1572868
  3.4 23.3 %collective-permute-start.2 = (f32[512,256]{1,0:T(8,128)S(1)}, f32[512,256]{1,0:T(8,128)S(1)}, u32[]{:S(2)}, u32[]{:S(2)}) collective-permute-start(f32[512,256]{1,0:T(8,128)S(1)} %get-tuple-element.68.refs_4_), channel_id=1, source_target_pairs={{0,4},{1,5},{2,6},{3,7},{8,12},{9,13},{10,14},{11,15},{16,20},{17,... | collective-permute-start | bytes 1572872 | tf_op jit(solution)/shard_map/ppermute | solution.py:322
  8.3 22.3 %collective-permute-start = (f32[512,256]{1,0:T(8,128)S(1)}, f32[512,256]{1,0:T(8,128)S(1)}, u32[]{:S(2)}, u32[]{:S(2)}) collective-permute-start(f32[512,256]{1,0:T(8,128)S(1)} %get-tuple-element.67), channel_id=1, source_target_pairs={{0,8},{8,0},{16,24},{24,16},{1,9},{9,1},{17,25},{25,17},{2,10},{10... | collective-permute-start | bytes 1572872 | tf_op jit(solution)/shard_map/ppermute | solution.py:223
  11.9 38.5 %collective-permute-start.1 = (f32[512,256]{1,0:T(8,128)}, f32[512,256]{1,0:T(8,128)S(1)}, u32[]{:S(2)}, u32[]{:S(2)}) collective-permute-start(f32[512,256]{1,0:T(8,128)} %get-tuple-element.34), channel_id=1, source_target_pairs={{0,16},{8,24},{16,0},{24,8},{1,17},{9,25},{17,1},{25,9},{2,18},{10... | collective-permute-start | bytes 1572872 | tf_op jit(solution)/shard_map/ppermute | solution.py:223
  30.6 35.8 %copy-start.1 = (f32[512,256]{1,0:T(8,128)}, f32[512,256]{1,0:T(8,128)S(1)}, u32[]{:S(2)}) copy-start(f32[512,256]{1,0:T(8,128)S(1)} %collective-permute-done.refs_5_) | copy-start | bytes 1572868
  30.6 19.8 %collective-permute-start.4 = (f32[512,256]{1,0:T(8,128)S(1)}, f32[512,256]{1,0:T(8,128)S(1)}, u32[]{:S(2)}, u32[]{:S(2)}) collective-permute-start(f32[512,256]{1,0:T(8,128)S(1)} %collective-permute-done.refs_5_), channel_id=1, source_target_pairs={{0,4},{1,5},{2,6},{3,7},{8,12},{9,13},{10,14},{11,15},{16,20},{17,... | collective-permute-start | bytes 1572872 | tf_op jit(solution)/shard_map/ppermute | solution.py:322
  32.2 40.8 %copy-start.3 = (f32[512,256]{1,0:T(8,128)}, f32[512,256]{1,0:T(8,128)S(1)}, u32[]{:S(2)}) copy-start(f32[512,256]{1,0:T(8,128)S(1)} %broadcast_select_fusion.3.refs_8_) | copy-start | bytes 1572868
  32.2 19.6 %collective-permute-start.11 = (f32[512,256]{1,0:T(8,128)S(1)}, f32[512,256]{1,0:T(8,128)S(1)}, u32[]{:S(2)}, u32[]{:S(2)}) collective-permute-start(f32[512,256]{1,0:T(8,128)S(1)} %broadcast_select_fusion.3.refs_8_), channel_id=1, source_target_pairs={{0,2},{1,3},{2,0},{3,1},{4,6},{5,7},{6,4},{7,5},{8,10},{9,11},{10,... | collective-permute-start | bytes 1572872 | tf_op jit(solution)/shard_map/ppermute | solution.py:223
  33.8 43.2 %copy-start.17 = (f32[512]{0:T(512)S(1)}, f32[512]{0:T(512)}, u32[]{:S(2)}) copy-start(f32[512]{0:T(512)} %param.7) | copy-start | bytes 6148
  33.8 19.6 %collective-permute-start.3 = (f32[512,256]{1,0:T(8,128)}, f32[512,256]{1,0:T(8,128)S(1)}, u32[]{:S(2)}, u32[]{:S(2)}) collective-permute-start(f32[512,256]{1,0:T(8,128)} %get-tuple-element.35), channel_id=1, source_target_pairs={{0,24},{8,16},{16,8},{24,0},{1,25},{9,17},{17,9},{25,1},{2,26},{10... | collective-permute-start | bytes 1572872 | tf_op jit(solution)/shard_map/ppermute | solution.py:223
  50.4 22.6 %copy-start.2 = (f32[512,256]{1,0:T(8,128)}, f32[512,256]{1,0:T(8,128)S(1)}, u32[]{:S(2)}) copy-start(f32[512,256]{1,0:T(8,128)S(1)} %collective-permute-done.1.refs_6_) | copy-start | bytes 1572868
  50.4 11.4 %collective-permute-start.5 = (f32[512,256]{1,0:T(8,128)S(1)}, f32[512,256]{1,0:T(8,128)S(1)}, u32[]{:S(2)}, u32[]{:S(2)}) collective-permute-start(f32[512,256]{1,0:T(8,128)S(1)} %collective-permute-done.1.refs_6_), channel_id=1, source_target_pairs={{0,4},{1,5},{2,6},{3,7},{8,12},{9,13},{10,14},{11,15},{16,20},{17,... | collective-permute-start | bytes 1572872 | tf_op jit(solution)/shard_map/ppermute | solution.py:322
  51.8 26.7 %copy-start.5 = (f32[512,256]{1,0:T(8,128)}, f32[512,256]{1,0:T(8,128)S(1)}, u32[]{:S(2)}) copy-start(f32[512,256]{1,0:T(8,128)S(1)} %broadcast_select_fusion.2.refs_9_) | copy-start | bytes 1572868
  51.8 23.8 %copy-start.9 = (f32[512,256]{1,0:T(8,128)}, f32[512,256]{1,0:T(8,128)S(1)}, u32[]{:S(2)}) copy-start(f32[512,256]{1,0:T(8,128)S(1)} %collective-permute-done.11.refs_6_) | copy-start | bytes 1572868
  51.9 14.5 %collective-permute-start.12 = (f32[512,256]{1,0:T(8,128)S(1)}, f32[512,256]{1,0:T(8,128)S(1)}, u32[]{:S(2)}, u32[]{:S(2)}) collective-permute-start(f32[512,256]{1,0:T(8,128)S(1)} %broadcast_select_fusion.2.refs_9_), channel_id=1, source_target_pairs={{0,2},{1,3},{2,0},{3,1},{4,6},{5,7},{6,4},{7,5},{8,10},{9,11},{10,... | collective-permute-start | bytes 1572872 | tf_op jit(solution)/shard_map/ppermute | solution.py:223
  53.4 25.1 %copy-start.4 = (f32[512,256]{1,0:T(8,128)}, f32[512,256]{1,0:T(8,128)S(1)}, u32[]{:S(2)}) copy-start(f32[512,256]{1,0:T(8,128)S(1)} %collective-permute-done.3.refs_7_) | copy-start | bytes 1572868
  61.9 11.1 %collective-permute-start.6 = (f32[512,256]{1,0:T(8,128)S(1)}, f32[512,256]{1,0:T(8,128)S(1)}, u32[]{:S(2)}, u32[]{:S(2)}) collective-permute-start(f32[512,256]{1,0:T(8,128)S(1)} %collective-permute-done.3.refs_7_), channel_id=1, source_target_pairs={{0,4},{1,5},{2,6},{3,7},{8,12},{9,13},{10,14},{11,15},{16,20},{17,... | collective-permute-start | bytes 1572872 | tf_op jit(solution)/shard_map/ppermute | solution.py:322
  66.4 12.1 %copy-start.6 = (f32[512,256]{1,0:T(8,128)}, f32[512,256]{1,0:T(8,128)S(1)}, u32[]{:S(2)}) copy-start(f32[512,256]{1,0:T(8,128)S(1)} %broadcast_select_fusion.1.refs_10_) | copy-start | bytes 1572868
  66.4 9.3 %copy-start.10 = (f32[512,256]{1,0:T(8,128)}, f32[512,256]{1,0:T(8,128)S(1)}, u32[]{:S(2)}) copy-start(f32[512,256]{1,0:T(8,128)S(1)} %collective-permute-done.12.refs_7_) | copy-start | bytes 1572868
  66.4 9.2 %collective-permute-start.13 = (f32[512,256]{1,0:T(8,128)S(1)}, f32[512,256]{1,0:T(8,128)S(1)}, u32[]{:S(2)}, u32[]{:S(2)}) collective-permute-start(f32[512,256]{1,0:T(8,128)S(1)} %broadcast_select_fusion.1.refs_10_), channel_id=1, source_target_pairs={{0,2},{1,3},{2,0},{3,1},{4,6},{5,7},{6,4},{7,5},{8,10},{9,11},{10,... | collective-permute-start | bytes 1572872 | tf_op jit(solution)/shard_map/ppermute | solution.py:223
  66.5 11.4 %collective-permute-start.7 = (f32[512,256]{1,0:T(8,128)S(1)}, f32[512,256]{1,0:T(8,128)}, u32[]{:S(2)}, u32[]{:S(2)}) collective-permute-start(f32[512,256]{1,0:T(8,128)S(1)} %broadcast_select_fusion.3.refs_8_), channel_id=1, source_target_pairs={{0,1},{1,0},{2,3},{3,2},{4,5},{5,4},{6,7},{7,6},{8,9},{9,8},{10,11... | collective-permute-start | bytes 1572872 | tf_op jit(solution)/shard_map/ppermute | solution.py:223
  66.6 11.4 %collective-permute-start.8 = (f32[512,256]{1,0:T(8,128)S(1)}, f32[512,256]{1,0:T(8,128)}, u32[]{:S(2)}, u32[]{:S(2)}) collective-permute-start(f32[512,256]{1,0:T(8,128)S(1)} %broadcast_select_fusion.2.refs_9_), channel_id=1, source_target_pairs={{0,1},{1,0},{2,3},{3,2},{4,5},{5,4},{6,7},{7,6},{8,9},{9,8},{10,11... | collective-permute-start | bytes 1572872 | tf_op jit(solution)/shard_map/ppermute | solution.py:223
  67.1 11.4 %collective-permute-start.9 = (f32[512,256]{1,0:T(8,128)S(1)}, f32[512,256]{1,0:T(8,128)}, u32[]{:S(2)}, u32[]{:S(2)}) collective-permute-start(f32[512,256]{1,0:T(8,128)S(1)} %broadcast_select_fusion.1.refs_10_), channel_id=1, source_target_pairs={{0,1},{1,0},{2,3},{3,2},{4,5},{5,4},{6,7},{7,6},{8,9},{9,8},{10,11... | collective-permute-start | bytes 1572872 | tf_op jit(solution)/shard_map/ppermute | solution.py:223
  73.0 5.5 %copy-start.7 = (f32[512,256]{1,0:T(8,128)}, f32[512,256]{1,0:T(8,128)S(1)}, u32[]{:S(2)}) copy-start(f32[512,256]{1,0:T(8,128)S(1)} %broadcast_select_fusion.refs_11_) | copy-start | bytes 1572868
  73.0 5.5 %collective-permute-start.10 = (f32[512,256]{1,0:T(8,128)S(1)}, f32[512,256]{1,0:T(8,128)}, u32[]{:S(2)}, u32[]{:S(2)}) collective-permute-start(f32[512,256]{1,0:T(8,128)S(1)} %broadcast_select_fusion.refs_11_), channel_id=1, source_target_pairs={{0,1},{1,0},{2,3},{3,2},{4,5},{5,4},{6,7},{7,6},{8,9},{9,8},{10,11... | collective-permute-start | bytes 1572872 | tf_op jit(solution)/shard_map/ppermute | solution.py:223
  75.7 0.8 copy-start.11
  76.5 15.4 %collective-permute-start.14 = (f32[512,256]{1,0:T(8,128)S(1)}, f32[512,256]{1,0:T(8,128)S(1)}, u32[]{:S(2)}, u32[]{:S(2)}) collective-permute-start(f32[512,256]{1,0:T(8,128)S(1)} %broadcast_select_fusion.refs_11_), channel_id=1, source_target_pairs={{0,2},{1,3},{2,0},{3,1},{4,6},{5,7},{6,4},{7,5},{8,10},{9,11},{10,... | collective-permute-start | bytes 1572872 | tf_op jit(solution)/shard_map/ppermute | solution.py:223
  77.9 14.5 %collective-permute-start.15 = (f32[512,256]{1,0:T(8,128)}, f32[512,256]{1,0:T(8,128)S(1)}, u32[]{:S(2)}, u32[]{:S(2)}) collective-permute-start(f32[512,256]{1,0:T(8,128)} %copy-done.9), channel_id=1, source_target_pairs={{0,1},{1,0},{2,3},{3,2},{4,5},{5,4},{6,7},{7,6},{8,9},{9,8},{10,11... | collective-permute-start | bytes 1572872 | tf_op jit(solution)/shard_map/ppermute | solution.py:223
  77.9 14.5 %collective-permute-start.16 = (f32[512,256]{1,0:T(8,128)}, f32[512,256]{1,0:T(8,128)}, u32[]{:S(2)}, u32[]{:S(2)}) collective-permute-start(f32[512,256]{1,0:T(8,128)} %copy-done.10), channel_id=1, source_target_pairs={{0,1},{1,0},{2,3},{3,2},{4,5},{5,4},{6,7},{7,6},{8,9},{9,8},{10,11... | collective-permute-start | bytes 1572872 | tf_op jit(solution)/shard_map/ppermute | solution.py:223
  78.4 14.0 %collective-permute-start.17 = (f32[512,256]{1,0:T(8,128)}, f32[512,256]{1,0:T(8,128)}, u32[]{:S(2)}, u32[]{:S(2)}) collective-permute-start(f32[512,256]{1,0:T(8,128)} %copy-done.11), channel_id=1, source_target_pairs={{0,1},{1,0},{2,3},{3,2},{4,5},{5,4},{6,7},{7,6},{8,9},{9,8},{10,11... | collective-permute-start | bytes 1572872 | tf_op jit(solution)/shard_map/ppermute | solution.py:223
  91.9 2.1 %copy-start.12 = (f32[512,256]{1,0:T(8,128)}, f32[512,256]{1,0:T(8,128)S(1)}, u32[]{:S(2)}) copy-start(f32[512,256]{1,0:T(8,128)S(1)} %collective-permute-done.14.refs_9_) | copy-start | bytes 1572868
  91.9 2.0 %collective-permute-start.18 = (f32[512,256]{1,0:T(8,128)S(1)}, f32[512,256]{1,0:T(8,128)S(1)}, u32[]{:S(2)}, u32[]{:S(2)}) collective-permute-start(f32[512,256]{1,0:T(8,128)S(1)} %collective-permute-done.14.refs_9_), channel_id=1, source_target_pairs={{0,1},{1,0},{2,3},{3,2},{4,5},{5,4},{6,7},{7,6},{8,9},{9,8},{10,11... | collective-permute-start | bytes 1572872 | tf_op jit(solution)/shard_map/ppermute | solution.py:223
  92.4 1.5 copy-start.13
  94.0 0.8 copy-start.14
  109.4 22.1 %copy-start.21 = (f32[128,256]{1,0:T(8,128)S(1)}, f32[128,256]{1,0:T(8,128)}, u32[]{:S(2)}) copy-start(f32[128,256]{1,0:T(8,128)} %get-tuple-element.54) | copy-start | bytes 393220
  110.5 2.0 %collective-permute-start.20 = (f32[256,512]{1,0:T(8,128)S(1)}, f32[256,512]{1,0:T(8,128)S(1)}, u32[]{:S(2)}, u32[]{:S(2)}) collective-permute-start(f32[256,512]{1,0:T(8,128)S(1)} %constant_dynamic-slice_fusion.3), channel_id=1, source_target_pairs={{0,1},{1,0},{2,3},{3,2},{4,5},{5,4},{6,7},{7,6},{8,9},{9,8},{10,11... | collective-permute-start | bytes 1572872 | tf_op jit(solution)/shard_map/ppermute | solution.py:223
  110.9 20.5 %collective-permute-start.19 = (f32[384,256]{1,0:T(8,128)}, f32[384,256]{1,0:T(8,128)S(1)}, u32[]{:S(2)}, u32[]{:S(2)}) collective-permute-start(f32[384,256]{1,0:T(8,128)} %get-tuple-element.51), channel_id=1, source_target_pairs={{0,16},{8,24},{16,0},{24,8},{1,17},{9,25},{17,1},{25,9},{2,18},{10... | collective-permute-start | bytes 1179656 | tf_op jit(solution)/shard_map/ppermute | solution.py:223
  113.6 27.6 %copy-start.19 = (f32[512,256]{1,0:T(8,128)S(1)}, f32[512,256]{1,0:T(8,128)}, u32[]{:S(2)}) copy-start(f32[512,256]{1,0:T(8,128)} %get-tuple-element.61) | copy-start | bytes 1572868
  113.6 29.7 %copy-start.20 = (f32[512,256]{1,0:T(8,128)S(1)}, f32[512,256]{1,0:T(8,128)}, u32[]{:S(2)}) copy-start(f32[512,256]{1,0:T(8,128)} %get-tuple-element.58) | copy-start | bytes 1572868
  113.7 6.2 %collective-permute-start.21 = (f32[64,512]{1,0:T(8,128)S(1)}, f32[64,512]{1,0:T(8,128)S(1)}, u32[]{:S(2)}, u32[]{:S(2)}) collective-permute-start(f32[64,512]{1,0:T(8,128)S(1)} %get-tuple-element.70), channel_id=1, source_target_pairs={{0,2},{1,3},{2,0},{3,1},{4,6},{5,7},{6,4},{7,5},{8,10},{9,11},{10,... | collective-permute-start | bytes 393224 | tf_op jit(solution)/shard_map/ppermute | solution.py:223
  115.2 8.3 %collective-permute-start.22 = (f32[64,512]{1,0:T(8,128)S(1)}, f32[64,512]{1,0:T(8,128)S(1)}, u32[]{:S(2)}, u32[]{:S(2)}) collective-permute-start(f32[64,512]{1,0:T(8,128)S(1)} %get-tuple-element.72), channel_id=1, source_target_pairs={{0,4},{1,5},{2,6},{3,7},{4,0},{5,1},{6,2},{7,3},{8,12},{9,13},{10,... | collective-permute-start | bytes 393224 | tf_op jit(solution)/shard_map/ppermute | solution.py:223
  115.3 8.2 %collective-permute-start.23 = (f32[64,512]{1,0:T(8,128)S(1)}, f32[64,512]{1,0:T(8,128)S(1)}, u32[]{:S(2)}, u32[]{:S(2)}) collective-permute-start(f32[64,512]{1,0:T(8,128)S(1)} %get-tuple-element.71), channel_id=1, source_target_pairs={{0,6},{1,7},{2,4},{3,5},{4,2},{5,3},{6,0},{7,1},{8,14},{9,15},{10,... | collective-permute-start | bytes 393224 | tf_op jit(solution)/shard_map/ppermute | solution.py:223
  131.5 7.5 %collective-permute-start.25 = (f32[64,512]{1,0:T(8,128)S(1)}, f32[64,512]{1,0:T(8,128)S(1)}, u32[]{:S(2)}, u32[]{:S(2)}) collective-permute-start(f32[64,512]{1,0:T(8,128)S(1)} %add_add_fusion), channel_id=1, source_target_pairs={{0,8},{8,0},{16,24},{24,16},{1,9},{9,1},{17,25},{25,17},{2,10},{10... | collective-permute-start | bytes 393224 | tf_op jit(solution)/shard_map/ppermute | solution.py:223
  131.5 9.2 %collective-permute-start.24 = (f32[128,256]{1,0:T(8,128)S(1)}, f32[128,256]{1,0:T(8,128)S(1)}, u32[]{:S(2)}, u32[]{:S(2)}) collective-permute-start(f32[128,256]{1,0:T(8,128)S(1)} %copy-done.21), channel_id=1, source_target_pairs={{0,16},{8,24},{16,0},{24,8},{1,17},{9,25},{17,1},{25,9},{2,18},{10... | collective-permute-start | bytes 393224 | tf_op jit(solution)/shard_map/ppermute | solution.py:223
  140.7 8.4 %collective-permute-start.28 = (f32[64,512]{1,0:T(8,128)S(1)}, f32[64,512]{1,0:T(8,128)S(1)}, u32[]{:S(2)}, u32[]{:S(2)}) collective-permute-start(f32[64,512]{1,0:T(8,128)S(1)} %add.176), channel_id=1, source_target_pairs={{0,16},{8,24},{16,0},{24,8},{1,17},{9,25},{17,1},{25,9},{2,18},{10... | collective-permute-start | bytes 393224 | tf_op jit(solution)/shard_map/ppermute | solution.py:223
  141.2 27.2 %copy-start.15 = (f32[512,256]{1,0:T(8,128)S(1)}, f32[512,256]{1,0:T(8,128)}, u32[]{:S(2)}) copy-start(f32[512,256]{1,0:T(8,128)} %get-tuple-element.59) | copy-start | bytes 1572868
  141.2 27.2 %collective-permute-start.27 = (f32[512,256]{1,0:T(8,128)S(1)}, f32[512,256]{1,0:T(8,128)S(1)}, u32[]{:S(2)}, u32[]{:S(2)}) collective-permute-start(f32[512,256]{1,0:T(8,128)S(1)} %copy-done.19), channel_id=1, source_target_pairs={{0,8},{8,0},{16,24},{24,16},{1,9},{9,1},{17,25},{25,17},{2,10},{10... | collective-permute-start | bytes 1572872 | tf_op jit(solution)/shard_map/ppermute | solution.py:223
  143.4 24.9 %collective-permute-start.26 = (f32[512,256]{1,0:T(8,128)S(1)}, f32[512,256]{1,0:T(8,128)S(1)}, u32[]{:S(2)}, u32[]{:S(2)}) collective-permute-start(f32[512,256]{1,0:T(8,128)S(1)} %copy-done.20), channel_id=1, source_target_pairs={{0,24},{8,16},{16,8},{24,0},{1,25},{9,17},{17,9},{25,1},{2,26},{10... | collective-permute-start | bytes 1572872 | tf_op jit(solution)/shard_map/ppermute | solution.py:223
  149.1 5.9 %collective-permute-start.29 = (f32[64,512]{1,0:T(8,128)S(1)}, f32[64,512]{1,0:T(8,128)S(1)}, u32[]{:S(2)}, u32[]{:S(2)}) collective-permute-start(f32[64,512]{1,0:T(8,128)S(1)} %add.179), channel_id=1, source_target_pairs={{0,2},{1,3},{2,0},{3,1},{4,6},{5,7},{6,4},{7,5},{8,10},{9,11},{10,... | collective-permute-start | bytes 393224 | tf_op jit(solution)/shard_map/ppermute | solution.py:223
  149.9 6.8 %collective-permute-start.30 = (f32[64,512]{1,0:T(8,128)S(1)}, f32[64,512]{1,0:T(8,128)S(1)}, u32[]{:S(2)}, u32[]{:S(2)}) collective-permute-start(f32[64,512]{1,0:T(8,128)S(1)} %add.179), channel_id=1, source_target_pairs={{0,4},{1,5},{2,6},{3,7},{4,0},{5,1},{6,2},{7,3},{8,12},{9,13},{10,... | collective-permute-start | bytes 393224 | tf_op jit(solution)/shard_map/ppermute | solution.py:223
  149.9 6.7 %collective-permute-start.31 = (f32[64,512]{1,0:T(8,128)S(1)}, f32[64,512]{1,0:T(8,128)S(1)}, u32[]{:S(2)}, u32[]{:S(2)}) collective-permute-start(f32[64,512]{1,0:T(8,128)S(1)} %add.179), channel_id=1, source_target_pairs={{0,6},{1,7},{2,4},{3,5},{4,2},{5,3},{6,0},{7,1},{8,14},{9,15},{10,... | collective-permute-start | bytes 393224 | tf_op jit(solution)/shard_map/ppermute | solution.py:223
  156.7 11.8 %collective-permute-start.32 = (f32[256,512]{1,0:T(8,128)S(1)}, f32[256,512]{1,0:T(8,128)S(1)}, u32[]{:S(2)}, u32[]{:S(2)}) collective-permute-start(f32[256,512]{1,0:T(8,128)S(1)} %maximum_select_fusion.1), channel_id=1, source_target_pairs={{0,1},{1,0},{2,3},{3,2},{4,5},{5,4},{6,7},{7,6},{8,9},{9,8},{10,11... | collective-permute-start | bytes 1572872 | tf_op jit(solution)/shard_map/ppermute | solution.py:223
  168.5 1.7 copy-start.8

commit v4 on v3

--- a/solution.py
+++ b/solution.py
@@ -295,7 +295,7 @@
         live = jnp.any(lists == panels[turn]).astype(jnp.float32)
         scalars += [occ_energy[own_orbital] + occ_energy[orbitals[1 + turn]], live]
     small = masks[:3], masks[3:], jnp.stack(scalars[:4]), jnp.stack(scalars[4:])
-    virtual = lax.optimization_barrier((vir_energy[:, None], vir_energy[None, :]))
+    virtual = vir_energy[:, None], vir_energy[None, :]
 
     own, came, near, far = [], [], [], []
 
@@ -324,7 +324,7 @@
             reach *= 2
         came.append(got)
         near.append(rows)
-        sent = after(rows, far[-1]) if at else after(rows, *small, *virtual)
+        sent = after(rows, far[-1]) if at else after(rows, *small)
         far.append(exchange(sent, "col", 2))
 
     near_twin = [exchange(piece, "col", 1) for piece in near]
@@ -346,15 +346,14 @@
     def leave(at, *others):
         return exchange(after(pieces[at], *others), "row", wanted[at][0])
 
-    ends = [leave(0)]
+    ends, others = [leave(0)], [leave(at) for at in range(4, len(wanted))]
     total = scatter_plane(scatter_chip(total))
     ends.append(leave(1, total))
-    total = after(total, ends[0])
+    total = after(total, ends[0], *others)
     for bit in bits("row")[:-1]:
         total = total + exchange(total, "row", bit)
     total = after(total, ends[1])
-    ends += [leave(2, total), pieces[3]]
-    ends += [leave(at, total) for at in range(4, len(wanted))]
+    ends += [leave(2, total), pieces[3], *others]
     total = total + exchange(total, "row", bits("row")[-1])
     total = gather_plane(total)
 

time: 171 us -> 173 us (1.012)
  waiting for transfers between devices: 77.2 us -> 79.9 us
    ppermute x29, waiting for transfers between devices: 63 us -> 65.7 us  [exchange(): return lax.ppermute(value, axis, [(at, at ^ bit) for at in range(size)])]
  transfers between devices with their start and end apart: 33 -> 33, of which waited for: 16 -> 16; matrix products, arithmetic and copies ran while one was open for 6% -> 5% of each run, Pallas kernels for 8% -> 8%
where the time goes in v4:
time: 173 us
  waiting for transfers between devices  79.9 us (46%)
  starting transfers between devices  40.8 us (24%)
  Pallas kernels  27.9 us (16%)
  local copies, waits for them, and re-layouts  10.1 us (6%)
  between operations  8.75 us (5%)
  other arithmetic  5.27 us (3%)
    ppermute x29, waiting for transfers between devices, exchange(): return lax.ppermute(value, axis, [(at, at ^ bit) for at in range(size)])  65.7 us
    pallas_call x2, Pallas kernels, call(): pl.pallas_call(functools.partial(staged, kernel, len(small), len(big), le...  27.9 us
    ppermute x29, starting transfers between devices, exchange(): return lax.ppermute(value, axis, [(at, at ^ bit) for at in range(size)])  27.8 us
    ppermute x4, waiting for transfers between devices, on_device(): got = lax.ppermute(rows, 'col', links)  14.2 us
    ppermute x4, starting transfers between devices, on_device(): got = lax.ppermute(rows, 'col', links)  12.9 us
  transfers between devices with their start and end apart: 33, of which 16 were waited for; matrix products, arithmetic and copies ran while one was open for 5% of the time, Pallas kernels for 8%

profile of v4, /device:TPU:0, one launch (start us, length us, event | category | flops | bytes accessed | tf_op | source)
XLA Modules:
  0.0 172.8 jit_solution(16177544817817862632)
XLA Ops:
  0.7 2.7 %dynamic-slice_bitcast_fusion = (f32[512,256]{1,0:T(8,128)}, f32[512,256]{1,0:T(8,128)S(1)}, f32[512,256]{1,0:T(8,128)S(1)}, f32[512,256]{1,0:T(8,128)}) fusion(f32[4,512,256]{2,1,0:T(8,128)} %param.5, s32[]{:T(128)S(6)} %select_n.171, s32[]{:T(128)S(6)} %select_n.169, s32[]{:T(128)S(6)} %select_n.163, s32[]{:T(128)S(6)} %select_n.170), kind=kLoop, calls=%fused_computation.8 | loop fusion | bytes 4194320 | tf_op jit(solution)/shard_map/jit(dynamic_index_in_dim)/squeeze | solution.py:304
  3.4 4.9 %collective-permute-start.2 = (f32[512,256]{1,0:T(8,128)S(1)}, f32[512,256]{1,0:T(8,128)S(1)}, u32[]{:S(2)}, u32[]{:S(2)}) collective-permute-start(f32[512,256]{1,0:T(8,128)S(1)} %get-tuple-element.62.refs_4_), channel_id=1, source_target_pairs={{0,4},{1,5},{2,6},{3,7},{8,12},{9,13},{10,14},{11,15},{16,20},{17,... | collective-permute-start | bytes 1572872 | tf_op jit(solution)/shard_map/ppermute | solution.py:322
  8.3 1.6 collective-permute-start
  9.9 1.4 compare_reduce_fusion.1
  12.0 2.7 %collective-permute-start.1 = (f32[512,256]{1,0:T(8,128)}, f32[512,256]{1,0:T(8,128)S(1)}, u32[]{:S(2)}, u32[]{:S(2)}) collective-permute-start(f32[512,256]{1,0:T(8,128)} %get-tuple-element.29), channel_id=1, source_target_pairs={{0,16},{8,24},{16,0},{24,8},{1,17},{9,25},{17,1},{25,9},{2,18},{10... | collective-permute-start | bytes 1572872 | tf_op jit(solution)/shard_map/ppermute | solution.py:223
  14.6 0.1 stack.59
  14.7 0.1 copy.12
  14.9 0.6 gather_fusion
  15.5 0.6 gather_fusion.1
  16.2 0.7 fusion.2
  23.8 0.1 broadcast_in_dim.35
  23.9 0.8 slice.25.refs_3_
  24.8 0.1 broadcast_in_dim.34
  24.9 0.7 slice.22.refs_3_
  25.6 0.6 pad_maximum_fusion.1.refs_0_
  26.2 0.6 pad_maximum_fusion.refs_0_
  26.8 3.7 %collective-permute-done.refs_5_ = f32[512,256]{1,0:T(8,128)S(1)} collective-permute-done((f32[512,256]{1,0:T(8,128)S(1)}, f32[512,256]{1,0:T(8,128)S(1)}, u32[]{:S(2)}, u32[]{:S(2)}) %collective-permute-start) | collective-permute-done | bytes 524320 | tf_op jit(solution)/shard_map/ppermute | solution.py:223
  30.5 2.3 %collective-permute-start.4 = (f32[512,256]{1,0:T(8,128)S(1)}, f32[512,256]{1,0:T(8,128)}, u32[]{:S(2)}, u32[]{:S(2)}) collective-permute-start(f32[512,256]{1,0:T(8,128)S(1)} %collective-permute-done.refs_5_), channel_id=1, source_target_pairs={{0,4},{1,5},{2,6},{3,7},{8,12},{9,13},{10,14},{11,15},{16,20},{17,... | collective-permute-start | bytes 1572872 | tf_op jit(solution)/shard_map/ppermute | solution.py:322
  33.0 1.6 collective-permute-start.11
  34.5 2.5 %collective-permute-start.3 = (f32[512,256]{1,0:T(8,128)}, f32[512,256]{1,0:T(8,128)S(1)}, u32[]{:S(2)}, u32[]{:S(2)}) collective-permute-start(f32[512,256]{1,0:T(8,128)} %get-tuple-element.30), channel_id=1, source_target_pairs={{0,24},{8,16},{16,8},{24,0},{1,25},{9,17},{17,9},{25,1},{2,26},{10... | collective-permute-start | bytes 1572872 | tf_op jit(solution)/shard_map/ppermute | solution.py:223
  37.0 13.5 %collective-permute-done.1.refs_6_ = f32[512,256]{1,0:T(8,128)S(1)} collective-permute-done((f32[512,256]{1,0:T(8,128)}, f32[512,256]{1,0:T(8,128)S(1)}, u32[]{:S(2)}, u32[]{:S(2)}) %collective-permute-start.1) | collective-permute-done | bytes 524320 | tf_op jit(solution)/shard_map/ppermute | solution.py:223
  50.5 1.3 collective-permute-start.5
  51.8 0.1 broadcast_select_fusion.2.refs_9_
  51.9 1.6 collective-permute-start.12
  53.5 8.4 %collective-permute-done.5 = f32[512,256]{1,0:T(8,128)S(1)} collective-permute-done((f32[512,256]{1,0:T(8,128)S(1)}, f32[512,256]{1,0:T(8,128)S(1)}, u32[]{:S(2)}, u32[]{:S(2)}) %collective-permute-start.5) | collective-permute-done | bytes 524320 | tf_op jit(solution)/shard_map/ppermute | solution.py:322
  61.9 4.4 %collective-permute-start.6 = (f32[512,256]{1,0:T(8,128)S(1)}, f32[512,256]{1,0:T(8,128)S(1)}, u32[]{:S(2)}, u32[]{:S(2)}) collective-permute-start(f32[512,256]{1,0:T(8,128)S(1)} %collective-permute-done.3.refs_7_), channel_id=1, source_target_pairs={{0,4},{1,5},{2,6},{3,7},{8,12},{9,13},{10,14},{11,15},{16,20},{17,... | collective-permute-start | bytes 1572872 | tf_op jit(solution)/shard_map/ppermute | solution.py:322
  66.6 0.5 collective-permute-start.8
  67.1 0.1 collective-permute-start.9
  67.2 5.8 %collective-permute-done.6 = f32[512,256]{1,0:T(8,128)S(1)} collective-permute-done((f32[512,256]{1,0:T(8,128)S(1)}, f32[512,256]{1,0:T(8,128)S(1)}, u32[]{:S(2)}, u32[]{:S(2)}) %collective-permute-start.6) | collective-permute-done | bytes 524320 | tf_op jit(solution)/shard_map/ppermute | solution.py:322
  73.1 2.5 %collective-permute-done.13.refs_8_ = f32[512,256]{1,0:T(8,128)S(1)} collective-permute-done((f32[512,256]{1,0:T(8,128)S(1)}, f32[512,256]{1,0:T(8,128)S(1)}, u32[]{:S(2)}, u32[]{:S(2)}) %collective-permute-start.13) | collective-permute-done | bytes 524320 | tf_op jit(solution)/shard_map/ppermute | solution.py:223
  75.7 0.6 collective-permute-start.14
  76.3 0.2 copy-done.11
  76.5 0.9 copy.19.refs_1_
  77.4 0.5 collective-permute-start.16
  78.0 13.4 %early.1 = (bf16[512,1024]{1,0:T(8,128)(2,1)}, bf16[512,1024]{1,0:T(8,128)(2,1)}, f32[512,512]{1,0:T(8,128)}, f32[512,256]{1,0:T(8,128)}, f32[512,256]{1,0:T(8,1...) custom-call(f32[4]{0:T(128)} %pad_maximum_fusion.1.refs_0_, f32[512,1]{1,0:T(8,128)} %copy.19.refs_1_, f32[1,512]{1,0:T(1,128)} %bitcast.45, ...), custom_call_target="tpu_custom_call" | custom-call | tf_op jit(solution)/shard_map/early/pallas_call | solution.py:41
  91.4 0.5 collective-permute-start.18
  91.9 1.5 collective-permute-done.18.refs_13_
  93.5 0.8 copy-done.14
  94.3 14.6 %late.1 = (f32[512,512]{1,0:T(8,128)}, f32[384,256]{1,0:T(8,128)}, f32[128,256]{1,0:T(8,128)}, f32[512,256]{1,0:T(8,128)}, f32[512,256]{1,0:T(8,128)}, /*index=5*/f32[512,256]{1,0:T(8,128)}) custom-call(f32[4]{0:T(128)} %pad_maximum_fusion.refs_0_, f32[512,1]{1,0:T(8,128)} %copy.19.refs_1_, f32[1,512]{1,0:T(1,128)} %bitcast.46, ...), custom_call_target="tpu_custom_call" | custom-call | tf_op jit(solution)/shard_map/late/pallas_call | solution.py:41
  108.8 1.1 constant_dynamic-slice_fusion.3
  110.0 0.4 collective-permute-start.20
  110.4 3.0 %collective-permute-start.19 = (f32[384,256]{1,0:T(8,128)}, f32[384,256]{1,0:T(8,128)S(1)}, u32[]{:S(2)}, u32[]{:S(2)}) collective-permute-start(f32[384,256]{1,0:T(8,128)} %get-tuple-element.46), channel_id=1, source_target_pairs={{0,16},{8,24},{16,0},{24,8},{1,17},{9,25},{17,1},{25,9},{2,18},{10... | collective-permute-start | bytes 1179656 | tf_op jit(solution)/shard_map/ppermute | solution.py:223
  113.4 1.1 dynamic-slice_add_fusion
  114.6 1.3 collective-permute-start.21
  115.9 2.2 %collective-permute-start.23 = (f32[64,512]{1,0:T(8,128)S(1)}, f32[64,512]{1,0:T(8,128)S(1)}, u32[]{:S(2)}, u32[]{:S(2)}) collective-permute-start(f32[64,512]{1,0:T(8,128)S(1)} %get-tuple-element.65), channel_id=1, source_target_pairs={{0,6},{1,7},{2,4},{3,5},{4,2},{5,3},{6,0},{7,1},{8,14},{9,15},{10,... | collective-permute-start | bytes 393224 | tf_op jit(solution)/shard_map/ppermute | solution.py:223
  118.2 2.2 %collective-permute-done.21 = f32[64,512]{1,0:T(8,128)S(1)} collective-permute-done((f32[64,512]{1,0:T(8,128)S(1)}, f32[64,512]{1,0:T(8,128)S(1)}, u32[]{:S(2)}, u32[]{:S(2)}) %collective-permute-start.21) | collective-permute-done | bytes 131104 | tf_op jit(solution)/shard_map/ppermute | solution.py:223
  120.4 3.0 %collective-permute-done.22 = f32[64,512]{1,0:T(8,128)S(1)} collective-permute-done((f32[64,512]{1,0:T(8,128)S(1)}, f32[64,512]{1,0:T(8,128)S(1)}, u32[]{:S(2)}, u32[]{:S(2)}) %collective-permute-start.22) | collective-permute-done | bytes 131104 | tf_op jit(solution)/shard_map/ppermute | solution.py:223
  123.5 7.5 %collective-permute-done.19 = f32[384,256]{1,0:T(8,128)S(1)} collective-permute-done((f32[384,256]{1,0:T(8,128)}, f32[384,256]{1,0:T(8,128)S(1)}, u32[]{:S(2)}, u32[]{:S(2)}) %collective-permute-start.19) | collective-permute-done | bytes 393248 | tf_op jit(solution)/shard_map/ppermute | solution.py:223
  130.9 2.1 %collective-permute-done.25 = f32[512,256]{1,0:T(8,128)S(1)} collective-permute-done((f32[512,256]{1,0:T(8,128)}, f32[512,256]{1,0:T(8,128)S(1)}, u32[]{:S(2)}, u32[]{:S(2)}) %collective-permute-start.25) | collective-permute-done | bytes 524320 | tf_op jit(solution)/shard_map/ppermute | solution.py:223
  133.0 1.3 collective-permute-start.26
  134.3 1.7 %collective-permute-start.24 = (f32[128,256]{1,0:T(8,128)S(1)}, f32[128,256]{1,0:T(8,128)S(1)}, u32[]{:S(2)}, u32[]{:S(2)}) collective-permute-start(f32[128,256]{1,0:T(8,128)S(1)} %copy-done.20), channel_id=1, source_target_pairs={{0,16},{8,24},{16,0},{24,8},{1,17},{9,25},{17,1},{25,9},{2,18},{10... | collective-permute-start | bytes 393224 | tf_op jit(solution)/shard_map/ppermute | solution.py:223
  136.1 2.9 %collective-permute-done.26 = f32[64,512]{1,0:T(8,128)S(1)} collective-permute-done((f32[64,512]{1,0:T(8,128)S(1)}, f32[64,512]{1,0:T(8,128)S(1)}, u32[]{:S(2)}, u32[]{:S(2)}) %collective-permute-start.26) | collective-permute-done | bytes 131104 | tf_op jit(solution)/shard_map/ppermute | solution.py:223
  139.0 3.8 %collective-permute-done.24 = f32[128,256]{1,0:T(8,128)S(1)} collective-permute-done((f32[128,256]{1,0:T(8,128)S(1)}, f32[128,256]{1,0:T(8,128)S(1)}, u32[]{:S(2)}, u32[]{:S(2)}) %collective-permute-start.24) | collective-permute-done | bytes 131104 | tf_op jit(solution)/shard_map/ppermute | solution.py:223
  142.8 0.4 collective-permute-start.28
  143.1 0.2 broadcast_in_dim.31
  143.4 1.4 collective-permute-start.27
  144.8 16.9 %collective-permute-done.28 = f32[64,512]{1,0:T(8,128)S(1)} collective-permute-done((f32[64,512]{1,0:T(8,128)S(1)}, f32[64,512]{1,0:T(8,128)S(1)}, u32[]{:S(2)}, u32[]{:S(2)}) %collective-permute-start.28) | collective-permute-done | bytes 131104 | tf_op jit(solution)/shard_map/ppermute | solution.py:223
  161.7 1.3 collective-permute-start.29
  162.9 0.1 collective-permute-start.30
  163.1 2.1 %collective-permute-start.31 = (f32[64,512]{1,0:T(8,128)S(1)}, f32[64,512]{1,0:T(8,128)S(1)}, u32[]{:S(2)}, u32[]{:S(2)}) collective-permute-start(f32[64,512]{1,0:T(8,128)S(1)} %add.179), channel_id=1, source_target_pairs={{0,6},{1,7},{2,4},{3,5},{4,2},{5,3},{6,0},{7,1},{8,14},{9,15},{10,... | collective-permute-start | bytes 393224 | tf_op jit(solution)/shard_map/ppermute | solution.py:223
  165.2 2.6 %collective-permute-done.29 = f32[64,512]{1,0:T(8,128)S(1)} collective-permute-done((f32[64,512]{1,0:T(8,128)S(1)}, f32[64,512]{1,0:T(8,128)S(1)}, u32[]{:S(2)}, u32[]{:S(2)}) %collective-permute-start.29) | collective-permute-done | bytes 131104 | tf_op jit(solution)/shard_map/ppermute | solution.py:223
  167.9 1.8 %collective-permute-done.30 = f32[64,512]{1,0:T(8,128)S(1)} collective-permute-done((f32[64,512]{1,0:T(8,128)S(1)}, f32[64,512]{1,0:T(8,128)S(1)}, u32[]{:S(2)}, u32[]{:S(2)}) %collective-permute-start.30) | collective-permute-done | bytes 131104 | tf_op jit(solution)/shard_map/ppermute | solution.py:223
  170.0 1.7 collective-permute-done.32
  171.7 1.1 maximum_select_fusion
  (92 shorter events, 1.4 us)
Async XLA Ops:
  0.7 14.1 %copy-start.16 = (s32[32,8,16]{0,2,1:T(8,128)S(1)}, s32[32,8,16]{0,2,1:T(8,128)}, u32[]{:S(2)}) copy-start(s32[32,8,16]{0,2,1:T(8,128)} %param.8) | copy-start | bytes 49156
  0.7 15.5 %copy-start.18 = (f32[32]{0:T(128)S(1)}, f32[32]{0:T(128)}, u32[]{:S(2)}) copy-start(f32[32]{0:T(128)} %param.6) | copy-start | bytes 388
  3.4 48.5 %copy-start = (f32[512,256]{1,0:T(8,128)}, f32[512,256]{1,0:T(8,128)S(1)}, u32[]{:S(2)}) copy-start(f32[512,256]{1,0:T(8,128)S(1)} %get-tuple-element.62.refs_4_) | copy-start | bytes 1572868
  3.4 23.4 %collective-permute-start.2 = (f32[512,256]{1,0:T(8,128)S(1)}, f32[512,256]{1,0:T(8,128)S(1)}, u32[]{:S(2)}, u32[]{:S(2)}) collective-permute-start(f32[512,256]{1,0:T(8,128)S(1)} %get-tuple-element.62.refs_4_), channel_id=1, source_target_pairs={{0,4},{1,5},{2,6},{3,7},{8,12},{9,13},{10,14},{11,15},{16,20},{17,... | collective-permute-start | bytes 1572872 | tf_op jit(solution)/shard_map/ppermute | solution.py:322
  8.3 22.3 %collective-permute-start = (f32[512,256]{1,0:T(8,128)S(1)}, f32[512,256]{1,0:T(8,128)S(1)}, u32[]{:S(2)}, u32[]{:S(2)}) collective-permute-start(f32[512,256]{1,0:T(8,128)S(1)} %get-tuple-element.61), channel_id=1, source_target_pairs={{0,8},{8,0},{16,24},{24,16},{1,9},{9,1},{17,25},{25,17},{2,10},{10... | collective-permute-start | bytes 1572872 | tf_op jit(solution)/shard_map/ppermute | solution.py:223
  12.0 38.5 %collective-permute-start.1 = (f32[512,256]{1,0:T(8,128)}, f32[512,256]{1,0:T(8,128)S(1)}, u32[]{:S(2)}, u32[]{:S(2)}) collective-permute-start(f32[512,256]{1,0:T(8,128)} %get-tuple-element.29), channel_id=1, source_target_pairs={{0,16},{8,24},{16,0},{24,8},{1,17},{9,25},{17,1},{25,9},{2,18},{10... | collective-permute-start | bytes 1572872 | tf_op jit(solution)/shard_map/ppermute | solution.py:223
  30.5 35.9 %copy-start.1 = (f32[512,256]{1,0:T(8,128)}, f32[512,256]{1,0:T(8,128)S(1)}, u32[]{:S(2)}) copy-start(f32[512,256]{1,0:T(8,128)S(1)} %collective-permute-done.refs_5_) | copy-start | bytes 1572868
  30.5 19.9 %collective-permute-start.4 = (f32[512,256]{1,0:T(8,128)S(1)}, f32[512,256]{1,0:T(8,128)}, u32[]{:S(2)}, u32[]{:S(2)}) collective-permute-start(f32[512,256]{1,0:T(8,128)S(1)} %collective-permute-done.refs_5_), channel_id=1, source_target_pairs={{0,4},{1,5},{2,6},{3,7},{8,12},{9,13},{10,14},{11,15},{16,20},{17,... | collective-permute-start | bytes 1572872 | tf_op jit(solution)/shard_map/ppermute | solution.py:322
  32.9 40.1 %copy-start.3 = (f32[512,256]{1,0:T(8,128)}, f32[512,256]{1,0:T(8,128)S(1)}, u32[]{:S(2)}) copy-start(f32[512,256]{1,0:T(8,128)S(1)} %broadcast_select_fusion.3.refs_8_) | copy-start | bytes 1572868
  33.0 18.9 %collective-permute-start.11 = (f32[512,256]{1,0:T(8,128)S(1)}, f32[512,256]{1,0:T(8,128)S(1)}, u32[]{:S(2)}, u32[]{:S(2)}) collective-permute-start(f32[512,256]{1,0:T(8,128)S(1)} %broadcast_select_fusion.3.refs_8_), channel_id=1, source_target_pairs={{0,2},{1,3},{2,0},{3,1},{4,6},{5,7},{6,4},{7,5},{8,10},{9,11},{10,... | collective-permute-start | bytes 1572872 | tf_op jit(solution)/shard_map/ppermute | solution.py:223
  34.5 42.0 %copy-start.17 = (f32[512]{0:T(512)S(1)}, f32[512]{0:T(512)}, u32[]{:S(2)}) copy-start(f32[512]{0:T(512)} %param.7) | copy-start | bytes 6148
  34.5 19.0 %collective-permute-start.3 = (f32[512,256]{1,0:T(8,128)}, f32[512,256]{1,0:T(8,128)S(1)}, u32[]{:S(2)}, u32[]{:S(2)}) collective-permute-start(f32[512,256]{1,0:T(8,128)} %get-tuple-element.30), channel_id=1, source_target_pairs={{0,24},{8,16},{16,8},{24,0},{1,25},{9,17},{17,9},{25,1},{2,26},{10... | collective-permute-start | bytes 1572872 | tf_op jit(solution)/shard_map/ppermute | solution.py:223
  50.5 22.6 %copy-start.2 = (f32[512,256]{1,0:T(8,128)}, f32[512,256]{1,0:T(8,128)S(1)}, u32[]{:S(2)}) copy-start(f32[512,256]{1,0:T(8,128)S(1)} %collective-permute-done.1.refs_6_) | copy-start | bytes 1572868
  50.5 11.4 %collective-permute-start.5 = (f32[512,256]{1,0:T(8,128)S(1)}, f32[512,256]{1,0:T(8,128)S(1)}, u32[]{:S(2)}, u32[]{:S(2)}) collective-permute-start(f32[512,256]{1,0:T(8,128)S(1)} %collective-permute-done.1.refs_6_), channel_id=1, source_target_pairs={{0,4},{1,5},{2,6},{3,7},{8,12},{9,13},{10,14},{11,15},{16,20},{17,... | collective-permute-start | bytes 1572872 | tf_op jit(solution)/shard_map/ppermute | solution.py:322
  51.9 26.1 %copy-start.5 = (f32[512,256]{1,0:T(8,128)}, f32[512,256]{1,0:T(8,128)S(1)}, u32[]{:S(2)}) copy-start(f32[512,256]{1,0:T(8,128)S(1)} %broadcast_select_fusion.2.refs_9_) | copy-start | bytes 1572868
  51.9 23.8 %copy-start.9 = (f32[512,256]{1,0:T(8,128)}, f32[512,256]{1,0:T(8,128)S(1)}, u32[]{:S(2)}) copy-start(f32[512,256]{1,0:T(8,128)S(1)} %collective-permute-done.11.refs_6_) | copy-start | bytes 1572868
  51.9 14.5 %collective-permute-start.12 = (f32[512,256]{1,0:T(8,128)S(1)}, f32[512,256]{1,0:T(8,128)S(1)}, u32[]{:S(2)}, u32[]{:S(2)}) collective-permute-start(f32[512,256]{1,0:T(8,128)S(1)} %broadcast_select_fusion.2.refs_9_), channel_id=1, source_target_pairs={{0,2},{1,3},{2,0},{3,1},{4,6},{5,7},{6,4},{7,5},{8,10},{9,11},{10,... | collective-permute-start | bytes 1572872 | tf_op jit(solution)/shard_map/ppermute | solution.py:223
  53.5 24.5 %copy-start.4 = (f32[512,256]{1,0:T(8,128)}, f32[512,256]{1,0:T(8,128)S(1)}, u32[]{:S(2)}) copy-start(f32[512,256]{1,0:T(8,128)S(1)} %collective-permute-done.3.refs_7_) | copy-start | bytes 1572868
  61.9 11.1 %collective-permute-start.6 = (f32[512,256]{1,0:T(8,128)S(1)}, f32[512,256]{1,0:T(8,128)S(1)}, u32[]{:S(2)}, u32[]{:S(2)}) collective-permute-start(f32[512,256]{1,0:T(8,128)S(1)} %collective-permute-done.3.refs_7_), channel_id=1, source_target_pairs={{0,4},{1,5},{2,6},{3,7},{8,12},{9,13},{10,14},{11,15},{16,20},{17,... | collective-permute-start | bytes 1572872 | tf_op jit(solution)/shard_map/ppermute | solution.py:322
  66.4 11.6 %copy-start.6 = (f32[512,256]{1,0:T(8,128)}, f32[512,256]{1,0:T(8,128)S(1)}, u32[]{:S(2)}) copy-start(f32[512,256]{1,0:T(8,128)S(1)} %broadcast_select_fusion.1.refs_10_) | copy-start | bytes 1572868
  66.4 9.8 %copy-start.10 = (f32[512,256]{1,0:T(8,128)}, f32[512,256]{1,0:T(8,128)S(1)}, u32[]{:S(2)}) copy-start(f32[512,256]{1,0:T(8,128)S(1)} %collective-permute-done.12.refs_7_) | copy-start | bytes 1572868
  66.4 9.2 %collective-permute-start.13 = (f32[512,256]{1,0:T(8,128)S(1)}, f32[512,256]{1,0:T(8,128)S(1)}, u32[]{:S(2)}, u32[]{:S(2)}) collective-permute-start(f32[512,256]{1,0:T(8,128)S(1)} %broadcast_select_fusion.1.refs_10_), channel_id=1, source_target_pairs={{0,2},{1,3},{2,0},{3,1},{4,6},{5,7},{6,4},{7,5},{8,10},{9,11},{10,... | collective-permute-start | bytes 1572872 | tf_op jit(solution)/shard_map/ppermute | solution.py:223
  66.5 10.9 %collective-permute-start.7 = (f32[512,256]{1,0:T(8,128)S(1)}, f32[512,256]{1,0:T(8,128)}, u32[]{:S(2)}, u32[]{:S(2)}) collective-permute-start(f32[512,256]{1,0:T(8,128)S(1)} %broadcast_select_fusion.3.refs_8_), channel_id=1, source_target_pairs={{0,1},{1,0},{2,3},{3,2},{4,5},{5,4},{6,7},{7,6},{8,9},{9,8},{10,11... | collective-permute-start | bytes 1572872 | tf_op jit(solution)/shard_map/ppermute | solution.py:223
  66.6 10.8 %collective-permute-start.8 = (f32[512,256]{1,0:T(8,128)S(1)}, f32[512,256]{1,0:T(8,128)}, u32[]{:S(2)}, u32[]{:S(2)}) collective-permute-start(f32[512,256]{1,0:T(8,128)S(1)} %broadcast_select_fusion.2.refs_9_), channel_id=1, source_target_pairs={{0,1},{1,0},{2,3},{3,2},{4,5},{5,4},{6,7},{7,6},{8,9},{9,8},{10,11... | collective-permute-start | bytes 1572872 | tf_op jit(solution)/shard_map/ppermute | solution.py:223
  67.1 10.8 %collective-permute-start.9 = (f32[512,256]{1,0:T(8,128)S(1)}, f32[512,256]{1,0:T(8,128)}, u32[]{:S(2)}, u32[]{:S(2)}) collective-permute-start(f32[512,256]{1,0:T(8,128)S(1)} %broadcast_select_fusion.1.refs_10_), channel_id=1, source_target_pairs={{0,1},{1,0},{2,3},{3,2},{4,5},{5,4},{6,7},{7,6},{8,9},{9,8},{10,11... | collective-permute-start | bytes 1572872 | tf_op jit(solution)/shard_map/ppermute | solution.py:223
  73.1 4.9 %copy-start.7 = (f32[512,256]{1,0:T(8,128)}, f32[512,256]{1,0:T(8,128)S(1)}, u32[]{:S(2)}) copy-start(f32[512,256]{1,0:T(8,128)S(1)} %broadcast_select_fusion.refs_11_) | copy-start | bytes 1572868
  73.1 4.9 %collective-permute-start.10 = (f32[512,256]{1,0:T(8,128)S(1)}, f32[512,256]{1,0:T(8,128)}, u32[]{:S(2)}, u32[]{:S(2)}) collective-permute-start(f32[512,256]{1,0:T(8,128)S(1)} %broadcast_select_fusion.refs_11_), channel_id=1, source_target_pairs={{0,1},{1,0},{2,3},{3,2},{4,5},{5,4},{6,7},{7,6},{8,9},{9,8},{10,11... | collective-permute-start | bytes 1572872 | tf_op jit(solution)/shard_map/ppermute | solution.py:223
  75.7 0.8 copy-start.11
  75.7 15.7 %collective-permute-start.14 = (f32[512,256]{1,0:T(8,128)S(1)}, f32[512,256]{1,0:T(8,128)S(1)}, u32[]{:S(2)}, u32[]{:S(2)}) collective-permute-start(f32[512,256]{1,0:T(8,128)S(1)} %broadcast_select_fusion.refs_11_), channel_id=1, source_target_pairs={{0,2},{1,3},{2,0},{3,1},{4,6},{5,7},{6,4},{7,5},{8,10},{9,11},{10,... | collective-permute-start | bytes 1572872 | tf_op jit(solution)/shard_map/ppermute | solution.py:223
  77.4 14.5 %collective-permute-start.15 = (f32[512,256]{1,0:T(8,128)}, f32[512,256]{1,0:T(8,128)S(1)}, u32[]{:S(2)}, u32[]{:S(2)}) collective-permute-start(f32[512,256]{1,0:T(8,128)} %copy-done.9), channel_id=1, source_target_pairs={{0,1},{1,0},{2,3},{3,2},{4,5},{5,4},{6,7},{7,6},{8,9},{9,8},{10,11... | collective-permute-start | bytes 1572872 | tf_op jit(solution)/shard_map/ppermute | solution.py:223
  77.4 14.5 %collective-permute-start.16 = (f32[512,256]{1,0:T(8,128)}, f32[512,256]{1,0:T(8,128)}, u32[]{:S(2)}, u32[]{:S(2)}) collective-permute-start(f32[512,256]{1,0:T(8,128)} %copy-done.10), channel_id=1, source_target_pairs={{0,1},{1,0},{2,3},{3,2},{4,5},{5,4},{6,7},{7,6},{8,9},{9,8},{10,11... | collective-permute-start | bytes 1572872 | tf_op jit(solution)/shard_map/ppermute | solution.py:223
  77.9 14.0 %collective-permute-start.17 = (f32[512,256]{1,0:T(8,128)}, f32[512,256]{1,0:T(8,128)}, u32[]{:S(2)}, u32[]{:S(2)}) collective-permute-start(f32[512,256]{1,0:T(8,128)} %copy-done.11), channel_id=1, source_target_pairs={{0,1},{1,0},{2,3},{3,2},{4,5},{5,4},{6,7},{7,6},{8,9},{9,8},{10,11... | collective-permute-start | bytes 1572872 | tf_op jit(solution)/shard_map/ppermute | solution.py:223
  91.4 2.1 %copy-start.12 = (f32[512,256]{1,0:T(8,128)}, f32[512,256]{1,0:T(8,128)S(1)}, u32[]{:S(2)}) copy-start(f32[512,256]{1,0:T(8,128)S(1)} %collective-permute-done.14.refs_9_) | copy-start | bytes 1572868
  91.4 2.0 %collective-permute-start.18 = (f32[512,256]{1,0:T(8,128)S(1)}, f32[512,256]{1,0:T(8,128)S(1)}, u32[]{:S(2)}, u32[]{:S(2)}) collective-permute-start(f32[512,256]{1,0:T(8,128)S(1)} %collective-permute-done.14.refs_9_), channel_id=1, source_target_pairs={{0,1},{1,0},{2,3},{3,2},{4,5},{5,4},{6,7},{7,6},{8,9},{9,8},{10,11... | collective-permute-start | bytes 1572872 | tf_op jit(solution)/shard_map/ppermute | solution.py:223
  91.9 1.5 copy-start.13
  93.5 0.8 copy-start.14
  108.8 25.5 %copy-start.20 = (f32[128,256]{1,0:T(8,128)S(1)}, f32[128,256]{1,0:T(8,128)}, u32[]{:S(2)}) copy-start(f32[128,256]{1,0:T(8,128)} %get-tuple-element.49) | copy-start | bytes 393220
  110.0 3.5 %collective-permute-start.20 = (f32[256,512]{1,0:T(8,128)S(1)}, f32[256,512]{1,0:T(8,128)S(1)}, u32[]{:S(2)}, u32[]{:S(2)}) collective-permute-start(f32[256,512]{1,0:T(8,128)S(1)} %constant_dynamic-slice_fusion.3), channel_id=1, source_target_pairs={{0,1},{1,0},{2,3},{3,2},{4,5},{5,4},{6,7},{7,6},{8,9},{9,8},{10,11... | collective-permute-start | bytes 1572872 | tf_op jit(solution)/shard_map/ppermute | solution.py:223
  110.4 22.6 %collective-permute-start.25 = (f32[512,256]{1,0:T(8,128)}, f32[512,256]{1,0:T(8,128)S(1)}, u32[]{:S(2)}, u32[]{:S(2)}) collective-permute-start(f32[512,256]{1,0:T(8,128)} %get-tuple-element.51), channel_id=1, source_target_pairs={{0,8},{8,0},{16,24},{24,16},{1,9},{9,1},{17,25},{25,17},{2,10},{10... | collective-permute-start | bytes 1572872 | tf_op jit(solution)/shard_map/ppermute | solution.py:223
  110.4 20.5 %collective-permute-start.19 = (f32[384,256]{1,0:T(8,128)}, f32[384,256]{1,0:T(8,128)S(1)}, u32[]{:S(2)}, u32[]{:S(2)}) collective-permute-start(f32[384,256]{1,0:T(8,128)} %get-tuple-element.46), channel_id=1, source_target_pairs={{0,16},{8,24},{16,0},{24,8},{1,17},{9,25},{17,1},{25,9},{2,18},{10... | collective-permute-start | bytes 1179656 | tf_op jit(solution)/shard_map/ppermute | solution.py:223
  114.6 28.7 %copy-start.19 = (f32[512,256]{1,0:T(8,128)S(1)}, f32[512,256]{1,0:T(8,128)}, u32[]{:S(2)}) copy-start(f32[512,256]{1,0:T(8,128)} %get-tuple-element.54) | copy-start | bytes 1572868
  114.6 5.8 %collective-permute-start.21 = (f32[64,512]{1,0:T(8,128)S(1)}, f32[64,512]{1,0:T(8,128)S(1)}, u32[]{:S(2)}, u32[]{:S(2)}) collective-permute-start(f32[64,512]{1,0:T(8,128)S(1)} %get-tuple-element.64), channel_id=1, source_target_pairs={{0,2},{1,3},{2,0},{3,1},{4,6},{5,7},{6,4},{7,5},{8,10},{9,11},{10,... | collective-permute-start | bytes 393224 | tf_op jit(solution)/shard_map/ppermute | solution.py:223
  115.9 7.5 %collective-permute-start.22 = (f32[64,512]{1,0:T(8,128)S(1)}, f32[64,512]{1,0:T(8,128)S(1)}, u32[]{:S(2)}, u32[]{:S(2)}) collective-permute-start(f32[64,512]{1,0:T(8,128)S(1)} %get-tuple-element.66), channel_id=1, source_target_pairs={{0,4},{1,5},{2,6},{3,7},{4,0},{5,1},{6,2},{7,3},{8,12},{9,13},{10,... | collective-permute-start | bytes 393224 | tf_op jit(solution)/shard_map/ppermute | solution.py:223
  115.9 7.5 %collective-permute-start.23 = (f32[64,512]{1,0:T(8,128)S(1)}, f32[64,512]{1,0:T(8,128)S(1)}, u32[]{:S(2)}, u32[]{:S(2)}) collective-permute-start(f32[64,512]{1,0:T(8,128)S(1)} %get-tuple-element.65), channel_id=1, source_target_pairs={{0,6},{1,7},{2,4},{3,5},{4,2},{5,3},{6,0},{7,1},{8,14},{9,15},{10,... | collective-permute-start | bytes 393224 | tf_op jit(solution)/shard_map/ppermute | solution.py:223
  133.0 5.9 %collective-permute-start.26 = (f32[64,512]{1,0:T(8,128)S(1)}, f32[64,512]{1,0:T(8,128)S(1)}, u32[]{:S(2)}, u32[]{:S(2)}) collective-permute-start(f32[64,512]{1,0:T(8,128)S(1)} %add_add_fusion), channel_id=1, source_target_pairs={{0,8},{8,0},{16,24},{24,16},{1,9},{9,1},{17,25},{25,17},{2,10},{10... | collective-permute-start | bytes 393224 | tf_op jit(solution)/shard_map/ppermute | solution.py:223
  134.3 8.5 %collective-permute-start.24 = (f32[128,256]{1,0:T(8,128)S(1)}, f32[128,256]{1,0:T(8,128)S(1)}, u32[]{:S(2)}, u32[]{:S(2)}) collective-permute-start(f32[128,256]{1,0:T(8,128)S(1)} %copy-done.20), channel_id=1, source_target_pairs={{0,16},{8,24},{16,0},{24,8},{1,17},{9,25},{17,1},{25,9},{2,18},{10... | collective-permute-start | bytes 393224 | tf_op jit(solution)/shard_map/ppermute | solution.py:223
  142.8 18.9 %collective-permute-start.28 = (f32[64,512]{1,0:T(8,128)S(1)}, f32[64,512]{1,0:T(8,128)S(1)}, u32[]{:S(2)}, u32[]{:S(2)}) collective-permute-start(f32[64,512]{1,0:T(8,128)S(1)} %add.176), channel_id=1, source_target_pairs={{0,16},{8,24},{16,0},{24,8},{1,17},{9,25},{17,1},{25,9},{2,18},{10... | collective-permute-start | bytes 393224 | tf_op jit(solution)/shard_map/ppermute | solution.py:223
  143.4 26.5 %copy-start.15 = (f32[512,256]{1,0:T(8,128)S(1)}, f32[512,256]{1,0:T(8,128)}, u32[]{:S(2)}) copy-start(f32[512,256]{1,0:T(8,128)} %get-tuple-element.55) | copy-start | bytes 1572868
  143.4 26.4 %collective-permute-start.27 = (f32[512,256]{1,0:T(8,128)S(1)}, f32[512,256]{1,0:T(8,128)S(1)}, u32[]{:S(2)}, u32[]{:S(2)}) collective-permute-start(f32[512,256]{1,0:T(8,128)S(1)} %copy-done.19), channel_id=1, source_target_pairs={{0,24},{8,16},{16,8},{24,0},{1,25},{9,17},{17,9},{25,1},{2,26},{10... | collective-permute-start | bytes 1572872 | tf_op jit(solution)/shard_map/ppermute | solution.py:223
  161.7 6.2 %collective-permute-start.29 = (f32[64,512]{1,0:T(8,128)S(1)}, f32[64,512]{1,0:T(8,128)S(1)}, u32[]{:S(2)}, u32[]{:S(2)}) collective-permute-start(f32[64,512]{1,0:T(8,128)S(1)} %add.179), channel_id=1, source_target_pairs={{0,2},{1,3},{2,0},{3,1},{4,6},{5,7},{6,4},{7,5},{8,10},{9,11},{10,... | collective-permute-start | bytes 393224 | tf_op jit(solution)/shard_map/ppermute | solution.py:223
  162.9 6.7 %collective-permute-start.30 = (f32[64,512]{1,0:T(8,128)S(1)}, f32[64,512]{1,0:T(8,128)S(1)}, u32[]{:S(2)}, u32[]{:S(2)}) collective-permute-start(f32[64,512]{1,0:T(8,128)S(1)} %add.179), channel_id=1, source_target_pairs={{0,4},{1,5},{2,6},{3,7},{4,0},{5,1},{6,2},{7,3},{8,12},{9,13},{10,... | collective-permute-start | bytes 393224 | tf_op jit(solution)/shard_map/ppermute | solution.py:223
  163.1 6.6 %collective-permute-start.31 = (f32[64,512]{1,0:T(8,128)S(1)}, f32[64,512]{1,0:T(8,128)S(1)}, u32[]{:S(2)}, u32[]{:S(2)}) collective-permute-start(f32[64,512]{1,0:T(8,128)S(1)} %add.179), channel_id=1, source_target_pairs={{0,6},{1,7},{2,4},{3,5},{4,2},{5,3},{6,0},{7,1},{8,14},{9,15},{10,... | collective-permute-start | bytes 393224 | tf_op jit(solution)/shard_map/ppermute | solution.py:223
  169.7 2.0 %collective-permute-start.32 = (f32[256,512]{1,0:T(8,128)S(1)}, f32[256,512]{1,0:T(8,128)S(1)}, u32[]{:S(2)}, u32[]{:S(2)}) collective-permute-start(f32[256,512]{1,0:T(8,128)S(1)} %maximum_select_fusion.1), channel_id=1, source_target_pairs={{0,1},{1,0},{2,3},{3,2},{4,5},{5,4},{6,7},{7,6},{8,9},{9,8},{10,11... | collective-permute-start | bytes 1572872 | tf_op jit(solution)/shard_map/ppermute | solution.py:223
  170.0 2.8 %copy-start.8 = (f32[4,512,256]{2,1,0:T(8,128)}, f32[4,512,256]{2,1,0:T(8,128)S(1)}, u32[]{:S(2)}) copy-start(f32[4,512,256]{2,1,0:T(8,128)S(1)} %bitcast_dynamic-update-slice_fusion) | copy-start | bytes 6291460

commit v5 on v3

--- a/solution.py
+++ b/solution.py
@@ -305,8 +305,6 @@
         rows = rows[first : first + count]
         if part == row_count - 1:
             rows = after(rows, near[0])
-        elif part > 1:
-            rows = after(rows, scalars[1])
         own.append(exchange(rows, "row", part) if part else rows)
 
     for at in range(len(cuts)):

time: 171 us -> 169 us (0.988)
  waiting for transfers between devices: 77.2 us -> 71 us
  starting transfers between devices: 39.8 us -> 44.6 us
    ppermute x29, waiting for transfers between devices: 63 us -> 51 us  [exchange(): return lax.ppermute(value, axis, [(at, at ^ bit) for at in range(size)])]
    ppermute x4, waiting for transfers between devices: 14.3 us -> 20 us  [on_device(): got = lax.ppermute(rows, 'col', links)]
    ppermute x4, starting transfers between devices: 12.2 us -> 15.3 us  [on_device(): got = lax.ppermute(rows, 'col', links)]
    ppermute x29, starting transfers between devices: 27.6 us -> 29.4 us  [exchange(): return lax.ppermute(value, axis, [(at, at ^ bit) for at in range(size)])]
where the time goes in v5:
time: 169 us
  waiting for transfers between devices  71 us (42%)
  starting transfers between devices  44.6 us (26%)
  Pallas kernels  27.9 us (17%)
  local copies, waits for them, and re-layouts  11.1 us (7%)
  between operations  8.63 us (5%)
  other arithmetic  5.44 us (3%)
    ppermute x29, waiting for transfers between devices, exchange(): return lax.ppermute(value, axis, [(at, at ^ bit) for at in range(size)])  51 us
    ppermute x29, starting transfers between devices, exchange(): return lax.ppermute(value, axis, [(at, at ^ bit) for at in range(size)])  29.4 us
    pallas_call x2, Pallas kernels, call(): pl.pallas_call(functools.partial(staged, kernel, len(small), len(big), le...  27.9 us
    ppermute x4, waiting for transfers between devices, on_device(): got = lax.ppermute(rows, 'col', links)  20 us
    ppermute x4, starting transfers between devices, on_device(): got = lax.ppermute(rows, 'col', links)  15.3 us
  transfers between devices with their start and end apart: 33, of which 16 were waited for; matrix products, arithmetic and copies ran while one was open for 6% of the time, Pallas kernels for 8%

profile of v5, /device:TPU:0, one launch (start us, length us, event | category | flops | bytes accessed | tf_op | source)
XLA Modules:
  0.0 168.8 jit_solution(5699472615108042816)
XLA Ops:
  0.7 2.7 %dynamic-slice_bitcast_fusion = (f32[512,256]{1,0:T(8,128)}, f32[512,256]{1,0:T(8,128)S(1)}, f32[512,256]{1,0:T(8,128)S(1)}, f32[512,256]{1,0:T(8,128)}) fusion(f32[4,512,256]{2,1,0:T(8,128)} %param.5, s32[]{:T(128)S(6)} %select_n.171, s32[]{:T(128)S(6)} %select_n.169, s32[]{:T(128)S(6)} %select_n.163, s32[]{:T(128)S(6)} %select_n.170), kind=kLoop, calls=%fused_computation.8 | loop fusion | bytes 4194320 | tf_op jit(solution)/shard_map/jit(dynamic_index_in_dim)/squeeze | solution.py:304
  3.4 4.9 %collective-permute-start.2 = (f32[512,256]{1,0:T(8,128)S(1)}, f32[512,256]{1,0:T(8,128)S(1)}, u32[]{:S(2)}, u32[]{:S(2)}) collective-permute-start(f32[512,256]{1,0:T(8,128)S(1)} %get-tuple-element.66.refs_4_), channel_id=1, source_target_pairs={{0,4},{1,5},{2,6},{3,7},{8,12},{9,13},{10,14},{11,15},{16,20},{17,... | collective-permute-start | bytes 1572872 | tf_op jit(solution)/shard_map/ppermute | solution.py:320
  8.3 1.6 collective-permute-start
  9.9 2.6 %collective-permute-start.1 = (f32[512,256]{1,0:T(8,128)}, f32[512,256]{1,0:T(8,128)S(1)}, u32[]{:S(2)}, u32[]{:S(2)}) collective-permute-start(f32[512,256]{1,0:T(8,128)} %get-tuple-element.67), channel_id=1, source_target_pairs={{0,16},{8,24},{16,0},{24,8},{1,17},{9,25},{17,1},{25,9},{2,18},{10... | collective-permute-start | bytes 1572872 | tf_op jit(solution)/shard_map/ppermute | solution.py:223
  12.5 0.1 stack.62
  12.6 0.1 copy.12
  12.8 0.6 gather_fusion
  13.4 0.6 gather_fusion.1
  14.1 0.7 fusion.2
  17.2 1.4 compare_reduce_fusion.1
  23.7 0.1 broadcast_in_dim.35
  23.8 0.8 slice.25.refs_3_
  24.8 0.7 slice.22.refs_3_
  25.5 0.6 pad_maximum_fusion.1.refs_0_
  26.1 0.6 pad_maximum_fusion.refs_0_
  26.7 6.0 %collective-permute-done.refs_5_ = f32[512,256]{1,0:T(8,128)S(1)} collective-permute-done((f32[512,256]{1,0:T(8,128)S(1)}, f32[512,256]{1,0:T(8,128)S(1)}, u32[]{:S(2)}, u32[]{:S(2)}) %collective-permute-start) | collective-permute-done | bytes 524320 | tf_op jit(solution)/shard_map/ppermute | solution.py:223
  32.6 1.6 collective-permute-start.4
  34.3 1.6 collective-permute-start.11
  35.9 2.5 %collective-permute-start.3 = (f32[512,256]{1,0:T(8,128)}, f32[512,256]{1,0:T(8,128)S(1)}, u32[]{:S(2)}, u32[]{:S(2)}) collective-permute-start(f32[512,256]{1,0:T(8,128)} %get-tuple-element.33), channel_id=1, source_target_pairs={{0,24},{8,16},{16,8},{24,0},{1,25},{9,17},{17,9},{25,1},{2,26},{10... | collective-permute-start | bytes 1572872 | tf_op jit(solution)/shard_map/ppermute | solution.py:223
  38.3 6.1 %collective-permute-done.4 = f32[512,256]{1,0:T(8,128)S(1)} collective-permute-done((f32[512,256]{1,0:T(8,128)S(1)}, f32[512,256]{1,0:T(8,128)S(1)}, u32[]{:S(2)}, u32[]{:S(2)}) %collective-permute-start.4) | collective-permute-done | bytes 524320 | tf_op jit(solution)/shard_map/ppermute | solution.py:320
  44.5 4.4 %collective-permute-start.5 = (f32[512,256]{1,0:T(8,128)S(1)}, f32[512,256]{1,0:T(8,128)S(1)}, u32[]{:S(2)}, u32[]{:S(2)}) collective-permute-start(f32[512,256]{1,0:T(8,128)S(1)} %collective-permute-done.1.refs_6_), channel_id=1, source_target_pairs={{0,4},{1,5},{2,6},{3,7},{8,12},{9,13},{10,14},{11,15},{16,20},{17,... | collective-permute-start | bytes 1572872 | tf_op jit(solution)/shard_map/ppermute | solution.py:320
  49.0 1.6 collective-permute-start.12
  50.6 7.7 %collective-permute-done.5 = f32[512,256]{1,0:T(8,128)S(1)} collective-permute-done((f32[512,256]{1,0:T(8,128)S(1)}, f32[512,256]{1,0:T(8,128)S(1)}, u32[]{:S(2)}, u32[]{:S(2)}) %collective-permute-start.5) | collective-permute-done | bytes 524320 | tf_op jit(solution)/shard_map/ppermute | solution.py:320
  58.2 4.4 %collective-permute-start.6 = (f32[512,256]{1,0:T(8,128)S(1)}, f32[512,256]{1,0:T(8,128)S(1)}, u32[]{:S(2)}, u32[]{:S(2)}) collective-permute-start(f32[512,256]{1,0:T(8,128)S(1)} %collective-permute-done.3.refs_7_), channel_id=1, source_target_pairs={{0,4},{1,5},{2,6},{3,7},{8,12},{9,13},{10,14},{11,15},{16,20},{17,... | collective-permute-start | bytes 1572872 | tf_op jit(solution)/shard_map/ppermute | solution.py:320
  62.8 1.6 collective-permute-start.13
  64.3 0.5 collective-permute-start.8
  64.8 6.2 %collective-permute-done.6 = f32[512,256]{1,0:T(8,128)S(1)} collective-permute-done((f32[512,256]{1,0:T(8,128)S(1)}, f32[512,256]{1,0:T(8,128)S(1)}, u32[]{:S(2)}, u32[]{:S(2)}) %collective-permute-start.6) | collective-permute-done | bytes 524320 | tf_op jit(solution)/shard_map/ppermute | solution.py:320
  71.2 2.3 %collective-permute-done.13.refs_8_ = f32[512,256]{1,0:T(8,128)S(1)} collective-permute-done((f32[512,256]{1,0:T(8,128)S(1)}, f32[512,256]{1,0:T(8,128)S(1)}, u32[]{:S(2)}, u32[]{:S(2)}) %collective-permute-start.13) | collective-permute-done | bytes 524320 | tf_op jit(solution)/shard_map/ppermute | solution.py:223
  73.5 0.8 copy-done.11
  74.3 1.5 collective-permute-start.14
  75.8 0.9 copy.19.refs_1_
  76.7 0.5 collective-permute-start.16
  77.3 13.4 %early.1 = (bf16[512,1024]{1,0:T(8,128)(2,1)}, bf16[512,1024]{1,0:T(8,128)(2,1)}, f32[512,512]{1,0:T(8,128)}, f32[512,256]{1,0:T(8,128)}, f32[512,256]{1,0:T(8,1...) custom-call(f32[4]{0:T(128)} %pad_maximum_fusion.1.refs_0_, f32[512,1]{1,0:T(8,128)} %copy.19.refs_1_, f32[1,512]{1,0:T(1,128)} %bitcast.45, ...), custom_call_target="tpu_custom_call" | custom-call | tf_op jit(solution)/shard_map/early/pallas_call | solution.py:41
  90.7 0.5 collective-permute-start.18
  91.2 1.5 collective-permute-done.18.refs_13_
  92.8 0.8 copy-done.14
  93.6 14.5 %late.1 = (f32[512,512]{1,0:T(8,128)}, f32[384,256]{1,0:T(8,128)}, f32[128,256]{1,0:T(8,128)}, f32[512,256]{1,0:T(8,128)}, f32[512,256]{1,0:T(8,128)}, /*index=5*/f32[512,256]{1,0:T(8,128)}) custom-call(f32[4]{0:T(128)} %pad_maximum_fusion.refs_0_, f32[512,1]{1,0:T(8,128)} %copy.19.refs_1_, f32[1,512]{1,0:T(1,128)} %bitcast.46, ...), custom_call_target="tpu_custom_call" | custom-call | tf_op jit(solution)/shard_map/late/pallas_call | solution.py:41
  108.1 1.1 constant_dynamic-slice_fusion.3
  109.3 0.4 collective-permute-start.20
  109.7 0.5 collective-permute-start.19
  110.3 1.0 collective-permute-done.20
  111.3 1.1 dynamic-slice_add_fusion
  112.4 0.6 collective-permute-start.21
  113.0 0.3 collective-permute-start.22
  113.4 2.6 %collective-permute-start.23 = (f32[64,512]{1,0:T(8,128)S(1)}, f32[64,512]{1,0:T(8,128)S(1)}, u32[]{:S(2)}, u32[]{:S(2)}) collective-permute-start(f32[64,512]{1,0:T(8,128)S(1)} %get-tuple-element.69), channel_id=1, source_target_pairs={{0,6},{1,7},{2,4},{3,5},{4,2},{5,3},{6,0},{7,1},{8,14},{9,15},{10,... | collective-permute-start | bytes 393224 | tf_op jit(solution)/shard_map/ppermute | solution.py:223
  116.0 2.8 %collective-permute-done.21 = f32[64,512]{1,0:T(8,128)S(1)} collective-permute-done((f32[64,512]{1,0:T(8,128)S(1)}, f32[64,512]{1,0:T(8,128)S(1)}, u32[]{:S(2)}, u32[]{:S(2)}) %collective-permute-start.21) | collective-permute-done | bytes 131104 | tf_op jit(solution)/shard_map/ppermute | solution.py:223
  118.8 2.5 %collective-permute-done.22 = f32[64,512]{1,0:T(8,128)S(1)} collective-permute-done((f32[64,512]{1,0:T(8,128)S(1)}, f32[64,512]{1,0:T(8,128)S(1)}, u32[]{:S(2)}, u32[]{:S(2)}) %collective-permute-start.22) | collective-permute-done | bytes 131104 | tf_op jit(solution)/shard_map/ppermute | solution.py:223
  121.4 8.8 %collective-permute-done.19 = f32[384,256]{1,0:T(8,128)S(1)} collective-permute-done((f32[384,256]{1,0:T(8,128)}, f32[384,256]{1,0:T(8,128)S(1)}, u32[]{:S(2)}, u32[]{:S(2)}) %collective-permute-start.19) | collective-permute-done | bytes 393248 | tf_op jit(solution)/shard_map/ppermute | solution.py:223
  130.2 2.2 %collective-permute-start.24 = (f32[128,256]{1,0:T(8,128)S(1)}, f32[128,256]{1,0:T(8,128)S(1)}, u32[]{:S(2)}, u32[]{:S(2)}) collective-permute-start(f32[128,256]{1,0:T(8,128)S(1)} %copy-done.21), channel_id=1, source_target_pairs={{0,16},{8,24},{16,0},{24,8},{1,17},{9,25},{17,1},{25,9},{2,18},{10... | collective-permute-start | bytes 393224 | tf_op jit(solution)/shard_map/ppermute | solution.py:223
  132.4 5.1 %collective-permute-done.25 = f32[64,512]{1,0:T(8,128)S(1)} collective-permute-done((f32[64,512]{1,0:T(8,128)S(1)}, f32[64,512]{1,0:T(8,128)S(1)}, u32[]{:S(2)}, u32[]{:S(2)}) %collective-permute-start.25) | collective-permute-done | bytes 131104 | tf_op jit(solution)/shard_map/ppermute | solution.py:223
  137.5 1.9 %collective-permute-done.24 = f32[128,256]{1,0:T(8,128)S(1)} collective-permute-done((f32[128,256]{1,0:T(8,128)S(1)}, f32[128,256]{1,0:T(8,128)S(1)}, u32[]{:S(2)}, u32[]{:S(2)}) %collective-permute-start.24) | collective-permute-done | bytes 131104 | tf_op jit(solution)/shard_map/ppermute | solution.py:223
  139.4 0.3 collective-permute-start.28
  139.8 0.2 broadcast_in_dim.31
  140.0 1.9 %collective-permute-start.27 = (f32[512,256]{1,0:T(8,128)S(1)}, f32[512,256]{1,0:T(8,128)S(1)}, u32[]{:S(2)}, u32[]{:S(2)}) collective-permute-start(f32[512,256]{1,0:T(8,128)S(1)} %copy-done.19), channel_id=1, source_target_pairs={{0,8},{8,0},{16,24},{24,16},{1,9},{9,1},{17,25},{25,17},{2,10},{10... | collective-permute-start | bytes 1572872 | tf_op jit(solution)/shard_map/ppermute | solution.py:223
  141.9 2.2 %collective-permute-start.26 = (f32[512,256]{1,0:T(8,128)S(1)}, f32[512,256]{1,0:T(8,128)S(1)}, u32[]{:S(2)}, u32[]{:S(2)}) collective-permute-start(f32[512,256]{1,0:T(8,128)S(1)} %copy-done.20), channel_id=1, source_target_pairs={{0,24},{8,16},{16,8},{24,0},{1,25},{9,17},{17,9},{25,1},{2,26},{10... | collective-permute-start | bytes 1572872 | tf_op jit(solution)/shard_map/ppermute | solution.py:223
  144.1 3.2 %collective-permute-done.28 = f32[64,512]{1,0:T(8,128)S(1)} collective-permute-done((f32[64,512]{1,0:T(8,128)S(1)}, f32[64,512]{1,0:T(8,128)S(1)}, u32[]{:S(2)}, u32[]{:S(2)}) %collective-permute-start.28) | collective-permute-done | bytes 131104 | tf_op jit(solution)/shard_map/ppermute | solution.py:223
  147.3 0.6 collective-permute-start.29
  147.9 0.3 collective-permute-start.30
  148.3 2.6 %collective-permute-start.31 = (f32[64,512]{1,0:T(8,128)S(1)}, f32[64,512]{1,0:T(8,128)S(1)}, u32[]{:S(2)}, u32[]{:S(2)}) collective-permute-start(f32[64,512]{1,0:T(8,128)S(1)} %add.179), channel_id=1, source_target_pairs={{0,6},{1,7},{2,4},{3,5},{4,2},{5,3},{6,0},{7,1},{8,14},{9,15},{10,... | collective-permute-start | bytes 393224 | tf_op jit(solution)/shard_map/ppermute | solution.py:223
  150.9 2.9 %collective-permute-done.29 = f32[64,512]{1,0:T(8,128)S(1)} collective-permute-done((f32[64,512]{1,0:T(8,128)S(1)}, f32[64,512]{1,0:T(8,128)S(1)}, u32[]{:S(2)}, u32[]{:S(2)}) %collective-permute-start.29) | collective-permute-done | bytes 131104 | tf_op jit(solution)/shard_map/ppermute | solution.py:223
  153.8 1.6 collective-permute-done.30
  155.6 11.4 %collective-permute-done.26 = f32[512,256]{1,0:T(8,128)S(1)} collective-permute-done((f32[512,256]{1,0:T(8,128)S(1)}, f32[512,256]{1,0:T(8,128)S(1)}, u32[]{:S(2)}, u32[]{:S(2)}) %collective-permute-start.26) | collective-permute-done | bytes 524320 | tf_op jit(solution)/shard_map/ppermute | solution.py:223
  167.2 1.2 maximum_select_fusion
  168.4 0.4 copy-done.8
  (94 shorter events, 1.4 us)
Async XLA Ops:
  0.7 12.0 %copy-start.16 = (s32[32,8,16]{0,2,1:T(8,128)S(1)}, s32[32,8,16]{0,2,1:T(8,128)}, u32[]{:S(2)}) copy-start(s32[32,8,16]{0,2,1:T(8,128)} %param.8) | copy-start | bytes 49156
  0.7 13.4 %copy-start.18 = (f32[32]{0:T(128)S(1)}, f32[32]{0:T(128)}, u32[]{:S(2)}) copy-start(f32[32]{0:T(128)} %param.6) | copy-start | bytes 388
  3.4 45.6 %copy-start = (f32[512,256]{1,0:T(8,128)}, f32[512,256]{1,0:T(8,128)S(1)}, u32[]{:S(2)}) copy-start(f32[512,256]{1,0:T(8,128)S(1)} %get-tuple-element.66.refs_4_) | copy-start | bytes 1572868
  3.4 23.3 %collective-permute-start.2 = (f32[512,256]{1,0:T(8,128)S(1)}, f32[512,256]{1,0:T(8,128)S(1)}, u32[]{:S(2)}, u32[]{:S(2)}) collective-permute-start(f32[512,256]{1,0:T(8,128)S(1)} %get-tuple-element.66.refs_4_), channel_id=1, source_target_pairs={{0,4},{1,5},{2,6},{3,7},{8,12},{9,13},{10,14},{11,15},{16,20},{17,... | collective-permute-start | bytes 1572872 | tf_op jit(solution)/shard_map/ppermute | solution.py:320
  8.3 24.4 %collective-permute-start = (f32[512,256]{1,0:T(8,128)S(1)}, f32[512,256]{1,0:T(8,128)S(1)}, u32[]{:S(2)}, u32[]{:S(2)}) collective-permute-start(f32[512,256]{1,0:T(8,128)S(1)} %get-tuple-element.65), channel_id=1, source_target_pairs={{0,8},{8,0},{16,24},{24,16},{1,9},{9,1},{17,25},{25,17},{2,10},{10... | collective-permute-start | bytes 1572872 | tf_op jit(solution)/shard_map/ppermute | solution.py:223
  9.9 28.4 %collective-permute-start.1 = (f32[512,256]{1,0:T(8,128)}, f32[512,256]{1,0:T(8,128)S(1)}, u32[]{:S(2)}, u32[]{:S(2)}) collective-permute-start(f32[512,256]{1,0:T(8,128)} %get-tuple-element.67), channel_id=1, source_target_pairs={{0,16},{8,24},{16,0},{24,8},{1,17},{9,25},{17,1},{25,9},{2,18},{10... | collective-permute-start | bytes 1572872 | tf_op jit(solution)/shard_map/ppermute | solution.py:223
  32.6 30.1 %copy-start.1 = (f32[512,256]{1,0:T(8,128)}, f32[512,256]{1,0:T(8,128)S(1)}, u32[]{:S(2)}) copy-start(f32[512,256]{1,0:T(8,128)S(1)} %collective-permute-done.refs_5_) | copy-start | bytes 1572868
  32.6 11.8 %collective-permute-start.4 = (f32[512,256]{1,0:T(8,128)S(1)}, f32[512,256]{1,0:T(8,128)S(1)}, u32[]{:S(2)}, u32[]{:S(2)}) collective-permute-start(f32[512,256]{1,0:T(8,128)S(1)} %collective-permute-done.refs_5_), channel_id=1, source_target_pairs={{0,4},{1,5},{2,6},{3,7},{8,12},{9,13},{10,14},{11,15},{16,20},{17,... | collective-permute-start | bytes 1572872 | tf_op jit(solution)/shard_map/ppermute | solution.py:320
  34.3 36.8 %copy-start.3 = (f32[512,256]{1,0:T(8,128)}, f32[512,256]{1,0:T(8,128)S(1)}, u32[]{:S(2)}) copy-start(f32[512,256]{1,0:T(8,128)S(1)} %broadcast_select_fusion.3.refs_8_) | copy-start | bytes 1572868
  34.3 14.7 %collective-permute-start.11 = (f32[512,256]{1,0:T(8,128)S(1)}, f32[512,256]{1,0:T(8,128)S(1)}, u32[]{:S(2)}, u32[]{:S(2)}) collective-permute-start(f32[512,256]{1,0:T(8,128)S(1)} %broadcast_select_fusion.3.refs_8_), channel_id=1, source_target_pairs={{0,2},{1,3},{2,0},{3,1},{4,6},{5,7},{6,4},{7,5},{8,10},{9,11},{10,... | collective-permute-start | bytes 1572872 | tf_op jit(solution)/shard_map/ppermute | solution.py:223
  35.9 40.0 %copy-start.17 = (f32[512]{0:T(512)S(1)}, f32[512]{0:T(512)}, u32[]{:S(2)}) copy-start(f32[512]{0:T(512)} %param.7) | copy-start | bytes 6148
  35.9 14.7 %collective-permute-start.3 = (f32[512,256]{1,0:T(8,128)}, f32[512,256]{1,0:T(8,128)S(1)}, u32[]{:S(2)}, u32[]{:S(2)}) collective-permute-start(f32[512,256]{1,0:T(8,128)} %get-tuple-element.33), channel_id=1, source_target_pairs={{0,24},{8,16},{16,8},{24,0},{1,25},{9,17},{17,9},{25,1},{2,26},{10... | collective-permute-start | bytes 1572872 | tf_op jit(solution)/shard_map/ppermute | solution.py:223
  38.3 32.8 %copy-start.2 = (f32[512,256]{1,0:T(8,128)}, f32[512,256]{1,0:T(8,128)S(1)}, u32[]{:S(2)}) copy-start(f32[512,256]{1,0:T(8,128)S(1)} %collective-permute-done.1.refs_6_) | copy-start | bytes 1572868
  44.5 13.8 %collective-permute-start.5 = (f32[512,256]{1,0:T(8,128)S(1)}, f32[512,256]{1,0:T(8,128)S(1)}, u32[]{:S(2)}, u32[]{:S(2)}) collective-permute-start(f32[512,256]{1,0:T(8,128)S(1)} %collective-permute-done.1.refs_6_), channel_id=1, source_target_pairs={{0,4},{1,5},{2,6},{3,7},{8,12},{9,13},{10,14},{11,15},{16,20},{17,... | collective-permute-start | bytes 1572872 | tf_op jit(solution)/shard_map/ppermute | solution.py:320
  49.0 28.3 %copy-start.5 = (f32[512,256]{1,0:T(8,128)}, f32[512,256]{1,0:T(8,128)S(1)}, u32[]{:S(2)}) copy-start(f32[512,256]{1,0:T(8,128)S(1)} %broadcast_select_fusion.2.refs_9_) | copy-start | bytes 1572868
  49.0 24.5 %copy-start.9 = (f32[512,256]{1,0:T(8,128)}, f32[512,256]{1,0:T(8,128)S(1)}, u32[]{:S(2)}) copy-start(f32[512,256]{1,0:T(8,128)S(1)} %collective-permute-done.11.refs_6_) | copy-start | bytes 1572868
  49.0 13.7 %collective-permute-start.12 = (f32[512,256]{1,0:T(8,128)S(1)}, f32[512,256]{1,0:T(8,128)S(1)}, u32[]{:S(2)}, u32[]{:S(2)}) collective-permute-start(f32[512,256]{1,0:T(8,128)S(1)} %broadcast_select_fusion.2.refs_9_), channel_id=1, source_target_pairs={{0,2},{1,3},{2,0},{3,1},{4,6},{5,7},{6,4},{7,5},{8,10},{9,11},{10,... | collective-permute-start | bytes 1572872 | tf_op jit(solution)/shard_map/ppermute | solution.py:223
  50.6 26.7 %copy-start.4 = (f32[512,256]{1,0:T(8,128)}, f32[512,256]{1,0:T(8,128)S(1)}, u32[]{:S(2)}) copy-start(f32[512,256]{1,0:T(8,128)S(1)} %collective-permute-done.3.refs_7_) | copy-start | bytes 1572868
  58.2 12.8 %collective-permute-start.6 = (f32[512,256]{1,0:T(8,128)S(1)}, f32[512,256]{1,0:T(8,128)S(1)}, u32[]{:S(2)}, u32[]{:S(2)}) collective-permute-start(f32[512,256]{1,0:T(8,128)S(1)} %collective-permute-done.3.refs_7_), channel_id=1, source_target_pairs={{0,4},{1,5},{2,6},{3,7},{8,12},{9,13},{10,14},{11,15},{16,20},{17,... | collective-permute-start | bytes 1572872 | tf_op jit(solution)/shard_map/ppermute | solution.py:320
  62.7 14.6 %copy-start.6 = (f32[512,256]{1,0:T(8,128)}, f32[512,256]{1,0:T(8,128)S(1)}, u32[]{:S(2)}) copy-start(f32[512,256]{1,0:T(8,128)S(1)} %broadcast_select_fusion.1.refs_10_) | copy-start | bytes 1572868
  62.7 10.7 %copy-start.10 = (f32[512,256]{1,0:T(8,128)}, f32[512,256]{1,0:T(8,128)S(1)}, u32[]{:S(2)}) copy-start(f32[512,256]{1,0:T(8,128)S(1)} %collective-permute-done.12.refs_7_) | copy-start | bytes 1572868
  62.8 10.7 %collective-permute-start.13 = (f32[512,256]{1,0:T(8,128)S(1)}, f32[512,256]{1,0:T(8,128)S(1)}, u32[]{:S(2)}, u32[]{:S(2)}) collective-permute-start(f32[512,256]{1,0:T(8,128)S(1)} %broadcast_select_fusion.1.refs_10_), channel_id=1, source_target_pairs={{0,2},{1,3},{2,0},{3,1},{4,6},{5,7},{6,4},{7,5},{8,10},{9,11},{10,... | collective-permute-start | bytes 1572872 | tf_op jit(solution)/shard_map/ppermute | solution.py:223
  64.3 12.4 %collective-permute-start.7 = (f32[512,256]{1,0:T(8,128)S(1)}, f32[512,256]{1,0:T(8,128)}, u32[]{:S(2)}, u32[]{:S(2)}) collective-permute-start(f32[512,256]{1,0:T(8,128)S(1)} %broadcast_select_fusion.3.refs_8_), channel_id=1, source_target_pairs={{0,1},{1,0},{2,3},{3,2},{4,5},{5,4},{6,7},{7,6},{8,9},{9,8},{10,11... | collective-permute-start | bytes 1572872 | tf_op jit(solution)/shard_map/ppermute | solution.py:223
  64.3 12.4 %collective-permute-start.8 = (f32[512,256]{1,0:T(8,128)S(1)}, f32[512,256]{1,0:T(8,128)}, u32[]{:S(2)}, u32[]{:S(2)}) collective-permute-start(f32[512,256]{1,0:T(8,128)S(1)} %broadcast_select_fusion.2.refs_9_), channel_id=1, source_target_pairs={{0,1},{1,0},{2,3},{3,2},{4,5},{5,4},{6,7},{7,6},{8,9},{9,8},{10,11... | collective-permute-start | bytes 1572872 | tf_op jit(solution)/shard_map/ppermute | solution.py:223
  64.8 12.4 %collective-permute-start.9 = (f32[512,256]{1,0:T(8,128)S(1)}, f32[512,256]{1,0:T(8,128)}, u32[]{:S(2)}, u32[]{:S(2)}) collective-permute-start(f32[512,256]{1,0:T(8,128)S(1)} %broadcast_select_fusion.1.refs_10_), channel_id=1, source_target_pairs={{0,1},{1,0},{2,3},{3,2},{4,5},{5,4},{6,7},{7,6},{8,9},{9,8},{10,11... | collective-permute-start | bytes 1572872 | tf_op jit(solution)/shard_map/ppermute | solution.py:223
  71.1 6.1 %copy-start.7 = (f32[512,256]{1,0:T(8,128)}, f32[512,256]{1,0:T(8,128)S(1)}, u32[]{:S(2)}) copy-start(f32[512,256]{1,0:T(8,128)S(1)} %broadcast_select_fusion.refs_11_) | copy-start | bytes 1572868
  71.2 6.1 %collective-permute-start.10 = (f32[512,256]{1,0:T(8,128)S(1)}, f32[512,256]{1,0:T(8,128)}, u32[]{:S(2)}, u32[]{:S(2)}) collective-permute-start(f32[512,256]{1,0:T(8,128)S(1)} %broadcast_select_fusion.refs_11_), channel_id=1, source_target_pairs={{0,1},{1,0},{2,3},{3,2},{4,5},{5,4},{6,7},{7,6},{8,9},{9,8},{10,11... | collective-permute-start | bytes 1572872 | tf_op jit(solution)/shard_map/ppermute | solution.py:223
  73.5 0.8 copy-start.11
  74.3 16.4 %collective-permute-start.14 = (f32[512,256]{1,0:T(8,128)S(1)}, f32[512,256]{1,0:T(8,128)S(1)}, u32[]{:S(2)}, u32[]{:S(2)}) collective-permute-start(f32[512,256]{1,0:T(8,128)S(1)} %broadcast_select_fusion.refs_11_), channel_id=1, source_target_pairs={{0,2},{1,3},{2,0},{3,1},{4,6},{5,7},{6,4},{7,5},{8,10},{9,11},{10,... | collective-permute-start | bytes 1572872 | tf_op jit(solution)/shard_map/ppermute | solution.py:223
  76.7 14.5 %collective-permute-start.15 = (f32[512,256]{1,0:T(8,128)}, f32[512,256]{1,0:T(8,128)S(1)}, u32[]{:S(2)}, u32[]{:S(2)}) collective-permute-start(f32[512,256]{1,0:T(8,128)} %copy-done.9), channel_id=1, source_target_pairs={{0,1},{1,0},{2,3},{3,2},{4,5},{5,4},{6,7},{7,6},{8,9},{9,8},{10,11... | collective-permute-start | bytes 1572872 | tf_op jit(solution)/shard_map/ppermute | solution.py:223
  76.7 14.5 %collective-permute-start.16 = (f32[512,256]{1,0:T(8,128)}, f32[512,256]{1,0:T(8,128)}, u32[]{:S(2)}, u32[]{:S(2)}) collective-permute-start(f32[512,256]{1,0:T(8,128)} %copy-done.10), channel_id=1, source_target_pairs={{0,1},{1,0},{2,3},{3,2},{4,5},{5,4},{6,7},{7,6},{8,9},{9,8},{10,11... | collective-permute-start | bytes 1572872 | tf_op jit(solution)/shard_map/ppermute | solution.py:223
  77.2 14.0 %collective-permute-start.17 = (f32[512,256]{1,0:T(8,128)}, f32[512,256]{1,0:T(8,128)}, u32[]{:S(2)}, u32[]{:S(2)}) collective-permute-start(f32[512,256]{1,0:T(8,128)} %copy-done.11), channel_id=1, source_target_pairs={{0,1},{1,0},{2,3},{3,2},{4,5},{5,4},{6,7},{7,6},{8,9},{9,8},{10,11... | collective-permute-start | bytes 1572872 | tf_op jit(solution)/shard_map/ppermute | solution.py:223
  90.7 2.1 %copy-start.12 = (f32[512,256]{1,0:T(8,128)}, f32[512,256]{1,0:T(8,128)S(1)}, u32[]{:S(2)}) copy-start(f32[512,256]{1,0:T(8,128)S(1)} %collective-permute-done.14.refs_9_) | copy-start | bytes 1572868
  90.7 2.0 %collective-permute-start.18 = (f32[512,256]{1,0:T(8,128)S(1)}, f32[512,256]{1,0:T(8,128)S(1)}, u32[]{:S(2)}, u32[]{:S(2)}) collective-permute-start(f32[512,256]{1,0:T(8,128)S(1)} %collective-permute-done.14.refs_9_), channel_id=1, source_target_pairs={{0,1},{1,0},{2,3},{3,2},{4,5},{5,4},{6,7},{7,6},{8,9},{9,8},{10,11... | collective-permute-start | bytes 1572872 | tf_op jit(solution)/shard_map/ppermute | solution.py:223
  91.2 1.5 copy-start.13
  92.7 0.8 copy-start.14
  108.1 22.1 %copy-start.21 = (f32[128,256]{1,0:T(8,128)S(1)}, f32[128,256]{1,0:T(8,128)}, u32[]{:S(2)}) copy-start(f32[128,256]{1,0:T(8,128)} %get-tuple-element.52) | copy-start | bytes 393220
  109.3 2.0 %collective-permute-start.20 = (f32[256,512]{1,0:T(8,128)S(1)}, f32[256,512]{1,0:T(8,128)S(1)}, u32[]{:S(2)}, u32[]{:S(2)}) collective-permute-start(f32[256,512]{1,0:T(8,128)S(1)} %constant_dynamic-slice_fusion.3), channel_id=1, source_target_pairs={{0,1},{1,0},{2,3},{3,2},{4,5},{5,4},{6,7},{7,6},{8,9},{9,8},{10,11... | collective-permute-start | bytes 1572872 | tf_op jit(solution)/shard_map/ppermute | solution.py:223
  109.7 20.5 %collective-permute-start.19 = (f32[384,256]{1,0:T(8,128)}, f32[384,256]{1,0:T(8,128)S(1)}, u32[]{:S(2)}, u32[]{:S(2)}) collective-permute-start(f32[384,256]{1,0:T(8,128)} %get-tuple-element.49), channel_id=1, source_target_pairs={{0,16},{8,24},{16,0},{24,8},{1,17},{9,25},{17,1},{25,9},{2,18},{10... | collective-permute-start | bytes 1179656 | tf_op jit(solution)/shard_map/ppermute | solution.py:223
  112.4 27.6 %copy-start.19 = (f32[512,256]{1,0:T(8,128)S(1)}, f32[512,256]{1,0:T(8,128)}, u32[]{:S(2)}) copy-start(f32[512,256]{1,0:T(8,128)} %get-tuple-element.59) | copy-start | bytes 1572868
  112.4 29.5 %copy-start.20 = (f32[512,256]{1,0:T(8,128)S(1)}, f32[512,256]{1,0:T(8,128)}, u32[]{:S(2)}) copy-start(f32[512,256]{1,0:T(8,128)} %get-tuple-element.56) | copy-start | bytes 1572868
  112.4 6.4 %collective-permute-start.21 = (f32[64,512]{1,0:T(8,128)S(1)}, f32[64,512]{1,0:T(8,128)S(1)}, u32[]{:S(2)}, u32[]{:S(2)}) collective-permute-start(f32[64,512]{1,0:T(8,128)S(1)} %get-tuple-element.68), channel_id=1, source_target_pairs={{0,2},{1,3},{2,0},{3,1},{4,6},{5,7},{6,4},{7,5},{8,10},{9,11},{10,... | collective-permute-start | bytes 393224 | tf_op jit(solution)/shard_map/ppermute | solution.py:223
  113.0 8.3 %collective-permute-start.22 = (f32[64,512]{1,0:T(8,128)S(1)}, f32[64,512]{1,0:T(8,128)S(1)}, u32[]{:S(2)}, u32[]{:S(2)}) collective-permute-start(f32[64,512]{1,0:T(8,128)S(1)} %get-tuple-element.70), channel_id=1, source_target_pairs={{0,4},{1,5},{2,6},{3,7},{4,0},{5,1},{6,2},{7,3},{8,12},{9,13},{10,... | collective-permute-start | bytes 393224 | tf_op jit(solution)/shard_map/ppermute | solution.py:223
  113.4 8.0 %collective-permute-start.23 = (f32[64,512]{1,0:T(8,128)S(1)}, f32[64,512]{1,0:T(8,128)S(1)}, u32[]{:S(2)}, u32[]{:S(2)}) collective-permute-start(f32[64,512]{1,0:T(8,128)S(1)} %get-tuple-element.69), channel_id=1, source_target_pairs={{0,6},{1,7},{2,4},{3,5},{4,2},{5,3},{6,0},{7,1},{8,14},{9,15},{10,... | collective-permute-start | bytes 393224 | tf_op jit(solution)/shard_map/ppermute | solution.py:223
  130.2 7.3 %collective-permute-start.25 = (f32[64,512]{1,0:T(8,128)S(1)}, f32[64,512]{1,0:T(8,128)S(1)}, u32[]{:S(2)}, u32[]{:S(2)}) collective-permute-start(f32[64,512]{1,0:T(8,128)S(1)} %add_add_fusion), channel_id=1, source_target_pairs={{0,8},{8,0},{16,24},{24,16},{1,9},{9,1},{17,25},{25,17},{2,10},{10... | collective-permute-start | bytes 393224 | tf_op jit(solution)/shard_map/ppermute | solution.py:223
  130.2 9.2 %collective-permute-start.24 = (f32[128,256]{1,0:T(8,128)S(1)}, f32[128,256]{1,0:T(8,128)S(1)}, u32[]{:S(2)}, u32[]{:S(2)}) collective-permute-start(f32[128,256]{1,0:T(8,128)S(1)} %copy-done.21), channel_id=1, source_target_pairs={{0,16},{8,24},{16,0},{24,8},{1,17},{9,25},{17,1},{25,9},{2,18},{10... | collective-permute-start | bytes 393224 | tf_op jit(solution)/shard_map/ppermute | solution.py:223
  139.4 7.9 %collective-permute-start.28 = (f32[64,512]{1,0:T(8,128)S(1)}, f32[64,512]{1,0:T(8,128)S(1)}, u32[]{:S(2)}, u32[]{:S(2)}) collective-permute-start(f32[64,512]{1,0:T(8,128)S(1)} %add.176), channel_id=1, source_target_pairs={{0,16},{8,24},{16,0},{24,8},{1,17},{9,25},{17,1},{25,9},{2,18},{10... | collective-permute-start | bytes 393224 | tf_op jit(solution)/shard_map/ppermute | solution.py:223
  140.0 27.0 %copy-start.15 = (f32[512,256]{1,0:T(8,128)S(1)}, f32[512,256]{1,0:T(8,128)}, u32[]{:S(2)}) copy-start(f32[512,256]{1,0:T(8,128)} %get-tuple-element.57) | copy-start | bytes 1572868
  140.0 27.1 %collective-permute-start.27 = (f32[512,256]{1,0:T(8,128)S(1)}, f32[512,256]{1,0:T(8,128)S(1)}, u32[]{:S(2)}, u32[]{:S(2)}) collective-permute-start(f32[512,256]{1,0:T(8,128)S(1)} %copy-done.19), channel_id=1, source_target_pairs={{0,8},{8,0},{16,24},{24,16},{1,9},{9,1},{17,25},{25,17},{2,10},{10... | collective-permute-start | bytes 1572872 | tf_op jit(solution)/shard_map/ppermute | solution.py:223
  141.9 25.0 %collective-permute-start.26 = (f32[512,256]{1,0:T(8,128)S(1)}, f32[512,256]{1,0:T(8,128)S(1)}, u32[]{:S(2)}, u32[]{:S(2)}) collective-permute-start(f32[512,256]{1,0:T(8,128)S(1)} %copy-done.20), channel_id=1, source_target_pairs={{0,24},{8,16},{16,8},{24,0},{1,25},{9,17},{17,9},{25,1},{2,26},{10... | collective-permute-start | bytes 1572872 | tf_op jit(solution)/shard_map/ppermute | solution.py:223
  147.3 6.4 %collective-permute-start.29 = (f32[64,512]{1,0:T(8,128)S(1)}, f32[64,512]{1,0:T(8,128)S(1)}, u32[]{:S(2)}, u32[]{:S(2)}) collective-permute-start(f32[64,512]{1,0:T(8,128)S(1)} %add.179), channel_id=1, source_target_pairs={{0,2},{1,3},{2,0},{3,1},{4,6},{5,7},{6,4},{7,5},{8,10},{9,11},{10,... | collective-permute-start | bytes 393224 | tf_op jit(solution)/shard_map/ppermute | solution.py:223
  147.9 7.5 %collective-permute-start.30 = (f32[64,512]{1,0:T(8,128)S(1)}, f32[64,512]{1,0:T(8,128)S(1)}, u32[]{:S(2)}, u32[]{:S(2)}) collective-permute-start(f32[64,512]{1,0:T(8,128)S(1)} %add.179), channel_id=1, source_target_pairs={{0,4},{1,5},{2,6},{3,7},{4,0},{5,1},{6,2},{7,3},{8,12},{9,13},{10,... | collective-permute-start | bytes 393224 | tf_op jit(solution)/shard_map/ppermute | solution.py:223
  148.3 7.1 %collective-permute-start.31 = (f32[64,512]{1,0:T(8,128)S(1)}, f32[64,512]{1,0:T(8,128)S(1)}, u32[]{:S(2)}, u32[]{:S(2)}) collective-permute-start(f32[64,512]{1,0:T(8,128)S(1)} %add.179), channel_id=1, source_target_pairs={{0,6},{1,7},{2,4},{3,5},{4,2},{5,3},{6,0},{7,1},{8,14},{9,15},{10,... | collective-permute-start | bytes 393224 | tf_op jit(solution)/shard_map/ppermute | solution.py:223
  155.5 11.7 %collective-permute-start.32 = (f32[256,512]{1,0:T(8,128)S(1)}, f32[256,512]{1,0:T(8,128)S(1)}, u32[]{:S(2)}, u32[]{:S(2)}) collective-permute-start(f32[256,512]{1,0:T(8,128)S(1)} %maximum_select_fusion.1), channel_id=1, source_target_pairs={{0,1},{1,0},{2,3},{3,2},{4,5},{5,4},{6,7},{7,6},{8,9},{9,8},{10,11... | collective-permute-start | bytes 1572872 | tf_op jit(solution)/shard_map/ppermute | solution.py:223
  167.1 1.7 copy-start.8

commit v6 on v5

--- a/solution.py
+++ b/solution.py
@@ -8,6 +8,7 @@
 from jax.sharding import PartitionSpec as P
 
 BLOCK = 64
+LANES = 128
 NPANEL = 4
 TILE = 256
 VMEM_LIMIT = 60 * 1024 * 1024
@@ -91,7 +92,7 @@
         cross = dot_nt(own[0][...], panel[0][cols, :])
         cross += dot_nt(own[0][...], panel[1][cols, :])
         cross += dot_nt(own[1][...], panel[0][cols, :])
-        value = cross / (energy - vir_col[...] - vir_row[:, cols]) * live
+        value = cross / (energy - vir_col[:, :1] - vir_row[:, cols]) * live
         amp[:, cols] = value
         a_parts[0][:, cols], a_parts[1][:, cols] = halves(value)
     for above in range(0, nvir, TILE):
@@ -295,7 +296,8 @@
         live = jnp.any(lists == panels[turn]).astype(jnp.float32)
         scalars += [occ_energy[own_orbital] + occ_energy[orbitals[1 + turn]], live]
     small = masks[:3], masks[3:], jnp.stack(scalars[:4]), jnp.stack(scalars[4:])
-    virtual = lax.optimization_barrier((vir_energy[:, None], vir_energy[None, :]))
+    column = jnp.broadcast_to(vir_energy[:, None], (nvir, LANES))
+    virtual = lax.optimization_barrier((column, vir_energy[None, :]))
 
     own, came, near, far = [], [], [], []
 

time: 169 us -> 169 us (level)
  no operation moved by 1% of the time
where the time goes in v6:
time: 169 us
  waiting for transfers between devices  71.2 us (42%)
  starting transfers between devices  44.1 us (26%)
  Pallas kernels  27.9 us (17%)
  local copies, waits for them, and re-layouts  11.4 us (7%)
  between operations  8.67 us (5%)
  other arithmetic  5.49 us (3%)
    ppermute x29, waiting for transfers between devices, exchange(): return lax.ppermute(value, axis, [(at, at ^ bit) for at in range(size)])  51.1 us
    ppermute x29, starting transfers between devices, exchange(): return lax.ppermute(value, axis, [(at, at ^ bit) for at in range(size)])  28.8 us
    pallas_call x2, Pallas kernels, call(): pl.pallas_call(functools.partial(staged, kernel, len(small), len(big), le...  27.9 us
    ppermute x4, waiting for transfers between devices, on_device(): got = lax.ppermute(rows, 'col', links)  20.1 us
    ppermute x4, starting transfers between devices, on_device(): got = lax.ppermute(rows, 'col', links)  15.3 us
  transfers between devices with their start and end apart: 33, of which 16 were waited for; matrix products, arithmetic and copies ran while one was open for 6% of the time, Pallas kernels for 8%

profile of v6, /device:TPU:0, one launch (start us, length us, event | category | flops | bytes accessed | tf_op | source)
XLA Modules:
  0.0 168.8 jit_solution(12199918621450314104)
XLA Ops:
  0.7 2.7 %dynamic-slice_bitcast_fusion = (f32[512,256]{1,0:T(8,128)S(1)}, f32[512,256]{1,0:T(8,128)}, f32[512,256]{1,0:T(8,128)S(1)}, f32[512,256]{1,0:T(8,128)}) fusion(f32[4,512,256]{2,1,0:T(8,128)} %param.5, s32[]{:T(128)S(6)} %select_n.171, s32[]{:T(128)S(6)} %select_n.169, s32[]{:T(128)S(6)} %select_n.163, s32[]{:T(128)S(6)} %select_n.170), kind=kLoop, calls=%fused_computation.8 | loop fusion | bytes 4194320 | tf_op jit(solution)/shard_map/jit(dynamic_index_in_dim)/squeeze | solution.py:306
  3.4 4.9 %collective-permute-start.2 = (f32[512,256]{1,0:T(8,128)S(1)}, f32[512,256]{1,0:T(8,128)S(1)}, u32[]{:S(2)}, u32[]{:S(2)}) collective-permute-start(f32[512,256]{1,0:T(8,128)S(1)} %get-tuple-element.66.refs_4_), channel_id=1, source_target_pairs={{0,4},{1,5},{2,6},{3,7},{8,12},{9,13},{10,14},{11,15},{16,20},{17,... | collective-permute-start | bytes 1572872 | tf_op jit(solution)/shard_map/ppermute | solution.py:322
  8.3 1.6 collective-permute-start
  9.9 2.6 %collective-permute-start.1 = (f32[512,256]{1,0:T(8,128)}, f32[512,256]{1,0:T(8,128)S(1)}, u32[]{:S(2)}, u32[]{:S(2)}) collective-permute-start(f32[512,256]{1,0:T(8,128)} %get-tuple-element.67), channel_id=1, source_target_pairs={{0,16},{8,24},{16,0},{24,8},{1,17},{9,25},{17,1},{25,9},{2,18},{10... | collective-permute-start | bytes 1572872 | tf_op jit(solution)/shard_map/ppermute | solution.py:224
  12.7 0.1 copy.10
  12.8 0.6 gather_fusion
  13.4 0.6 gather_fusion.1
  14.1 0.7 fusion.2
  17.2 1.4 compare_reduce_fusion.1
  23.7 0.1 broadcast_in_dim.38
  23.8 0.8 slice.25.refs_3_
  24.7 0.7 slice.22.refs_3_
  25.4 0.8 broadcast_in_dim.35.refs_1_
  26.3 0.7 pad_maximum_fusion.1.refs_0_
  26.9 0.6 pad_maximum_fusion.refs_0_
  27.5 5.5 %collective-permute-done.refs_5_ = f32[512,256]{1,0:T(8,128)S(1)} collective-permute-done((f32[512,256]{1,0:T(8,128)}, f32[512,256]{1,0:T(8,128)S(1)}, u32[]{:S(2)}, u32[]{:S(2)}) %collective-permute-start) | collective-permute-done | bytes 524320 | tf_op jit(solution)/shard_map/ppermute | solution.py:224
  33.1 1.6 collective-permute-start.4
  34.7 1.6 collective-permute-start.11
  36.3 2.5 %collective-permute-start.3 = (f32[512,256]{1,0:T(8,128)S(1)}, f32[512,256]{1,0:T(8,128)S(1)}, u32[]{:S(2)}, u32[]{:S(2)}) collective-permute-start(f32[512,256]{1,0:T(8,128)S(1)} %get-tuple-element.33), channel_id=1, source_target_pairs={{0,24},{8,16},{16,8},{24,0},{1,25},{9,17},{17,9},{25,1},{2,26},{10... | collective-permute-start | bytes 1572872 | tf_op jit(solution)/shard_map/ppermute | solution.py:224
  38.8 6.1 %collective-permute-done.4 = f32[512,256]{1,0:T(8,128)S(1)} collective-permute-done((f32[512,256]{1,0:T(8,128)S(1)}, f32[512,256]{1,0:T(8,128)S(1)}, u32[]{:S(2)}, u32[]{:S(2)}) %collective-permute-start.4) | collective-permute-done | bytes 524320 | tf_op jit(solution)/shard_map/ppermute | solution.py:322
  44.9 4.4 %collective-permute-start.5 = (f32[512,256]{1,0:T(8,128)S(1)}, f32[512,256]{1,0:T(8,128)S(1)}, u32[]{:S(2)}, u32[]{:S(2)}) collective-permute-start(f32[512,256]{1,0:T(8,128)S(1)} %collective-permute-done.1.refs_6_), channel_id=1, source_target_pairs={{0,4},{1,5},{2,6},{3,7},{8,12},{9,13},{10,14},{11,15},{16,20},{17,... | collective-permute-start | bytes 1572872 | tf_op jit(solution)/shard_map/ppermute | solution.py:322
  49.4 1.6 collective-permute-start.12
  51.0 7.7 %collective-permute-done.5 = f32[512,256]{1,0:T(8,128)S(1)} collective-permute-done((f32[512,256]{1,0:T(8,128)S(1)}, f32[512,256]{1,0:T(8,128)S(1)}, u32[]{:S(2)}, u32[]{:S(2)}) %collective-permute-start.5) | collective-permute-done | bytes 524320 | tf_op jit(solution)/shard_map/ppermute | solution.py:322
  58.7 4.4 %collective-permute-start.6 = (f32[512,256]{1,0:T(8,128)S(1)}, f32[512,256]{1,0:T(8,128)S(1)}, u32[]{:S(2)}, u32[]{:S(2)}) collective-permute-start(f32[512,256]{1,0:T(8,128)S(1)} %collective-permute-done.3.refs_7_), channel_id=1, source_target_pairs={{0,4},{1,5},{2,6},{3,7},{8,12},{9,13},{10,14},{11,15},{16,20},{17,... | collective-permute-start | bytes 1572872 | tf_op jit(solution)/shard_map/ppermute | solution.py:322
  63.2 1.6 collective-permute-start.13
  64.7 0.5 collective-permute-start.8
  65.2 6.3 %collective-permute-done.6 = f32[512,256]{1,0:T(8,128)S(1)} collective-permute-done((f32[512,256]{1,0:T(8,128)S(1)}, f32[512,256]{1,0:T(8,128)S(1)}, u32[]{:S(2)}, u32[]{:S(2)}) %collective-permute-start.6) | collective-permute-done | bytes 524320 | tf_op jit(solution)/shard_map/ppermute | solution.py:322
  71.8 2.3 %collective-permute-done.13.refs_8_ = f32[512,256]{1,0:T(8,128)} collective-permute-done((f32[512,256]{1,0:T(8,128)S(1)}, f32[512,256]{1,0:T(8,128)}, u32[]{:S(2)}, u32[]{:S(2)}) %collective-permute-start.13) | collective-permute-done | bytes 524320 | tf_op jit(solution)/shard_map/ppermute | solution.py:224
  74.1 1.5 collective-permute-start.14
  75.6 0.5 collective-permute-start.16
  76.1 0.3 copy-done.11
  76.4 0.2 copy-done.12
  76.6 0.7 copy-done.13
  77.3 13.4 %early.1 = (bf16[512,1024]{1,0:T(8,128)(2,1)}, bf16[512,1024]{1,0:T(8,128)(2,1)}, f32[512,512]{1,0:T(8,128)}, f32[512,256]{1,0:T(8,128)}, f32[512,256]{1,0:T(8,1...) custom-call(f32[4]{0:T(128)} %pad_maximum_fusion.1.refs_0_, f32[512,128]{1,0:T(8,128)} %broadcast_in_dim.35.refs_1_, ...), custom_call_target="tpu_custom_call" | custom-call | tf_op jit(solution)/shard_map/early/pallas_call | solution.py:42
  90.8 1.8 %collective-permute-done.18.refs_13_ = f32[512,256]{1,0:T(8,128)S(1)} collective-permute-done((f32[512,256]{1,0:T(8,128)S(1)}, f32[512,256]{1,0:T(8,128)S(1)}, u32[]{:S(2)}, u32[]{:S(2)}) %collective-permute-start.18) | collective-permute-done | bytes 524320 | tf_op jit(solution)/shard_map/ppermute | solution.py:224
  92.7 0.8 copy-done.14
  93.5 14.5 %late.1 = (f32[512,512]{1,0:T(8,128)}, f32[384,256]{1,0:T(8,128)}, f32[128,256]{1,0:T(8,128)}, f32[512,256]{1,0:T(8,128)}, f32[512,256]{1,0:T(8,128)}, /*index=5*/f32[512,256]{1,0:T(8,128)}) custom-call(f32[4]{0:T(128)} %pad_maximum_fusion.refs_0_, f32[512,128]{1,0:T(8,128)} %broadcast_in_dim.35.refs_1_, f32[1,512]{1,0:T(1,128)} %bitcast.45, ...), custom_call_target="tpu_custom_call" | custom-call | tf_op jit(solution)/shard_map/late/pallas_call | solution.py:42
  108.1 1.1 constant_dynamic-slice_fusion.3
  109.2 0.2 collective-permute-start.20
  109.4 0.7 collective-permute-start.19
  110.1 1.1 collective-permute-done.20
  111.2 1.1 dynamic-slice_add_fusion
  112.4 0.6 collective-permute-start.21
  113.0 0.2 collective-permute-start.22
  113.2 2.8 %collective-permute-start.23 = (f32[64,512]{1,0:T(8,128)S(1)}, f32[64,512]{1,0:T(8,128)S(1)}, u32[]{:S(2)}, u32[]{:S(2)}) collective-permute-start(f32[64,512]{1,0:T(8,128)S(1)} %get-tuple-element.69), channel_id=1, source_target_pairs={{0,6},{1,7},{2,4},{3,5},{4,2},{5,3},{6,0},{7,1},{8,14},{9,15},{10,... | collective-permute-start | bytes 393224 | tf_op jit(solution)/shard_map/ppermute | solution.py:224
  115.9 2.9 %collective-permute-done.21 = f32[64,512]{1,0:T(8,128)S(1)} collective-permute-done((f32[64,512]{1,0:T(8,128)S(1)}, f32[64,512]{1,0:T(8,128)S(1)}, u32[]{:S(2)}, u32[]{:S(2)}) %collective-permute-start.21) | collective-permute-done | bytes 131104 | tf_op jit(solution)/shard_map/ppermute | solution.py:224
  118.8 2.3 %collective-permute-done.22 = f32[64,512]{1,0:T(8,128)S(1)} collective-permute-done((f32[64,512]{1,0:T(8,128)S(1)}, f32[64,512]{1,0:T(8,128)S(1)}, u32[]{:S(2)}, u32[]{:S(2)}) %collective-permute-start.22) | collective-permute-done | bytes 131104 | tf_op jit(solution)/shard_map/ppermute | solution.py:224
  121.1 9.1 %collective-permute-done.19 = f32[384,256]{1,0:T(8,128)S(1)} collective-permute-done((f32[384,256]{1,0:T(8,128)}, f32[384,256]{1,0:T(8,128)S(1)}, u32[]{:S(2)}, u32[]{:S(2)}) %collective-permute-start.19) | collective-permute-done | bytes 393248 | tf_op jit(solution)/shard_map/ppermute | solution.py:224
  130.2 2.3 %collective-permute-start.24 = (f32[128,256]{1,0:T(8,128)S(1)}, f32[128,256]{1,0:T(8,128)S(1)}, u32[]{:S(2)}, u32[]{:S(2)}) collective-permute-start(f32[128,256]{1,0:T(8,128)S(1)} %copy-done.21), channel_id=1, source_target_pairs={{0,16},{8,24},{16,0},{24,8},{1,17},{9,25},{17,1},{25,9},{2,18},{10... | collective-permute-start | bytes 393224 | tf_op jit(solution)/shard_map/ppermute | solution.py:224
  132.5 5.1 %collective-permute-done.25 = f32[64,512]{1,0:T(8,128)S(1)} collective-permute-done((f32[64,512]{1,0:T(8,128)S(1)}, f32[64,512]{1,0:T(8,128)S(1)}, u32[]{:S(2)}, u32[]{:S(2)}) %collective-permute-start.25) | collective-permute-done | bytes 131104 | tf_op jit(solution)/shard_map/ppermute | solution.py:224
  137.6 1.8 %collective-permute-done.24 = f32[128,256]{1,0:T(8,128)S(1)} collective-permute-done((f32[128,256]{1,0:T(8,128)S(1)}, f32[128,256]{1,0:T(8,128)S(1)}, u32[]{:S(2)}, u32[]{:S(2)}) %collective-permute-start.24) | collective-permute-done | bytes 131104 | tf_op jit(solution)/shard_map/ppermute | solution.py:224
  139.4 0.3 collective-permute-start.28
  139.8 0.2 broadcast_in_dim.34
  140.0 2.0 %collective-permute-start.27 = (f32[512,256]{1,0:T(8,128)S(1)}, f32[512,256]{1,0:T(8,128)S(1)}, u32[]{:S(2)}, u32[]{:S(2)}) collective-permute-start(f32[512,256]{1,0:T(8,128)S(1)} %copy-done.19), channel_id=1, source_target_pairs={{0,8},{8,0},{16,24},{24,16},{1,9},{9,1},{17,25},{25,17},{2,10},{10... | collective-permute-start | bytes 1572872 | tf_op jit(solution)/shard_map/ppermute | solution.py:224
  142.0 2.1 %collective-permute-start.26 = (f32[512,256]{1,0:T(8,128)S(1)}, f32[512,256]{1,0:T(8,128)S(1)}, u32[]{:S(2)}, u32[]{:S(2)}) collective-permute-start(f32[512,256]{1,0:T(8,128)S(1)} %copy-done.20), channel_id=1, source_target_pairs={{0,24},{8,16},{16,8},{24,0},{1,25},{9,17},{17,9},{25,1},{2,26},{10... | collective-permute-start | bytes 1572872 | tf_op jit(solution)/shard_map/ppermute | solution.py:224
  144.1 3.7 %collective-permute-done.28 = f32[64,512]{1,0:T(8,128)S(1)} collective-permute-done((f32[64,512]{1,0:T(8,128)S(1)}, f32[64,512]{1,0:T(8,128)S(1)}, u32[]{:S(2)}, u32[]{:S(2)}) %collective-permute-start.28) | collective-permute-done | bytes 131104 | tf_op jit(solution)/shard_map/ppermute | solution.py:224
  147.8 0.6 collective-permute-start.29
  148.4 0.2 collective-permute-start.30
  148.6 2.8 %collective-permute-start.31 = (f32[64,512]{1,0:T(8,128)S(1)}, f32[64,512]{1,0:T(8,128)S(1)}, u32[]{:S(2)}, u32[]{:S(2)}) collective-permute-start(f32[64,512]{1,0:T(8,128)S(1)} %add.179), channel_id=1, source_target_pairs={{0,6},{1,7},{2,4},{3,5},{4,2},{5,3},{6,0},{7,1},{8,14},{9,15},{10,... | collective-permute-start | bytes 393224 | tf_op jit(solution)/shard_map/ppermute | solution.py:224
  151.3 1.5 collective-permute-done.29
  152.8 1.9 %collective-permute-done.30 = f32[64,512]{1,0:T(8,128)S(1)} collective-permute-done((f32[64,512]{1,0:T(8,128)S(1)}, f32[64,512]{1,0:T(8,128)S(1)}, u32[]{:S(2)}, u32[]{:S(2)}) %collective-permute-start.30) | collective-permute-done | bytes 131104 | tf_op jit(solution)/shard_map/ppermute | solution.py:224
  154.9 12.1 %collective-permute-done.26 = f32[512,256]{1,0:T(8,128)S(1)} collective-permute-done((f32[512,256]{1,0:T(8,128)S(1)}, f32[512,256]{1,0:T(8,128)S(1)}, u32[]{:S(2)}, u32[]{:S(2)}) %collective-permute-start.26) | collective-permute-done | bytes 524320 | tf_op jit(solution)/shard_map/ppermute | solution.py:224
  167.1 1.2 maximum_select_fusion
  168.3 0.4 copy-done.8
  (94 shorter events, 1.5 us)
Async XLA Ops:
  0.7 12.0 %copy-start.16 = (s32[32,8,16]{0,2,1:T(8,128)S(1)}, s32[32,8,16]{0,2,1:T(8,128)}, u32[]{:S(2)}) copy-start(s32[32,8,16]{0,2,1:T(8,128)} %param.8) | copy-start | bytes 49156
  0.7 13.4 %copy-start.18 = (f32[32]{0:T(128)S(1)}, f32[32]{0:T(128)}, u32[]{:S(2)}) copy-start(f32[32]{0:T(128)} %param.6) | copy-start | bytes 388
  0.7 24.8 %copy-start.17 = (f32[512]{0:T(512)S(1)}, f32[512]{0:T(512)}, u32[]{:S(2)}) copy-start(f32[512]{0:T(512)} %param.7) | copy-start | bytes 6148
  3.4 46.0 %copy-start = (f32[512,256]{1,0:T(8,128)}, f32[512,256]{1,0:T(8,128)S(1)}, u32[]{:S(2)}) copy-start(f32[512,256]{1,0:T(8,128)S(1)} %get-tuple-element.66.refs_4_) | copy-start | bytes 1572868
  3.4 24.1 %collective-permute-start.2 = (f32[512,256]{1,0:T(8,128)S(1)}, f32[512,256]{1,0:T(8,128)S(1)}, u32[]{:S(2)}, u32[]{:S(2)}) collective-permute-start(f32[512,256]{1,0:T(8,128)S(1)} %get-tuple-element.66.refs_4_), channel_id=1, source_target_pairs={{0,4},{1,5},{2,6},{3,7},{8,12},{9,13},{10,14},{11,15},{16,20},{17,... | collective-permute-start | bytes 1572872 | tf_op jit(solution)/shard_map/ppermute | solution.py:322
  8.3 24.8 %collective-permute-start = (f32[512,256]{1,0:T(8,128)}, f32[512,256]{1,0:T(8,128)S(1)}, u32[]{:S(2)}, u32[]{:S(2)}) collective-permute-start(f32[512,256]{1,0:T(8,128)} %get-tuple-element.65), channel_id=1, source_target_pairs={{0,8},{8,0},{16,24},{24,16},{1,9},{9,1},{17,25},{25,17},{2,10},{10... | collective-permute-start | bytes 1572872 | tf_op jit(solution)/shard_map/ppermute | solution.py:224
  9.9 28.8 %collective-permute-start.1 = (f32[512,256]{1,0:T(8,128)}, f32[512,256]{1,0:T(8,128)S(1)}, u32[]{:S(2)}, u32[]{:S(2)}) collective-permute-start(f32[512,256]{1,0:T(8,128)} %get-tuple-element.67), channel_id=1, source_target_pairs={{0,16},{8,24},{16,0},{24,8},{1,17},{9,25},{17,1},{25,9},{2,18},{10... | collective-permute-start | bytes 1572872 | tf_op jit(solution)/shard_map/ppermute | solution.py:224
  33.1 30.1 %copy-start.1 = (f32[512,256]{1,0:T(8,128)}, f32[512,256]{1,0:T(8,128)S(1)}, u32[]{:S(2)}) copy-start(f32[512,256]{1,0:T(8,128)S(1)} %collective-permute-done.refs_5_) | copy-start | bytes 1572868
  33.1 11.8 %collective-permute-start.4 = (f32[512,256]{1,0:T(8,128)S(1)}, f32[512,256]{1,0:T(8,128)S(1)}, u32[]{:S(2)}, u32[]{:S(2)}) collective-permute-start(f32[512,256]{1,0:T(8,128)S(1)} %collective-permute-done.refs_5_), channel_id=1, source_target_pairs={{0,4},{1,5},{2,6},{3,7},{8,12},{9,13},{10,14},{11,15},{16,20},{17,... | collective-permute-start | bytes 1572872 | tf_op jit(solution)/shard_map/ppermute | solution.py:322
  34.7 36.9 %copy-start.3 = (f32[512,256]{1,0:T(8,128)}, f32[512,256]{1,0:T(8,128)S(1)}, u32[]{:S(2)}) copy-start(f32[512,256]{1,0:T(8,128)S(1)} %broadcast_select_fusion.3.refs_8_) | copy-start | bytes 1572868
  34.7 14.7 %collective-permute-start.11 = (f32[512,256]{1,0:T(8,128)S(1)}, f32[512,256]{1,0:T(8,128)S(1)}, u32[]{:S(2)}, u32[]{:S(2)}) collective-permute-start(f32[512,256]{1,0:T(8,128)S(1)} %broadcast_select_fusion.3.refs_8_), channel_id=1, source_target_pairs={{0,2},{1,3},{2,0},{3,1},{4,6},{5,7},{6,4},{7,5},{8,10},{9,11},{10,... | collective-permute-start | bytes 1572872 | tf_op jit(solution)/shard_map/ppermute | solution.py:224
  36.3 14.7 %collective-permute-start.3 = (f32[512,256]{1,0:T(8,128)S(1)}, f32[512,256]{1,0:T(8,128)S(1)}, u32[]{:S(2)}, u32[]{:S(2)}) collective-permute-start(f32[512,256]{1,0:T(8,128)S(1)} %get-tuple-element.33), channel_id=1, source_target_pairs={{0,24},{8,16},{16,8},{24,0},{1,25},{9,17},{17,9},{25,1},{2,26},{10... | collective-permute-start | bytes 1572872 | tf_op jit(solution)/shard_map/ppermute | solution.py:224
  38.8 32.9 %copy-start.2 = (f32[512,256]{1,0:T(8,128)}, f32[512,256]{1,0:T(8,128)S(1)}, u32[]{:S(2)}) copy-start(f32[512,256]{1,0:T(8,128)S(1)} %collective-permute-done.1.refs_6_) | copy-start | bytes 1572868
  44.9 13.8 %collective-permute-start.5 = (f32[512,256]{1,0:T(8,128)S(1)}, f32[512,256]{1,0:T(8,128)S(1)}, u32[]{:S(2)}, u32[]{:S(2)}) collective-permute-start(f32[512,256]{1,0:T(8,128)S(1)} %collective-permute-done.1.refs_6_), channel_id=1, source_target_pairs={{0,4},{1,5},{2,6},{3,7},{8,12},{9,13},{10,14},{11,15},{16,20},{17,... | collective-permute-start | bytes 1572872 | tf_op jit(solution)/shard_map/ppermute | solution.py:322
  49.4 27.9 %copy-start.5 = (f32[512,256]{1,0:T(8,128)}, f32[512,256]{1,0:T(8,128)S(1)}, u32[]{:S(2)}) copy-start(f32[512,256]{1,0:T(8,128)S(1)} %broadcast_select_fusion.2.refs_9_) | copy-start | bytes 1572868
  49.4 41.2 %copy-start.9 = (f32[512,256]{1,0:T(8,128)}, f32[512,256]{1,0:T(8,128)S(1)}, u32[]{:S(2)}) copy-start(f32[512,256]{1,0:T(8,128)S(1)} %collective-permute-done.11.refs_6_) | copy-start | bytes 1572868
  49.4 13.7 %collective-permute-start.12 = (f32[512,256]{1,0:T(8,128)S(1)}, f32[512,256]{1,0:T(8,128)}, u32[]{:S(2)}, u32[]{:S(2)}) collective-permute-start(f32[512,256]{1,0:T(8,128)S(1)} %broadcast_select_fusion.2.refs_9_), channel_id=1, source_target_pairs={{0,2},{1,3},{2,0},{3,1},{4,6},{5,7},{6,4},{7,5},{8,10},{9,11},{10,... | collective-permute-start | bytes 1572872 | tf_op jit(solution)/shard_map/ppermute | solution.py:224
  51.0 26.3 %copy-start.4 = (f32[512,256]{1,0:T(8,128)}, f32[512,256]{1,0:T(8,128)S(1)}, u32[]{:S(2)}) copy-start(f32[512,256]{1,0:T(8,128)S(1)} %collective-permute-done.3.refs_7_) | copy-start | bytes 1572868
  58.7 12.9 %collective-permute-start.6 = (f32[512,256]{1,0:T(8,128)S(1)}, f32[512,256]{1,0:T(8,128)S(1)}, u32[]{:S(2)}, u32[]{:S(2)}) collective-permute-start(f32[512,256]{1,0:T(8,128)S(1)} %collective-permute-done.3.refs_7_), channel_id=1, source_target_pairs={{0,4},{1,5},{2,6},{3,7},{8,12},{9,13},{10,14},{11,15},{16,20},{17,... | collective-permute-start | bytes 1572872 | tf_op jit(solution)/shard_map/ppermute | solution.py:322
  63.2 14.1 %copy-start.6 = (f32[512,256]{1,0:T(8,128)}, f32[512,256]{1,0:T(8,128)S(1)}, u32[]{:S(2)}) copy-start(f32[512,256]{1,0:T(8,128)S(1)} %broadcast_select_fusion.1.refs_10_) | copy-start | bytes 1572868
  63.2 10.9 %collective-permute-start.13 = (f32[512,256]{1,0:T(8,128)S(1)}, f32[512,256]{1,0:T(8,128)}, u32[]{:S(2)}, u32[]{:S(2)}) collective-permute-start(f32[512,256]{1,0:T(8,128)S(1)} %broadcast_select_fusion.1.refs_10_), channel_id=1, source_target_pairs={{0,2},{1,3},{2,0},{3,1},{4,6},{5,7},{6,4},{7,5},{8,10},{9,11},{10,... | collective-permute-start | bytes 1572872 | tf_op jit(solution)/shard_map/ppermute | solution.py:224
  64.7 10.9 %collective-permute-start.7 = (f32[512,256]{1,0:T(8,128)S(1)}, f32[512,256]{1,0:T(8,128)S(1)}, u32[]{:S(2)}, u32[]{:S(2)}) collective-permute-start(f32[512,256]{1,0:T(8,128)S(1)} %broadcast_select_fusion.3.refs_8_), channel_id=1, source_target_pairs={{0,1},{1,0},{2,3},{3,2},{4,5},{5,4},{6,7},{7,6},{8,9},{9,8},{10,11... | collective-permute-start | bytes 1572872 | tf_op jit(solution)/shard_map/ppermute | solution.py:224
  64.7 10.9 %collective-permute-start.8 = (f32[512,256]{1,0:T(8,128)S(1)}, f32[512,256]{1,0:T(8,128)S(1)}, u32[]{:S(2)}, u32[]{:S(2)}) collective-permute-start(f32[512,256]{1,0:T(8,128)S(1)} %broadcast_select_fusion.2.refs_9_), channel_id=1, source_target_pairs={{0,1},{1,0},{2,3},{3,2},{4,5},{5,4},{6,7},{7,6},{8,9},{9,8},{10,11... | collective-permute-start | bytes 1572872 | tf_op jit(solution)/shard_map/ppermute | solution.py:224
  65.2 10.9 %collective-permute-start.9 = (f32[512,256]{1,0:T(8,128)S(1)}, f32[512,256]{1,0:T(8,128)S(1)}, u32[]{:S(2)}, u32[]{:S(2)}) collective-permute-start(f32[512,256]{1,0:T(8,128)S(1)} %broadcast_select_fusion.1.refs_10_), channel_id=1, source_target_pairs={{0,1},{1,0},{2,3},{3,2},{4,5},{5,4},{6,7},{7,6},{8,9},{9,8},{10,11... | collective-permute-start | bytes 1572872 | tf_op jit(solution)/shard_map/ppermute | solution.py:224
  71.7 5.6 %copy-start.7 = (f32[512,256]{1,0:T(8,128)}, f32[512,256]{1,0:T(8,128)S(1)}, u32[]{:S(2)}) copy-start(f32[512,256]{1,0:T(8,128)S(1)} %broadcast_select_fusion.refs_11_) | copy-start | bytes 1572868
  71.7 5.6 %collective-permute-start.10 = (f32[512,256]{1,0:T(8,128)S(1)}, f32[512,256]{1,0:T(8,128)}, u32[]{:S(2)}, u32[]{:S(2)}) collective-permute-start(f32[512,256]{1,0:T(8,128)S(1)} %broadcast_select_fusion.refs_11_), channel_id=1, source_target_pairs={{0,1},{1,0},{2,3},{3,2},{4,5},{5,4},{6,7},{7,6},{8,9},{9,8},{10,11... | collective-permute-start | bytes 1572872 | tf_op jit(solution)/shard_map/ppermute | solution.py:224
  74.1 16.6 %collective-permute-start.14 = (f32[512,256]{1,0:T(8,128)S(1)}, f32[512,256]{1,0:T(8,128)S(1)}, u32[]{:S(2)}, u32[]{:S(2)}) collective-permute-start(f32[512,256]{1,0:T(8,128)S(1)} %broadcast_select_fusion.refs_11_), channel_id=1, source_target_pairs={{0,2},{1,3},{2,0},{3,1},{4,6},{5,7},{6,4},{7,5},{8,10},{9,11},{10,... | collective-permute-start | bytes 1572872 | tf_op jit(solution)/shard_map/ppermute | solution.py:224
  75.6 0.8 copy-start.11
  75.6 15.2 %collective-permute-start.15 = (f32[512,256]{1,0:T(8,128)S(1)}, f32[512,256]{1,0:T(8,128)}, u32[]{:S(2)}, u32[]{:S(2)}) collective-permute-start(f32[512,256]{1,0:T(8,128)S(1)} %collective-permute-done.11.refs_6_), channel_id=1, source_target_pairs={{0,1},{1,0},{2,3},{3,2},{4,5},{5,4},{6,7},{7,6},{8,9},{9,8},{10,11... | collective-permute-start | bytes 1572872 | tf_op jit(solution)/shard_map/ppermute | solution.py:224
  75.6 0.9 copy-start.12
  75.6 15.2 %collective-permute-start.16 = (f32[512,256]{1,0:T(8,128)}, f32[512,256]{1,0:T(8,128)}, u32[]{:S(2)}, u32[]{:S(2)}) collective-permute-start(f32[512,256]{1,0:T(8,128)} %collective-permute-done.12.refs_7_), channel_id=1, source_target_pairs={{0,1},{1,0},{2,3},{3,2},{4,5},{5,4},{6,7},{7,6},{8,9},{9,8},{10,11... | collective-permute-start | bytes 1572872 | tf_op jit(solution)/shard_map/ppermute | solution.py:224
  76.4 0.8 copy-start.13
  76.4 14.4 %collective-permute-start.17 = (f32[512,256]{1,0:T(8,128)}, f32[512,256]{1,0:T(8,128)}, u32[]{:S(2)}, u32[]{:S(2)}) collective-permute-start(f32[512,256]{1,0:T(8,128)} %collective-permute-done.13.refs_8_), channel_id=1, source_target_pairs={{0,1},{1,0},{2,3},{3,2},{4,5},{5,4},{6,7},{7,6},{8,9},{9,8},{10,11... | collective-permute-start | bytes 1572872 | tf_op jit(solution)/shard_map/ppermute | solution.py:224
  90.7 2.0 %copy-start.10 = (f32[512,256]{1,0:T(8,128)}, f32[512,256]{1,0:T(8,128)S(1)}, u32[]{:S(2)}) copy-start(f32[512,256]{1,0:T(8,128)S(1)} %collective-permute-done.14.refs_9_) | copy-start | bytes 1572868
  90.7 2.0 %collective-permute-start.18 = (f32[512,256]{1,0:T(8,128)S(1)}, f32[512,256]{1,0:T(8,128)S(1)}, u32[]{:S(2)}, u32[]{:S(2)}) collective-permute-start(f32[512,256]{1,0:T(8,128)S(1)} %collective-permute-done.14.refs_9_), channel_id=1, source_target_pairs={{0,1},{1,0},{2,3},{3,2},{4,5},{5,4},{6,7},{7,6},{8,9},{9,8},{10,11... | collective-permute-start | bytes 1572872 | tf_op jit(solution)/shard_map/ppermute | solution.py:224
  92.7 0.8 copy-start.14
  108.1 22.1 %copy-start.21 = (f32[128,256]{1,0:T(8,128)S(1)}, f32[128,256]{1,0:T(8,128)}, u32[]{:S(2)}) copy-start(f32[128,256]{1,0:T(8,128)} %get-tuple-element.52) | copy-start | bytes 393220
  109.2 2.0 %collective-permute-start.20 = (f32[256,512]{1,0:T(8,128)S(1)}, f32[256,512]{1,0:T(8,128)S(1)}, u32[]{:S(2)}, u32[]{:S(2)}) collective-permute-start(f32[256,512]{1,0:T(8,128)S(1)} %constant_dynamic-slice_fusion.3), channel_id=1, source_target_pairs={{0,1},{1,0},{2,3},{3,2},{4,5},{5,4},{6,7},{7,6},{8,9},{9,8},{10,11... | collective-permute-start | bytes 1572872 | tf_op jit(solution)/shard_map/ppermute | solution.py:224
  109.4 20.8 %collective-permute-start.19 = (f32[384,256]{1,0:T(8,128)}, f32[384,256]{1,0:T(8,128)S(1)}, u32[]{:S(2)}, u32[]{:S(2)}) collective-permute-start(f32[384,256]{1,0:T(8,128)} %get-tuple-element.49), channel_id=1, source_target_pairs={{0,16},{8,24},{16,0},{24,8},{1,17},{9,25},{17,1},{25,9},{2,18},{10... | collective-permute-start | bytes 1179656 | tf_op jit(solution)/shard_map/ppermute | solution.py:224
  112.3 27.6 %copy-start.19 = (f32[512,256]{1,0:T(8,128)S(1)}, f32[512,256]{1,0:T(8,128)}, u32[]{:S(2)}) copy-start(f32[512,256]{1,0:T(8,128)} %get-tuple-element.59) | copy-start | bytes 1572868
  112.4 29.6 %copy-start.20 = (f32[512,256]{1,0:T(8,128)S(1)}, f32[512,256]{1,0:T(8,128)}, u32[]{:S(2)}) copy-start(f32[512,256]{1,0:T(8,128)} %get-tuple-element.56) | copy-start | bytes 1572868
  112.4 6.4 %collective-permute-start.21 = (f32[64,512]{1,0:T(8,128)S(1)}, f32[64,512]{1,0:T(8,128)S(1)}, u32[]{:S(2)}, u32[]{:S(2)}) collective-permute-start(f32[64,512]{1,0:T(8,128)S(1)} %get-tuple-element.68), channel_id=1, source_target_pairs={{0,2},{1,3},{2,0},{3,1},{4,6},{5,7},{6,4},{7,5},{8,10},{9,11},{10,... | collective-permute-start | bytes 393224 | tf_op jit(solution)/shard_map/ppermute | solution.py:224
  113.0 8.1 %collective-permute-start.22 = (f32[64,512]{1,0:T(8,128)S(1)}, f32[64,512]{1,0:T(8,128)S(1)}, u32[]{:S(2)}, u32[]{:S(2)}) collective-permute-start(f32[64,512]{1,0:T(8,128)S(1)} %get-tuple-element.70), channel_id=1, source_target_pairs={{0,4},{1,5},{2,6},{3,7},{4,0},{5,1},{6,2},{7,3},{8,12},{9,13},{10,... | collective-permute-start | bytes 393224 | tf_op jit(solution)/shard_map/ppermute | solution.py:224
  113.2 7.9 %collective-permute-start.23 = (f32[64,512]{1,0:T(8,128)S(1)}, f32[64,512]{1,0:T(8,128)S(1)}, u32[]{:S(2)}, u32[]{:S(2)}) collective-permute-start(f32[64,512]{1,0:T(8,128)S(1)} %get-tuple-element.69), channel_id=1, source_target_pairs={{0,6},{1,7},{2,4},{3,5},{4,2},{5,3},{6,0},{7,1},{8,14},{9,15},{10,... | collective-permute-start | bytes 393224 | tf_op jit(solution)/shard_map/ppermute | solution.py:224
  130.2 7.4 %collective-permute-start.25 = (f32[64,512]{1,0:T(8,128)S(1)}, f32[64,512]{1,0:T(8,128)S(1)}, u32[]{:S(2)}, u32[]{:S(2)}) collective-permute-start(f32[64,512]{1,0:T(8,128)S(1)} %add_add_fusion), channel_id=1, source_target_pairs={{0,8},{8,0},{16,24},{24,16},{1,9},{9,1},{17,25},{25,17},{2,10},{10... | collective-permute-start | bytes 393224 | tf_op jit(solution)/shard_map/ppermute | solution.py:224
  130.2 9.2 %collective-permute-start.24 = (f32[128,256]{1,0:T(8,128)S(1)}, f32[128,256]{1,0:T(8,128)S(1)}, u32[]{:S(2)}, u32[]{:S(2)}) collective-permute-start(f32[128,256]{1,0:T(8,128)S(1)} %copy-done.21), channel_id=1, source_target_pairs={{0,16},{8,24},{16,0},{24,8},{1,17},{9,25},{17,1},{25,9},{2,18},{10... | collective-permute-start | bytes 393224 | tf_op jit(solution)/shard_map/ppermute | solution.py:224
  139.4 8.3 %collective-permute-start.28 = (f32[64,512]{1,0:T(8,128)S(1)}, f32[64,512]{1,0:T(8,128)S(1)}, u32[]{:S(2)}, u32[]{:S(2)}) collective-permute-start(f32[64,512]{1,0:T(8,128)S(1)} %add.176), channel_id=1, source_target_pairs={{0,16},{8,24},{16,0},{24,8},{1,17},{9,25},{17,1},{25,9},{2,18},{10... | collective-permute-start | bytes 393224 | tf_op jit(solution)/shard_map/ppermute | solution.py:224
  140.0 27.0 %copy-start.15 = (f32[512,256]{1,0:T(8,128)S(1)}, f32[512,256]{1,0:T(8,128)}, u32[]{:S(2)}) copy-start(f32[512,256]{1,0:T(8,128)} %get-tuple-element.57) | copy-start | bytes 1572868
  140.0 27.1 %collective-permute-start.27 = (f32[512,256]{1,0:T(8,128)S(1)}, f32[512,256]{1,0:T(8,128)S(1)}, u32[]{:S(2)}, u32[]{:S(2)}) collective-permute-start(f32[512,256]{1,0:T(8,128)S(1)} %copy-done.19), channel_id=1, source_target_pairs={{0,8},{8,0},{16,24},{24,16},{1,9},{9,1},{17,25},{25,17},{2,10},{10... | collective-permute-start | bytes 1572872 | tf_op jit(solution)/shard_map/ppermute | solution.py:224
  142.0 25.0 %collective-permute-start.26 = (f32[512,256]{1,0:T(8,128)S(1)}, f32[512,256]{1,0:T(8,128)S(1)}, u32[]{:S(2)}, u32[]{:S(2)}) collective-permute-start(f32[512,256]{1,0:T(8,128)S(1)} %copy-done.20), channel_id=1, source_target_pairs={{0,24},{8,16},{16,8},{24,0},{1,25},{9,17},{17,9},{25,1},{2,26},{10... | collective-permute-start | bytes 1572872 | tf_op jit(solution)/shard_map/ppermute | solution.py:224
  147.8 5.0 %collective-permute-start.29 = (f32[64,512]{1,0:T(8,128)S(1)}, f32[64,512]{1,0:T(8,128)S(1)}, u32[]{:S(2)}, u32[]{:S(2)}) collective-permute-start(f32[64,512]{1,0:T(8,128)S(1)} %add.179), channel_id=1, source_target_pairs={{0,2},{1,3},{2,0},{3,1},{4,6},{5,7},{6,4},{7,5},{8,10},{9,11},{10,... | collective-permute-start | bytes 393224 | tf_op jit(solution)/shard_map/ppermute | solution.py:224
  148.4 6.4 %collective-permute-start.30 = (f32[64,512]{1,0:T(8,128)S(1)}, f32[64,512]{1,0:T(8,128)S(1)}, u32[]{:S(2)}, u32[]{:S(2)}) collective-permute-start(f32[64,512]{1,0:T(8,128)S(1)} %add.179), channel_id=1, source_target_pairs={{0,4},{1,5},{2,6},{3,7},{4,0},{5,1},{6,2},{7,3},{8,12},{9,13},{10,... | collective-permute-start | bytes 393224 | tf_op jit(solution)/shard_map/ppermute | solution.py:224
  148.6 6.2 %collective-permute-start.31 = (f32[64,512]{1,0:T(8,128)S(1)}, f32[64,512]{1,0:T(8,128)S(1)}, u32[]{:S(2)}, u32[]{:S(2)}) collective-permute-start(f32[64,512]{1,0:T(8,128)S(1)} %add.179), channel_id=1, source_target_pairs={{0,6},{1,7},{2,4},{3,5},{4,2},{5,3},{6,0},{7,1},{8,14},{9,15},{10,... | collective-permute-start | bytes 393224 | tf_op jit(solution)/shard_map/ppermute | solution.py:224
  154.8 12.3 %collective-permute-start.32 = (f32[256,512]{1,0:T(8,128)S(1)}, f32[256,512]{1,0:T(8,128)S(1)}, u32[]{:S(2)}, u32[]{:S(2)}) collective-permute-start(f32[256,512]{1,0:T(8,128)S(1)} %maximum_select_fusion.1), channel_id=1, source_target_pairs={{0,1},{1,0},{2,3},{3,2},{4,5},{5,4},{6,7},{7,6},{8,9},{9,8},{10,11... | collective-permute-start | bytes 1572872 | tf_op jit(solution)/shard_map/ppermute | solution.py:224
  167.1 1.7 copy-start.8
